TPU v7x, 128 devices: a whole 4x4x4 slice. The times are simulated.
128 devices in a mesh: expert: 64 (over z, x, y), mp: 2 (over core).
Axes of the slice: x: 4, y: 4, z: 4, core: 2. Of those that a mesh axis runs over, the one named last changes fastest.
Arguments:
- tokens: bfloat16 [4096, 3584], P('expert', 'mp'), may hold values from -6 to 6
- cotangent: bfloat16 [4096, 3584], P('expert', 'mp'), may hold values from -6 to 6
- route_ids: int32 [4096, 8], P('expert'), may hold values from 0 to 63, all different within a row; in each aligned block of 64 rows (0 to 63, 64 to 127, ...) at most 12 rows name the same one
- gate_probs: float32 [4096, 8], P('expert'), may hold values from 0.02 to 0.5
- w_gate: bfloat16 [64, 3584, 1024], P('expert', None, 'mp'), may hold values from -0.09375 to 0.09375
- w_up: bfloat16 [64, 3584, 1024], P('expert', None, 'mp'), may hold values from -0.09375 to 0.09375
- w_down: bfloat16 [64, 1024, 3584], P('expert', 'mp'), may hold values from -0.1875 to 0.1875
Outputs:
- layer_out: bfloat16 [4096, 3584], P('expert', 'mp')
- grad_tokens: bfloat16 [4096, 3584], P('expert', 'mp')
- grad_probs: float32 [4096, 8], P('expert')
- grad_w_gate: bfloat16 [64, 3584, 1024], P('expert', None, 'mp')
- grad_w_up: bfloat16 [64, 3584, 1024], P('expert', None, 'mp')
- grad_w_down: bfloat16 [64, 1024, 3584], P('expert', 'mp')
Inputs may be any that keep to these rules, and one draw needn't show every extreme that they name: `route_ids`: each token names 8 different experts. Within the tokens of one device (aligned blocks of 64 tokens) no expert is named more than 12 times, and in some block one expert is named exactly 12 times.
All inputs are finite; a program needn't handle non-finite values.
Results may differ from a plain program's by a relative error of at most 0.015.
Values may be sent and summed in bfloat16 or wider, within the bound.
No kernel may reach another device: no remote copies, remote signals or barrier semaphores. Data moves between devices by JAX's collectives and lax.ppermute only.
A program may use at most 192 MiB of HBM per device.

v0:
```python
import jax
import jax.numpy as jnp
from jax import lax
from jax.sharding import PartitionSpec as P


def spread_rows(select, slot_probs, feat_tokens, feat_cot, experts, most_rows):
    select_half = select.astype(jnp.bfloat16)
    token_rows = jnp.dot(select_half, feat_tokens, preferred_element_type=jnp.float32).astype(
        jnp.bfloat16
    )
    cot_rows = jnp.dot(select_half, feat_cot, preferred_element_type=jnp.float32)
    scaled_rows = (slot_probs[:, None] * cot_rows).astype(jnp.bfloat16)
    return (token_rows.reshape(experts, most_rows, -1), scaled_rows.reshape(experts, most_rows, -1))


def body(tokens, cotangent, route_ids, gate_probs, w_gate, w_up, w_down):
    tok_rows, half_width = tokens.shape
    top_count = route_ids.shape[1]
    experts = lax.axis_size("expert")
    most_rows = max(2, min(tok_rows, 3 * tok_rows * top_count // (2 * experts)))
    slots_all = experts * most_rows
    flat_ids = route_ids.reshape(-1)
    onehot = (flat_ids[:, None] == jnp.arange(experts, dtype=jnp.int32)[None, :]).astype(jnp.int32)
    earlier = jnp.cumsum(onehot, axis=0) - onehot
    slot_of = jnp.sum(earlier * onehot, axis=1)
    position = flat_ids * most_rows + slot_of
    placed = (position[:, None] == jnp.arange(slots_all, dtype=jnp.int32)[None, :]).astype(
        jnp.float32
    )
    placed_three = placed.reshape(tok_rows, top_count, slots_all)
    select = jnp.transpose(jnp.sum(placed_three, axis=1))
    slot_probs = jnp.sum(placed_three * gate_probs[:, :, None], axis=(0, 1))
    whole_tokens, whole_cot = (
        lax.all_gather(tokens, "mp", axis=1, tiled=True),
        lax.all_gather(cotangent, "mp", axis=1, tiled=True),
    )
    sent_tokens, sent_cot = spread_rows(
        select, slot_probs, whole_tokens, whole_cot, experts, most_rows
    )
    recv_tokens, recv_cot = (
        lax.all_to_all(sent_tokens, "expert", split_axis=0, concat_axis=0, tiled=True),
        lax.all_to_all(sent_cot, "expert", split_axis=0, concat_axis=0, tiled=True),
    )
    token_rows = recv_tokens.reshape(slots_all, -1)
    scaled_rows = recv_cot.reshape(slots_all, -1)
    gate_mat = w_gate[0]
    up_mat = w_up[0]
    down_mat = w_down[0]
    contract_last = (((1,), (1,)), ((), ()))
    contract_first = (((0,), (0,)), ((), ()))
    gate_pre = jnp.dot(token_rows, gate_mat, preferred_element_type=jnp.float32)
    up_pre = jnp.dot(token_rows, up_mat, preferred_element_type=jnp.float32)
    logistic = jax.nn.sigmoid(gate_pre)
    swish = gate_pre * logistic
    hidden = (swish * up_pre).astype(jnp.bfloat16)
    hidden_grad = lax.dot_general(
        scaled_rows, down_mat, contract_last, preferred_element_type=jnp.float32
    )
    slope = logistic * (1.0 + gate_pre * (1.0 - logistic))
    gate_grad = (hidden_grad * up_pre * slope).astype(jnp.bfloat16)
    up_grad = (hidden_grad * swish).astype(jnp.bfloat16)
    grad_w_down = lax.dot_general(
        hidden, scaled_rows, contract_first, preferred_element_type=jnp.float32
    ).astype(jnp.bfloat16)[None]
    grad_w_gate = lax.dot_general(
        token_rows, gate_grad, contract_first, preferred_element_type=jnp.float32
    ).astype(jnp.bfloat16)[None]
    grad_w_up = lax.dot_general(
        token_rows, up_grad, contract_first, preferred_element_type=jnp.float32
    ).astype(jnp.bfloat16)[None]
    out_part = jnp.dot(hidden, down_mat, preferred_element_type=jnp.float32)
    input_part = lax.dot_general(
        gate_grad, gate_mat, contract_last, preferred_element_type=jnp.float32
    ) + lax.dot_general(up_grad, up_mat, contract_last, preferred_element_type=jnp.float32)
    out_share, input_share = (
        lax.psum_scatter(
            out_part.reshape(experts, most_rows, -1), "mp", scatter_dimension=2, tiled=True
        ),
        lax.psum_scatter(
            input_part.reshape(experts, most_rows, -1), "mp", scatter_dimension=2, tiled=True
        ),
    )
    back_out, back_input = (
        lax.all_to_all(
            out_share.astype(jnp.bfloat16), "expert", split_axis=0, concat_axis=0, tiled=True
        ),
        lax.all_to_all(
            input_share.astype(jnp.bfloat16), "expert", split_axis=0, concat_axis=0, tiled=True
        ),
    )
    out_sel = jnp.take(back_out.reshape(slots_all, -1), position, axis=0)
    out_sel = out_sel.reshape(tok_rows, top_count, half_width).astype(jnp.float32)
    input_sel = jnp.take(back_input.reshape(slots_all, -1), position, axis=0)
    input_sel = input_sel.reshape(tok_rows, top_count, half_width).astype(jnp.float32)
    layer_out = jnp.sum(gate_probs[:, :, None] * out_sel, axis=1).astype(jnp.bfloat16)
    grad_tokens = jnp.sum(input_sel, axis=1).astype(jnp.bfloat16)
    gate_part = jnp.sum(cotangent.astype(jnp.float32)[:, None, :] * out_sel, axis=2)
    grad_probs = lax.psum(gate_part, "mp")
    return (layer_out, grad_tokens, grad_probs, grad_w_gate, grad_w_up, grad_w_down)


def solution(mesh):
    return jax.shard_map(
        body,
        mesh=mesh,
        in_specs=(
            P("expert", "mp"),
            P("expert", "mp"),
            P("expert", None),
            P("expert", None),
            P("expert", None, "mp"),
            P("expert", None, "mp"),
            P("expert", "mp", None),
        ),
        out_specs=(
            P("expert", "mp"),
            P("expert", "mp"),
            P("expert", None),
            P("expert", None, "mp"),
            P("expert", None, "mp"),
            P("expert", "mp", None),
        ),
        check_vma=False,
    )
```

profile of v0, /device:TPU:7, one launch (start us, length us, event | category | flops | bytes accessed | tf_op | source)
XLA Modules:
  0.0 428.5 jit_solution(15973934367986376887)
XLA Ops:
  14.7 4.0 convolution_convert_fusion
  18.7 9.3 %reshape.87 = bf16[64,12,3584]{2,1,0:T(8,128)(2,1)} reshape(bf16[768,3584]{1,0:T(8,128)(2,1)} %convolution_convert_fusion) | data formatting | bytes 11010048 | tf_op jit(solution)/shard_map/reshape | solution.py:14
  28.0 11.2 %all-to-all-start = ((bf16[64,12,3584]{2,1,0:T(8,128)(2,1)}), bf16[64,12,3584]{2,1,0:T(8,128)(2,1)}, u32[]{:S(2)}, u32[]{:S(2)}) async-start(bf16[64,12,3584]{2,1,0:T(8,128)(2,1)} %reshape.87), calls=%async_computation | async-start | bytes 14680064 | tf_op jit(solution)/shard_map/all_to_all | solution.py:42
  41.9 4.0 multiply_convert_fusion
  45.9 9.3 %reshape.90 = bf16[64,12,3584]{2,1,0:T(8,128)(2,1)} reshape(bf16[768,3584]{1,0:T(8,128)(2,1)} %multiply_convert_fusion) | data formatting | bytes 11010048 | tf_op jit(solution)/shard_map/reshape | solution.py:14
  55.2 83.4 %all-to-all-done = bf16[64,12,3584]{2,1,0:T(8,128)(2,1)} async-done(((bf16[64,12,3584]{2,1,0:T(8,128)(2,1)}), bf16[64,12,3584]{2,1,0:T(8,128)(2,1)}, u32[]{:S(2)}, u32[]{:S(2)}) %all-to-all-start) | async-done | bytes 5505056 | tf_op jit(solution)/shard_map/all_to_all | solution.py:42
  138.6 8.9 %all-to-all-start.2 = ((bf16[64,12,3584]{2,1,0:T(8,128)(2,1)}), bf16[64,12,3584]{2,1,0:T(8,128)(2,1)}, u32[]{:S(2)}, u32[]{:S(2)}) async-start(bf16[64,12,3584]{2,1,0:T(8,128)(2,1)} %reshape.90), calls=%async_computation.3 | async-start | bytes 14680064 | tf_op jit(solution)/shard_map/all_to_all | solution.py:43
  147.8 9.4 %reshape.88 = bf16[768,3584]{1,0:T(8,128)(2,1)} reshape(bf16[64,12,3584]{2,1,0:T(8,128)(2,1)} %all-to-all-done) | data formatting | bytes 11010048 | tf_op jit(solution)/shard_map/reshape | solution.py:45
  157.2 7.9 %fusion.11 = f32[768,512]{1,0:T(8,128)} fusion(bf16[768,3584]{1,0:T(8,128)(2,1)} %reshape.88, bf16[1,3584,512]{2,1,0:T(8,128)(2,1)} %param.14), kind=kOutput, calls=%fused_computation.21 | convolution fusion | flops 2818572288 | bytes 10747904 | tf_op jit(solution)/shard_map/dot_general | solution.py:53
  165.1 4.1 fusion.15
  169.3 71.8 %all-to-all-done.2 = bf16[64,12,3584]{2,1,0:T(8,128)(2,1)} async-done(((bf16[64,12,3584]{2,1,0:T(8,128)(2,1)}), bf16[64,12,3584]{2,1,0:T(8,128)(2,1)}, u32[]{:S(2)}, u32[]{:S(2)}) %all-to-all-start.2) | async-done | bytes 5505056 | tf_op jit(solution)/shard_map/all_to_all | solution.py:43
  241.1 9.4 %reshape.91 = bf16[768,3584]{1,0:T(8,128)(2,1)} reshape(bf16[64,12,3584]{2,1,0:T(8,128)(2,1)} %all-to-all-done.2) | data formatting | bytes 11010048 | tf_op jit(solution)/shard_map/reshape | solution.py:46
  250.4 9.0 %multiply_convert_fusion.1 = (bf16[768,512]{1,0:T(8,128)(2,1)S(1)}, bf16[768,512]{1,0:T(8,128)(2,1)}, bf16[768,512]{1,0:T(8,128)(2,1)S(1)}) fusion(f32[768,512]{1,0:T(8,128)} %fusion.15, f32[768,512]{1,0:T(8,128)} %fusion.11, bf16[768,3584]{1,0:T(8,128)(2,1)} %reshape.91, bf16[1,512,3584]{2,1,0:T(8,128)(2,1)} %param.15), kind=kOutput, calls=%fused_computation.29 | convolution fusion | flops 2824470528 | bytes 14680064 | tf_op jit(solution)/shard_map/dot_general | solution.py:57
  259.6 7.8 %fusion.6 = f32[64,12,3584]{2,0,1:T(8,128)} fusion(bf16[1,512,3584]{2,1,0:T(8,128)(2,1)} %param.15, bf16[64,12,512]{2,1,0:T(8,128)(2,1)S(1)} %dot_general.38), kind=kOutput, calls=%fused_computation.16 | convolution fusion | flops 2818572288 | bytes 15466496 | tf_op jit(solution)/shard_map/dot_general | solution.py:72
  268.6 5.2 %fusion.13 = f32[768,3584]{1,0:T(8,128)S(1)} fusion(bf16[768,512]{1,0:T(8,128)(2,1)S(1)} %copy-done.6, bf16[1,3584,512]{2,1,0:T(8,128)(2,1)} %param.13), kind=kOutput, calls=%fused_computation.23 | convolution fusion | flops 2818572288 | bytes 15466496 | tf_op jit(solution)/shard_map/dot_general | solution.py:73
  273.8 5.9 %convolution_add_fusion = f32[768,3584]{1,0:T(8,128)} fusion(f32[768,3584]{1,0:T(8,128)S(1)} %fusion.13, bf16[768,512]{1,0:T(8,128)(2,1)S(1)} %get-tuple-element.35, bf16[1,3584,512]{2,1,0:T(8,128)(2,1)S(1)} %copy-done.2), kind=kOutput, calls=%fused_computation.3 | convolution fusion | flops 2821324800 | bytes 26476544 | tf_op jit(solution)/shard_map/dot_general | solution.py:75
  279.7 13.4 %reshape.92 = f32[64,12,3584]{2,1,0:T(8,128)} reshape(f32[768,3584]{1,0:T(8,128)} %convolution_add_fusion) | data formatting | bytes 22020096 | tf_op jit(solution)/shard_map/reshape | solution.py:81
  293.1 3.7 reduce-scatter.3.cloned.1.call-done
  299.7 3.4 copy.54
  303.1 10.7 %all-to-all-start.1 = ((bf16[64,12,1792]{2,1,0:T(8,128)(2,1)}), bf16[64,12,1792]{2,1,0:T(8,128)(2,1)}, u32[]{:S(2)}, u32[]{:S(2)}) async-start(bf16[64,12,1792]{2,1,0:T(8,128)(2,1)} %copy.54), calls=%async_computation.2 | async-start | bytes 7340032 | tf_op jit(solution)/shard_map/all_to_all | solution.py:85
  313.8 14.9 %reduce-scatter.5.cloned.1.call-done = f32[64,12,1792]{2,1,0:T(8,128)} async-done(((f32[64,12,3584]{2,1,0:T(8,128)}), f32[64,12,1792]{2,1,0:T(8,128)}) %reduce-scatter.5.cloned.1.call-update) | async-done | bytes 5505040 | tf_op jit(solution)/shard_map/reduce_scatter | solution.py:80
  328.7 5.3 %convert_element_type.75 = bf16[64,12,1792]{2,1,0:T(8,128)(2,1)} convert(f32[64,12,1792]{2,1,0:T(8,128)} %reduce-scatter.5.cloned.1.call-done) | non-fusion elementwise | flops 1376256 | bytes 8257536 | tf_op jit(solution)/shard_map/convert_element_type | solution.py:89
  334.0 26.4 %all-to-all-done.1 = bf16[64,12,1792]{2,1,0:T(8,128)(2,1)} async-done(((bf16[64,12,1792]{2,1,0:T(8,128)(2,1)}), bf16[64,12,1792]{2,1,0:T(8,128)(2,1)}, u32[]{:S(2)}, u32[]{:S(2)}) %all-to-all-start.1) | async-done | bytes 2752544 | tf_op jit(solution)/shard_map/all_to_all | solution.py:85
  360.4 5.6 %all-to-all-start.3 = ((bf16[64,12,1792]{2,1,0:T(8,128)(2,1)}), bf16[64,12,1792]{2,1,0:T(8,128)(2,1)}, u32[]{:S(2)}, u32[]{:S(2)}) async-start(bf16[64,12,1792]{2,1,0:T(8,128)(2,1)} %convert_element_type.75), calls=%async_computation.5 | async-start | bytes 7340032 | tf_op jit(solution)/shard_map/all_to_all | solution.py:88
  366.1 7.8 %fusion.2 = bf16[1,512,3584]{2,1,0:T(8,128)(2,1)} fusion(bf16[768,512]{1,0:T(8,128)(2,1)} %copy-done.4, bf16[768,3584]{1,0:T(8,128)(2,1)} %reshape.91), kind=kOutput, calls=%fused_computation.10 | convolution fusion | flops 2820407296 | bytes 9961472 | tf_op jit(solution)/shard_map/dot_general | solution.py:63
  373.9 4.6 %fusion.1 = bf16[1,3584,512]{2,1,0:T(8,128)(2,1)} fusion(bf16[768,3584]{1,0:T(8,128)(2,1)S(1)} %bitcast.69, bf16[768,512]{1,0:T(8,128)(2,1)S(1)} %get-tuple-element.35), kind=kOutput, calls=%fused_computation.9 | convolution fusion | flops 2820407296 | bytes 9961472 | tf_op jit(solution)/shard_map/dot_general | solution.py:69
  378.5 4.5 %fusion = bf16[1,3584,512]{2,1,0:T(8,128)(2,1)} fusion(bf16[768,3584]{1,0:T(8,128)(2,1)S(1)} %bitcast.69, bf16[768,512]{1,0:T(8,128)(2,1)S(1)} %copy-done.7), kind=kOutput, calls=%fused_computation.8 | convolution fusion | flops 2820407296 | bytes 9961472 | tf_op jit(solution)/shard_map/dot_general | solution.py:66
  383.1 3.8 reshape.89
  392.4 6.3 %psum.7 = f32[64,8]{1,0:T(8,128)S(1)} all-reduce(f32[64,8]{1,0:T(8,128)S(1)} %reduce_sum.68), channel_id=1, replica_groups=mesh['expert'=64,'mp'=2] {'mp'}, use_global_device_ids=true, to_apply=%region_10.12 | all-reduce | flops 512 | bytes 4096 | tf_op jit(solution)/shard_map/psum | solution.py:99
  401.6 10.0 %all-to-all-done.3 = bf16[64,12,1792]{2,1,0:T(8,128)(2,1)} async-done(((bf16[64,12,1792]{2,1,0:T(8,128)(2,1)}), bf16[64,12,1792]{2,1,0:T(8,128)(2,1)}, u32[]{:S(2)}, u32[]{:S(2)}) %all-to-all-start.3) | async-done | bytes 2752544 | tf_op jit(solution)/shard_map/all_to_all | solution.py:88
  411.6 3.8 reshape.93
  415.4 3.2 gather_fusion.1
  (53 shorter events, 26.3 us)
Async XLA Ops:
  28.0 11.2 %copy-start.3 = (bf16[64,1792]{1,0:T(8,128)(2,1)S(1)}, bf16[64,1792]{1,0:T(8,128)(2,1)}, u32[]{:S(2)}) copy-start(bf16[64,1792]{1,0:T(8,128)(2,1)} %param.10) | copy-start | bytes 688132
  28.0 110.6 %all-to-all-start = ((bf16[64,12,3584]{2,1,0:T(8,128)(2,1)}), bf16[64,12,3584]{2,1,0:T(8,128)(2,1)}, u32[]{:S(2)}, u32[]{:S(2)}) async-start(bf16[64,12,3584]{2,1,0:T(8,128)(2,1)} %reshape.87), calls=%async_computation | async-start | bytes 14680064 | tf_op jit(solution)/shard_map/all_to_all | solution.py:42
  138.6 102.5 %all-to-all-start.2 = ((bf16[64,12,3584]{2,1,0:T(8,128)(2,1)}), bf16[64,12,3584]{2,1,0:T(8,128)(2,1)}, u32[]{:S(2)}, u32[]{:S(2)}) async-start(bf16[64,12,3584]{2,1,0:T(8,128)(2,1)} %reshape.90), calls=%async_computation.3 | async-start | bytes 14680064 | tf_op jit(solution)/shard_map/all_to_all | solution.py:43
  147.6 149.2 %reduce-scatter.3.cloned.1.call-start = ((), (), s32[]{:S(2)}) async-start(), calls=%async_computation.6 | async-start | bytes 16515072 | tf_op jit(solution)/shard_map/reduce_scatter | solution.py:77
  157.2 7.9 %copy-start.1 = (bf16[768,3584]{1,0:T(8,128)(2,1)S(1)}, bf16[768,3584]{1,0:T(8,128)(2,1)}, u32[]{:S(2)}) copy-start(bf16[768,3584]{1,0:T(8,128)(2,1)} %reshape.88) | copy-start | bytes 16515076
  157.2 7.9 %copy-start.5 = (bf16[1,3584,512]{2,1,0:T(8,128)(2,1)S(1)}, bf16[1,3584,512]{2,1,0:T(8,128)(2,1)}, u32[]{:S(2)}) copy-start(bf16[1,3584,512]{2,1,0:T(8,128)(2,1)} %param.13) | copy-start | bytes 11010052
  259.4 8.0 %copy-start.4 = (bf16[768,512]{1,0:T(8,128)(2,1)}, bf16[768,512]{1,0:T(8,128)(2,1)S(1)}, u32[]{:S(2)}) copy-start(bf16[768,512]{1,0:T(8,128)(2,1)S(1)} %get-tuple-element.37) | copy-start | bytes 2359300
  267.4 1.1 copy-start.6
  267.5 61.3 %reduce-scatter.5.cloned.1.call-start = ((), (), s32[]{:S(2)}) async-start(), calls=%async_computation.7 | async-start | bytes 22020096 | tf_op jit(solution)/shard_map/reduce_scatter | solution.py:80
  268.6 5.2 %copy-start.2 = (bf16[1,3584,512]{2,1,0:T(8,128)(2,1)S(1)}, bf16[1,3584,512]{2,1,0:T(8,128)(2,1)}, u32[]{:S(2)}) copy-start(bf16[1,3584,512]{2,1,0:T(8,128)(2,1)} %param.14) | copy-start | bytes 11010052
  303.1 57.4 %all-to-all-start.1 = ((bf16[64,12,1792]{2,1,0:T(8,128)(2,1)}), bf16[64,12,1792]{2,1,0:T(8,128)(2,1)}, u32[]{:S(2)}, u32[]{:S(2)}) async-start(bf16[64,12,1792]{2,1,0:T(8,128)(2,1)} %copy.54), calls=%async_computation.2 | async-start | bytes 7340032 | tf_op jit(solution)/shard_map/all_to_all | solution.py:85
  360.4 13.5 %slice-start = ((s8[5505024]{0:T(1024)(128)(4,1)}), s8[1310720]{0:T(1024)(128)(4,1)S(1)}, s32[]{:S(2)}) async-start(s8[5505024]{0:T(1024)(128)(4,1)} %bitcast.68), calls=%async_computation.8 | async-start | bytes 2621440
  360.4 51.1 %all-to-all-start.3 = ((bf16[64,12,1792]{2,1,0:T(8,128)(2,1)}), bf16[64,12,1792]{2,1,0:T(8,128)(2,1)}, u32[]{:S(2)}, u32[]{:S(2)}) async-start(bf16[64,12,1792]{2,1,0:T(8,128)(2,1)} %convert_element_type.75), calls=%async_computation.5 | async-start | bytes 7340032 | tf_op jit(solution)/shard_map/all_to_all | solution.py:88
  366.1 7.9 %slice-start.1 = ((s8[5505024]{0:T(1024)(128)(4,1)}), s8[4194304]{0:T(1024)(128)(4,1)S(1)}, s32[]{:S(2)}) async-start(s8[5505024]{0:T(1024)(128)(4,1)} %bitcast.68), calls=%async_computation.9 | async-start | bytes 8388608
  373.9 4.6 %copy-start.7 = (bf16[768,512]{1,0:T(8,128)(2,1)S(1)}, bf16[768,512]{1,0:T(8,128)(2,1)}, u32[]{:S(2)}) copy-start(bf16[768,512]{1,0:T(8,128)(2,1)} %get-tuple-element.36) | copy-start | bytes 2359300
  390.0 9.3 %copy-start = (bf16[512,1792]{1,0:T(8,128)(2,1)S(1)}, bf16[512,1792]{1,0:T(8,128)(2,1)}, u32[]{:S(2)}) copy-start(bf16[512,1792]{1,0:T(8,128)(2,1)} %gather_fusion) | copy-start | bytes 5505028
Sparse Core Ops, SparseCore 0:
  267.6 29.1 reduce-scatter.2
  299.2 29.4 reduce-scatter.4
where the time goes:
time: 433 us; the launch traced here: 429 us
  waiting for transfers between devices  210 us (48%)
  local copies, waits for them, and re-layouts  72 us (17%)
  matrix products  65 us (15%)
  starting transfers between devices  36.9 us (9%)
  other arithmetic  18.6 us (4%)
  between operations  14.2 us (3%)
  blocking collectives  11.6 us (3%)
    all_to_all x1, waiting for transfers between devices, body(): lax.all_to_all(sent_tokens, 'expert', split_axis=0, concat_axis=0, tiled=...  83.4 us
    all_to_all x1, waiting for transfers between devices, body(): lax.all_to_all(sent_cot, 'expert', split_axis=0, concat_axis=0, tiled=True)  71.8 us
    all_to_all x1, waiting for transfers between devices, body(): lax.all_to_all(out_share.astype(jnp.bfloat16), 'expert', split_axis=0, co...  26.4 us
    reduce_scatter x1, waiting for transfers between devices, body(): lax.psum_scatter(input_part.reshape(experts, most_rows, -1), 'mp', scatte...  14.9 us
    reshape x1, local copies, waits for them, and re-layouts, body(): input_part.reshape(experts, most_rows, -1)  13.4 us
    all_to_all x1, starting transfers between devices, body(): lax.all_to_all(sent_tokens, 'expert', split_axis=0, concat_axis=0, tiled=...  11.2 us
    all_to_all x1, starting transfers between devices, body(): lax.all_to_all(out_share.astype(jnp.bfloat16), 'expert', split_axis=0, co...  10.7 us
    all_to_all x1, waiting for transfers between devices, body(): lax.all_to_all(input_share.astype(jnp.bfloat16), 'expert', split_axis=0,...  9.96 us
  transfers between devices with their start and end apart: 6, of which 6 were waited for; matrix products, arithmetic and copies ran while one was open for 23% of the time, Pallas kernels for 0%

commit v1 on v0

v1 whole, which is shorter than its diff:
```python
import functools
import jax
import jax.numpy as jnp
from jax import lax
from jax.experimental import pallas as pl
from jax.experimental.pallas import tpu as pltpu
from jax.sharding import PartitionSpec as P

BF16 = jnp.bfloat16
F32 = jnp.float32
SLOTS = 12
ROWS = 2 * SLOTS
GROUP = 16
TILE = GROUP * ROWS
VMEM_BYTES = 52 * 1024 * 1024

NN = (((1,), (0,)), ((), ()))
NT = (((1,), (1,)), ((), ()))
TN = (((0,), (0,)), ((), ()))


def dot(a, b, dims=NN):
    return lax.dot_general(a, b, dims, preferred_element_type=F32)


def params():
    return pltpu.CompilerParams(
        vmem_limit_bytes=VMEM_BYTES, dimension_semantics=("arbitrary",)
    )


def cost(flops, nbytes):
    return pl.CostEstimate(flops=int(flops), bytes_accessed=int(nbytes), transcendentals=0)


def spread(rows_of):
    return jnp.concatenate(
        [jnp.broadcast_to(rows_of[i : i + 1], (ROWS, rows_of.shape[1])) for i in range(GROUP)], axis=0
    )


def routing(route_ref, first):
    top, toks = route_ref.shape
    route = route_ref[...]
    ids = lax.broadcasted_iota(jnp.int32, (GROUP, toks), 0) + first
    hits = [jnp.broadcast_to(route[k : k + 1], (GROUP, toks)) == ids for k in range(top)]
    named = sum(h.astype(F32) for h in hits)
    return named, hits


def selection(named):
    toks = named.shape[1]
    before = (
        lax.broadcasted_iota(jnp.int32, (toks, toks), 0)
        < lax.broadcasted_iota(jnp.int32, (toks, toks), 1)
    ).astype(BF16)
    slot = dot(named.astype(BF16), before)
    code = jnp.where(named > 0, slot, -100.0)
    code = jnp.concatenate([code, code + float(SLOTS)], axis=1)
    place = lax.broadcasted_iota(jnp.int32, (ROWS, 2 * toks), 0).astype(F32)
    place = jnp.concatenate([place] * GROUP, axis=0)
    return spread(code) == place


def probs_of(hits, probs_ref):
    probs = probs_ref[...]
    chosen = sum(
        jnp.where(h, jnp.broadcast_to(probs[k : k + 1], h.shape), 0.0) for k, h in enumerate(hits)
    )
    return spread(jnp.concatenate([chosen, chosen], axis=1))


def stacked(x):
    half = x.shape[1] // 2
    return jnp.concatenate([x[:, :half], x[:, half:]], axis=0)


def send_kernel(scaled, route_ref, probs_ref, rows_ref, out_ref):
    named, hits = routing(route_ref, pl.program_id(0) * GROUP)
    sel = selection(named)
    picked = dot(sel.astype(F32).astype(BF16), stacked(rows_ref[...]))
    if scaled:
        weight = jnp.sum(jnp.where(sel, probs_of(hits, probs_ref), 0.0), axis=1, keepdims=True)
        picked = picked * weight
    out_ref[...] = picked.astype(BF16)


def send_rows(scaled, route_t, probs_t, rows, experts):
    toks, width = rows.shape
    top = route_t.shape[0]
    half = width // 2
    return pl.pallas_call(
        functools.partial(send_kernel, scaled),
        grid=(experts // GROUP,),
        in_specs=[
            pl.BlockSpec((top, toks), lambda i: (0, 0)),
            pl.BlockSpec((top, toks), lambda i: (0, 0)),
            pl.BlockSpec((toks, width), lambda i: (0, 0)),
        ],
        out_specs=pl.BlockSpec((TILE, half), lambda i: (i, 0)),
        out_shape=jax.ShapeDtypeStruct((experts * ROWS, half), BF16),
        compiler_params=params(),
        cost_estimate=cost(2 * experts * ROWS * 2 * toks * half, experts * ROWS * half * 2),
        name="send_scaled" if scaled else "send_tokens",
    )(route_t, probs_t, rows)


SUB = 8


def ordering():
    n = SUB * ROWS
    row = lax.broadcasted_iota(jnp.int32, (n, n), 0)
    col = lax.broadcasted_iota(jnp.int32, (n, n), 1)
    upper = (row >= n // 2).astype(jnp.int32)
    within = row - upper * (n // 2)
    source = (within * 43) >> 9
    return (col == SLOTS * source + SLOTS * upper + within).astype(F32).astype(BF16)


def put_in_order(own_ref, other_ref, mine, step, held, out_ref):
    order = ordering()
    n = SUB * ROWS
    for which, ref in ((mine, own_ref), (1 - mine, other_ref)):
        for b in range(GROUP // SUB):
            both = dot(order, ref[b * n : (b + 1) * n, :]).astype(BF16)
            at = pl.multiple_of(step * (GROUP * SLOTS) + b * (n // 2), n // 2)
            for h in range(2):
                part = both[h * (n // 2) : (h + 1) * (n // 2)]
                held[2 * which + h, pl.ds(at, n // 2), :] = part
                out_ref[2 * which + h, b * (n // 2) : (b + 1) * (n // 2), :] = part


def forward_kernel(
    steps, ff_steps, mine_ref, own_ref, other_ref, gate_w, up_w, down_w,
    gate_ref, up_ref, hidden_ref, rows_ref, far_ref, near_ref, held, hidden_all,
):
    i = pl.program_id(0)
    mine = mine_ref[0]
    quarter = own_ref.shape[1]

    @pl.when(i < steps)
    def _():
        put_in_order(own_ref, other_ref, mine, i, held, rows_ref)

    for f in range(ff_steps):
        @pl.when(i == steps + f)
        def _():
            gate = sum(dot(held[q], gate_w[q * quarter : (q + 1) * quarter, :]) for q in range(4))
            up = sum(dot(held[q], up_w[q * quarter : (q + 1) * quarter, :]) for q in range(4))
            gate_ref[...] = gate
            up_ref[...] = up
            hidden = (gate * jax.nn.sigmoid(gate) * up).astype(BF16)
            hidden_ref[...] = hidden
            wide = hidden.shape[1]
            hidden_all[:, f * wide : (f + 1) * wide] = hidden

    @pl.when(jnp.logical_and(i >= steps + ff_steps, i < steps + ff_steps + 2))
    def _():
        far_ref[...] = dot(hidden_all[...], down_w[...]).astype(BF16)

    @pl.when(i >= steps + ff_steps + 2)
    def _():
        near_ref[...] = dot(hidden_all[...], down_w[...])


def quarter_of(i, start, mine):
    q = jnp.clip(i - start, 0, 3)
    return jnp.where(q < 2, 2 * (1 - mine[0]) + q, 2 * mine[0] + q - 2)


def forward(mine, own, other, gate_w, up_w, down_w):
    raw, quarter = own.shape
    model, ff = gate_w.shape
    rows = raw // 2
    steps, ff_steps = raw // TILE, 2
    wide = ff // ff_steps
    last = steps + ff_steps
    ffi = lambda i, m: (0, jnp.clip(i - steps, 0, ff_steps - 1))
    step_rows = GROUP * SLOTS
    return pl.pallas_call(
        functools.partial(forward_kernel, steps, ff_steps),
        grid_spec=pltpu.PrefetchScalarGridSpec(
            num_scalar_prefetch=1,
            grid=(last + 4,),
            in_specs=[
                pl.BlockSpec((TILE, quarter), lambda i, m: (jnp.minimum(i, steps - 1), 0)),
                pl.BlockSpec((TILE, quarter), lambda i, m: (jnp.minimum(i, steps - 1), 0)),
                pl.BlockSpec((model, wide), ffi),
                pl.BlockSpec((model, wide), ffi),
                pl.BlockSpec((ff, quarter), lambda i, m: (0, quarter_of(i, last, m))),
            ],
            out_specs=[
                pl.BlockSpec((rows, wide), ffi),
                pl.BlockSpec((rows, wide), ffi),
                pl.BlockSpec((rows, wide), ffi),
                pl.BlockSpec((4, step_rows, quarter), lambda i, m: (0, jnp.minimum(i, steps - 1), 0)),
                pl.BlockSpec((rows, quarter), lambda i, m: (0, jnp.clip(i - last, 0, 1))),
                pl.BlockSpec((rows, quarter), lambda i, m: (0, jnp.clip(i - last - 2, 0, 1))),
            ],
            scratch_shapes=[pltpu.VMEM((4, rows, quarter), BF16), pltpu.VMEM((rows, ff), BF16)],
        ),
        out_shape=[
            jax.ShapeDtypeStruct((rows, ff), F32),
            jax.ShapeDtypeStruct((rows, ff), F32),
            jax.ShapeDtypeStruct((rows, ff), BF16),
            jax.ShapeDtypeStruct((4, rows, quarter), BF16),
            jax.ShapeDtypeStruct((rows, 2 * quarter), BF16),
            jax.ShapeDtypeStruct((rows, 2 * quarter), F32),
        ],
        compiler_params=params(),
        cost_estimate=cost(6 * rows * model * ff, 6 * model * ff + 30e6),
        name="expert_forward",
    )(mine, own, other, gate_w, up_w, down_w)


def backward_kernel(
    steps, ff_steps, mine_ref, own_ref, other_ref, down_w, gate_ref, up_ref, gate_w, up_w,
    gate_grad_ref, up_grad_ref, rows_ref, far_ref, near_ref, held, gate_grads, up_grads,
):
    i = pl.program_id(0)
    mine = mine_ref[0]
    quarter = own_ref.shape[1]

    @pl.when(i < steps)
    def _():
        put_in_order(own_ref, other_ref, mine, i, held, rows_ref)

    for f in range(ff_steps):
        @pl.when(i == steps + f)
        def _():
            hidden_grad = sum(
                dot(held[q], down_w[:, q * quarter : (q + 1) * quarter], NT) for q in range(4)
            )
            gate, up = gate_ref[...], up_ref[...]
            logistic = jax.nn.sigmoid(gate)
            gate_grad = (hidden_grad * up * logistic * (1.0 + gate * (1.0 - logistic))).astype(BF16)
            up_grad = (hidden_grad * (gate * logistic)).astype(BF16)
            gate_grad_ref[...] = gate_grad
            up_grad_ref[...] = up_grad
            wide = gate_grad.shape[1]
            gate_grads[:, f * wide : (f + 1) * wide] = gate_grad
            up_grads[:, f * wide : (f + 1) * wide] = up_grad

    @pl.when(jnp.logical_and(i >= steps + ff_steps, i < steps + ff_steps + 2))
    def _():
        far_ref[...] = (
            dot(gate_grads[...], gate_w[...], NT) + dot(up_grads[...], up_w[...], NT)
        ).astype(BF16)

    @pl.when(i >= steps + ff_steps + 2)
    def _():
        near_ref[...] = dot(gate_grads[...], gate_w[...], NT) + dot(up_grads[...], up_w[...], NT)


def backward(mine, own, other, down_w, gate_pre, up_pre, gate_w, up_w):
    raw, quarter = own.shape
    model, ff = gate_w.shape
    rows = raw // 2
    steps, ff_steps = raw // TILE, 2
    wide = ff // ff_steps
    last = steps + ff_steps
    ffi = lambda i, m: (0, jnp.clip(i - steps, 0, ff_steps - 1))
    step_rows = GROUP * SLOTS
    return pl.pallas_call(
        functools.partial(backward_kernel, steps, ff_steps),
        grid_spec=pltpu.PrefetchScalarGridSpec(
            num_scalar_prefetch=1,
            grid=(last + 4,),
            in_specs=[
                pl.BlockSpec((TILE, quarter), lambda i, m: (jnp.minimum(i, steps - 1), 0)),
                pl.BlockSpec((TILE, quarter), lambda i, m: (jnp.minimum(i, steps - 1), 0)),
                pl.BlockSpec((wide, model), lambda i, m: (jnp.clip(i - steps, 0, ff_steps - 1), 0)),
                pl.BlockSpec((rows, wide), ffi),
                pl.BlockSpec((rows, wide), ffi),
                pl.BlockSpec((quarter, ff), lambda i, m: (quarter_of(i, last, m), 0)),
                pl.BlockSpec((quarter, ff), lambda i, m: (quarter_of(i, last, m), 0)),
            ],
            out_specs=[
                pl.BlockSpec((rows, wide), ffi),
                pl.BlockSpec((rows, wide), ffi),
                pl.BlockSpec((4, step_rows, quarter), lambda i, m: (0, jnp.minimum(i, steps - 1), 0)),
                pl.BlockSpec((rows, quarter), lambda i, m: (0, jnp.clip(i - last, 0, 1))),
                pl.BlockSpec((rows, quarter), lambda i, m: (0, jnp.clip(i - last - 2, 0, 1))),
            ],
            scratch_shapes=[
                pltpu.VMEM((4, rows, quarter), BF16),
                pltpu.VMEM((rows, ff), BF16),
                pltpu.VMEM((rows, ff), BF16),
            ],
        ),
        out_shape=[
            jax.ShapeDtypeStruct((rows, ff), BF16),
            jax.ShapeDtypeStruct((rows, ff), BF16),
            jax.ShapeDtypeStruct((4, rows, quarter), BF16),
            jax.ShapeDtypeStruct((rows, 2 * quarter), BF16),
            jax.ShapeDtypeStruct((rows, 2 * quarter), F32),
        ],
        compiler_params=params(),
        cost_estimate=cost(6 * rows * model * ff, 6 * model * ff + 30e6),
        name="expert_backward",
    )(mine, own, other, down_w, gate_pre, up_pre, gate_w, up_w)


def pack_kernel(near_ref, far_ref, out_ref):
    order = ordering()
    n = SUB * ROWS
    quarter = out_ref.shape[1]
    for b in range(GROUP // SUB):
        at = slice(b * (n // 2), (b + 1) * (n // 2))
        total = (near_ref[at, :] + far_ref[at, :].astype(F32)).astype(BF16)
        both = jnp.concatenate([total[:, :quarter], total[:, quarter:]], axis=0)
        out_ref[b * n : (b + 1) * n, :] = dot(order, both, TN).astype(BF16)


def pack(near, far):
    rows, width = near.shape
    step_rows = GROUP * SLOTS
    return pl.pallas_call(
        pack_kernel,
        grid=(rows // step_rows,),
        in_specs=[pl.BlockSpec((step_rows, width), lambda i: (i, 0))] * 2,
        out_specs=pl.BlockSpec((TILE, width // 2), lambda i: (i, 0)),
        out_shape=jax.ShapeDtypeStruct((2 * rows, width // 2), BF16),
        compiler_params=params(),
        cost_estimate=cost(2 * rows * width * SUB * ROWS, 8 * rows * width),
        name="pack",
    )(near, far)


def weights_kernel(rows_ref, scaled_ref, hidden_ref, gate_grad_ref, up_grad_ref, gate_w, up_w, down_w):
    rows = rows_ref[0]
    gate_w[...] = dot(rows, gate_grad_ref[...], TN).astype(BF16)
    up_w[...] = dot(rows, up_grad_ref[...], TN).astype(BF16)
    down_w[...] = dot(hidden_ref[...], scaled_ref[0], TN).astype(BF16)


def weight_grads(token_rows, scaled_rows, hidden, gate_grad, up_grad):
    quarters, rows, quarter = token_rows.shape
    ff = hidden.shape[1]
    whole = pl.BlockSpec((rows, ff), lambda i: (0, 0))
    part = pl.BlockSpec((1, rows, quarter), lambda i: (i, 0, 0))
    return pl.pallas_call(
        weights_kernel,
        grid=(quarters,),
        in_specs=[part, part, whole, whole, whole],
        out_specs=[
            pl.BlockSpec((quarter, ff), lambda i: (i, 0)),
            pl.BlockSpec((quarter, ff), lambda i: (i, 0)),
            pl.BlockSpec((ff, quarter), lambda i: (0, i)),
        ],
        out_shape=[
            jax.ShapeDtypeStruct((quarters * quarter, ff), BF16),
            jax.ShapeDtypeStruct((quarters * quarter, ff), BF16),
            jax.ShapeDtypeStruct((ff, quarters * quarter), BF16),
        ],
        compiler_params=params(),
        cost_estimate=cost(6 * rows * quarters * quarter * ff, 10 * quarters * quarter * ff),
        name="weight_grads",
    )(token_rows, scaled_rows, hidden, gate_grad, up_grad)


def outputs_kernel(route_ref, probs_ref, cot_ref, back_ref, out_ref, grad_ref, total):
    i = pl.program_id(0)

    @pl.when(i == 0)
    def _():
        total[...] = jnp.zeros_like(total)
        grad_ref[...] = jnp.zeros_like(grad_ref)

    toks = cot_ref.shape[0]
    half = back_ref.shape[1]
    named, hits = routing(route_ref, i * GROUP)
    sel = selection(named)
    weight = jnp.where(sel, probs_of(hits, probs_ref), 0.0)
    high = weight.astype(BF16)
    low = (weight - high.astype(F32)).astype(BF16)
    back = back_ref[...]
    total[...] += dot(high, back, TN) + dot(low, back, TN)
    products = jnp.where(sel, dot(back, stacked(cot_ref[...]), NT), 0.0)
    sums = jnp.concatenate(
        [
            jnp.sum(products[e * ROWS : (e + 1) * ROWS], axis=0, keepdims=True)
            for e in range(GROUP)
        ],
        axis=0,
    )
    sums = sums[:, :toks] + sums[:, toks:]
    grad_ref[...] += jnp.concatenate(
        [jnp.sum(jnp.where(h, sums, 0.0), axis=0, keepdims=True) for h in hits], axis=0
    )

    @pl.when(i == pl.num_programs(0) - 1)
    def _():
        out_ref[:, :half] = total[:toks].astype(BF16)
        out_ref[:, half:] = total[toks:].astype(BF16)


def token_outputs(route_t, probs_t, cot, back):
    toks, width = cot.shape
    top = route_t.shape[0]
    steps = back.shape[0] // TILE
    small = pl.BlockSpec((top, toks), lambda i: (0, 0))
    wide = pl.BlockSpec((toks, width), lambda i: (0, 0))
    return pl.pallas_call(
        outputs_kernel,
        grid=(steps,),
        in_specs=[small, small, wide, pl.BlockSpec((TILE, width // 2), lambda i: (i, 0))],
        out_specs=[wide, small],
        out_shape=[
            jax.ShapeDtypeStruct((toks, width), BF16),
            jax.ShapeDtypeStruct((top, toks), F32),
        ],
        scratch_shapes=[pltpu.VMEM((2 * toks, width // 2), F32)],
        compiler_params=params(),
        cost_estimate=cost(6 * back.shape[0] * 2 * toks * width // 2, 3 * back.shape[0] * width),
        name="token_outputs",
    )(route_t, probs_t, cot, back)


def inputs_kernel(route_ref, back_ref, out_ref, total):
    i = pl.program_id(0)

    @pl.when(i == 0)
    def _():
        total[...] = jnp.zeros_like(total)

    toks = out_ref.shape[0]
    half = back_ref.shape[1]
    named, _ = routing(route_ref, i * GROUP)
    sel = selection(named).astype(F32).astype(BF16)
    total[...] += dot(sel, back_ref[...], TN)

    @pl.when(i == pl.num_programs(0) - 1)
    def _():
        out_ref[:, :half] = total[:toks].astype(BF16)
        out_ref[:, half:] = total[toks:].astype(BF16)


def token_grads(route_t, back):
    top, toks = route_t.shape
    width = 2 * back.shape[1]
    steps = back.shape[0] // TILE
    return pl.pallas_call(
        inputs_kernel,
        grid=(steps,),
        in_specs=[
            pl.BlockSpec((top, toks), lambda i: (0, 0)),
            pl.BlockSpec((TILE, width // 2), lambda i: (i, 0)),
        ],
        out_specs=pl.BlockSpec((toks, width), lambda i: (0, 0)),
        out_shape=jax.ShapeDtypeStruct((toks, width), BF16),
        scratch_shapes=[pltpu.VMEM((2 * toks, width // 2), F32)],
        compiler_params=params(),
        cost_estimate=cost(2 * back.shape[0] * 2 * toks * width // 2, back.shape[0] * width),
        name="token_grads",
    )(route_t, back)


def exchange(x):
    experts = lax.axis_size("expert")
    y = lax.all_to_all(
        x.reshape(experts, ROWS, -1), "expert", split_axis=0, concat_axis=0, tiled=True
    )
    return y.reshape(x.shape)


def swap(x):
    return lax.ppermute(x, "mp", [(0, 1), (1, 0)])


def body(tokens, cotangent, route_ids, gate_probs, w_gate, w_up, w_down):
    experts = lax.axis_size("expert")
    mine = lax.axis_index("mp").astype(jnp.int32).reshape(1)
    route_t, probs_t = route_ids.T, gate_probs.T
    gate_w, up_w, down_w = w_gate[0], w_up[0], w_down[0]

    got_tokens = exchange(send_rows(False, route_t, probs_t, tokens, experts))
    got_scaled = exchange(send_rows(True, route_t, probs_t, cotangent, experts))

    gate_pre, up_pre, hidden, token_rows, out_far, out_near = forward(
        mine, got_tokens, swap(got_tokens), gate_w, up_w, down_w
    )
    back_out = exchange(pack(out_near, swap(out_far)))

    gate_grad, up_grad, scaled_rows, in_far, in_near = backward(
        mine, got_scaled, swap(got_scaled), down_w, gate_pre, up_pre, gate_w, up_w
    )
    back_in = exchange(pack(in_near, swap(in_far)))

    grad_w_gate, grad_w_up, grad_w_down = weight_grads(
        token_rows, scaled_rows, hidden, gate_grad, up_grad
    )
    layer_out, grad_part = token_outputs(route_t, probs_t, cotangent, back_out)
    grad_probs = lax.psum(grad_part, "mp").T
    grad_tokens = token_grads(route_t, back_in)
    return (
        layer_out, grad_tokens, grad_probs, grad_w_gate[None], grad_w_up[None], grad_w_down[None],
    )


def solution(mesh):
    return jax.shard_map(
        body,
        mesh=mesh,
        in_specs=(
            P("expert", "mp"),
            P("expert", "mp"),
            P("expert", None),
            P("expert", None),
            P("expert", None, "mp"),
            P("expert", None, "mp"),
            P("expert", "mp", None),
        ),
        out_specs=(
            P("expert", "mp"),
            P("expert", "mp"),
            P("expert", None),
            P("expert", None, "mp"),
            P("expert", None, "mp"),
            P("expert", "mp", None),
        ),
        check_vma=False,
    )
```

time: 433 us -> 246 us (0.57)
  waiting for transfers between devices: 210 us -> 44.3 us
  Pallas kernels: 0 us -> 86.1 us
  blocking collectives: 11.6 us -> 92.8 us
  local copies, waits for them, and re-layouts: 72 us -> 3.86 us
  matrix products: 65 us -> 0 us
  starting transfers between devices: 36.9 us -> 15.9 us
  other arithmetic: 18.6 us -> 0 us
  between operations: 14.2 us -> 0.7 us
    all_to_all x4 -> x2, waiting for transfers between devices: 192 us -> 44.3 us  [exchange(): lax.all_to_all(x.reshape(experts, ROWS, -1), 'expert', split_axis=0, conc...]
    all_to_all x0 -> x2, blocking collectives: none -> 88.8 us  [exchange(): lax.all_to_all(x.reshape(experts, ROWS, -1), 'expert', split_axis=0, conc...]
    pallas_call x0 -> x9, Pallas kernels: none -> 86.1 us  [the longest x1 22.2 us: forward(): pl.pallas_call(functools.partial(forward_kernel, steps, ff_steps), grid_s...]
    dot_general x11 -> x0, matrix products: 65 us -> none  [the longest x1 8.98 us: body(): lax.dot_general(scaled_rows, down_mat, contract_last, preferred_element_t...]
    reshape x7 -> x0, local copies, waits for them, and re-layouts: 58.3 us -> none  [the longest x1 13.4 us: body(): input_part.reshape(experts, most_rows, -1)]
    all_to_all x4 -> x2, starting transfers between devices: 36.4 us -> 12.8 us  [exchange(): lax.all_to_all(x.reshape(experts, ROWS, -1), 'expert', split_axis=0, conc...]
    reduce_scatter x2 -> x0, waiting for transfers between devices: 18.6 us -> none  [the longest x1 14.9 us: body(): lax.psum_scatter(input_part.reshape(experts, most_rows, -1), 'mp', scatte...]
    reduce_sum x5 -> x0, other arithmetic: 8.43 us -> none  [the longest x1 3.13 us: body(): grad_tokens = jnp.sum(input_sel, axis=1).astype(jnp.bfloat16)]
  transfers between devices with their start and end apart: 6 -> 6, of which waited for: 6 -> 2; matrix products, arithmetic and copies ran while one was open for 23% -> 0% of each run, Pallas kernels for 0% -> 32%
where the time goes in v1:
time: 246 us; the launch traced here: 244 us
  blocking collectives  92.8 us (38%)
  Pallas kernels  86.1 us (35%)
  waiting for transfers between devices  44.3 us (18%)
  starting transfers between devices  15.9 us (6%)
  local copies, waits for them, and re-layouts  3.86 us (2%)
    all_to_all x2, blocking collectives, exchange(): lax.all_to_all(x.reshape(experts, ROWS, -1), 'expert', split_axis=0, conc...  88.8 us
    all_to_all x2, waiting for transfers between devices, exchange(): lax.all_to_all(x.reshape(experts, ROWS, -1), 'expert', split_axis=0, conc...  44.3 us
    pallas_call x1, Pallas kernels, forward(): pl.pallas_call(functools.partial(forward_kernel, steps, ff_steps), grid_s...  22.2 us
    pallas_call x1, Pallas kernels, backward(): pl.pallas_call(functools.partial(backward_kernel, steps, ff_steps), grid_...  22.1 us
    pallas_call x1, Pallas kernels, weight_grads(): pl.pallas_call(weights_kernel, grid=(quarters,), in_specs=[part, part, wh...  13 us
    all_to_all x2, starting transfers between devices, exchange(): lax.all_to_all(x.reshape(experts, ROWS, -1), 'expert', split_axis=0, conc...  12.8 us
    pallas_call x2, Pallas kernels, pack(): pl.pallas_call(pack_kernel, grid=(rows // step_rows,), in_specs=[pl.Block...  11.9 us
    pallas_call x2, Pallas kernels, send_rows(): pl.pallas_call(functools.partial(send_kernel, scaled), grid=(experts // G...  6.51 us
  transfers between devices with their start and end apart: 6, of which 2 were waited for; matrix products, arithmetic and copies ran while one was open for 0% of the time, Pallas kernels for 32%

profile of v1, /device:TPU:7, one launch (start us, length us, event | category | flops | bytes accessed | tf_op | source)
XLA Modules:
  0.0 243.6 jit_solution(3532097732525526568)
XLA Ops:
  0.6 0.9 copy-done
  1.6 0.7 copy-done.2
  2.3 0.7 copy-done.4
  2.9 3.3 %send_tokens.1 = bf16[1536,896]{1,0:T(8,128)(2,1)} custom-call(s32[8,64]{1,0:T(8,128)S(1)} %bitcast.18, f32[8,64]{1,0:T(8,128)S(1)} %bitcast.22, bf16[64,1792]{1,0:T(8,128)(2,1)S(1)} %copy-done), custom_call_target="tpu_custom_call" | custom-call | flops 352321536 | bytes 2752512 | tf_op jit(solution)/shard_map/send_tokens/pallas_call | solution.py:92
  6.2 45.3 %all_to_all.20 = bf16[64,24,896]{2,1,0:T(8,128)(2,1)} all-to-all(bf16[64,24,896]{2,1,0:T(8,128)(2,1)} %bitcast.28), channel_id=1, replica_groups=mesh['expert'=64,'mp'=2] {'expert'}, dimensions={0} | all-to-all | bytes 5505024 | tf_op jit(solution)/shard_map/all_to_all | solution.py:462
  51.5 2.0 collective-permute-start
  53.5 0.0 copy-done.1
  53.5 3.3 %send_scaled.1 = bf16[1536,896]{1,0:T(8,128)(2,1)} custom-call(s32[8,64]{1,0:T(8,128)S(1)} %bitcast.19, f32[8,64]{1,0:T(8,128)S(1)} %bitcast.23, bf16[64,1792]{1,0:T(8,128)(2,1)S(1)} %copy-done.1), custom_call_target="tpu_custom_call" | custom-call | flops 352321536 | bytes 2752512 | tf_op jit(solution)/shard_map/send_scaled/pallas_call | solution.py:92
  56.7 43.6 %all_to_all.21 = bf16[64,24,896]{2,1,0:T(8,128)(2,1)} all-to-all(bf16[64,24,896]{2,1,0:T(8,128)(2,1)} %bitcast.29), channel_id=1, replica_groups=mesh['expert'=64,'mp'=2] {'expert'}, dimensions={0} | all-to-all | bytes 5505024 | tf_op jit(solution)/shard_map/all_to_all | solution.py:462
  100.3 0.4 collective-permute-start.2
  100.7 0.0 collective-permute-done.other_ref
  100.7 22.2 %expert_forward.1 = (f32[768,512]{1,0:T(8,128)}, f32[768,512]{1,0:T(8,128)}, bf16[768,512]{1,0:T(8,128)(2,1)S(1)}, bf16[4,768,896]{2,1,0:T(8,128)(2,1)}, bf16[768,1792]{1,0:T(8,128)(2,1)}, /*index=5*/f32[768,1792]{1,0:T(8,128)}) custom-call(s32[1]{0:T(128)} %bitcast.2.mine_ref, bf16[1536,896]{1,0:T(8,128)(2,1)} %bitcast.4.own_ref, ...), custom_call_target="tpu_custom_call" | custom-call | flops 8455716864 | bytes 41010048 | tf_op jit(solution)/shard_map/expert_forward/pallas_call | solution.py:181
  122.9 0.1 collective-permute-start.1
  123.0 0.0 collective-permute-done.2.other_ref
  123.0 22.1 %expert_backward.1 = (bf16[768,512]{1,0:T(8,128)(2,1)S(1)}, bf16[768,512]{1,0:T(8,128)(2,1)S(1)}, bf16[4,768,896]{2,1,0:T(8,128)(2,1)}, bf16[768,1792]{1,0:T(8,128)(2,1)}, f32[768,1792]{1,0:T(8,128)}) custom-call(s32[1]{0:T(128)} %bitcast.2.mine_ref, bf16[1536,896]{1,0:T(8,128)(2,1)} %bitcast.11.own_ref, bf16[1536,896]{1,0:T(8,128)(2,1)} %collective-permute-done.2.other_ref, ...), custom_call_target="tpu_custom_call" | custom-call | flops 8455716864 | bytes 41010048 | tf_op jit(solution)/shard_map/expert_backward/pallas_call | solution.py:265
  145.1 0.5 collective-permute-start.3
  145.6 0.0 collective-permute-done.1.far_ref
  145.6 1.5 copy-done.7
  147.2 5.9 %pack.2 = bf16[1536,896]{1,0:T(8,128)(2,1)} custom-call(f32[768,1792]{1,0:T(8,128)} %get-tuple-element.22.near_ref, bf16[768,1792]{1,0:T(8,128)(2,1)} %copy-done.7), custom_call_target="tpu_custom_call" | custom-call | flops 528482304 | bytes 11010048 | tf_op jit(solution)/shard_map/pack/pallas_call | solution.py:319
  153.1 6.9 %all-to-all-start.1 = ((bf16[64,24,896]{2,1,0:T(8,128)(2,1)}), bf16[64,24,896]{2,1,0:T(8,128)(2,1)}, u32[]{:S(2)}, u32[]{:S(2)}) async-start(bf16[64,24,896]{2,1,0:T(8,128)(2,1)} %bitcast.27), calls=%async_computation.1 | async-start | bytes 5505024 | tf_op jit(solution)/shard_map/all_to_all | solution.py:462
  160.0 0.0 collective-permute-done.3.far_ref
  160.0 5.9 %pack.3 = bf16[1536,896]{1,0:T(8,128)(2,1)} custom-call(f32[768,1792]{1,0:T(8,128)} %get-tuple-element.27.near_ref, bf16[768,1792]{1,0:T(8,128)(2,1)} %collective-permute-done.3.far_ref), custom_call_target="tpu_custom_call" | custom-call | flops 528482304 | bytes 11010048 | tf_op jit(solution)/shard_map/pack/pallas_call | solution.py:319
  166.0 31.2 %all-to-all-done.1 = bf16[64,24,896]{2,1,0:T(8,128)(2,1)} async-done(((bf16[64,24,896]{2,1,0:T(8,128)(2,1)}), bf16[64,24,896]{2,1,0:T(8,128)(2,1)}, u32[]{:S(2)}, u32[]{:S(2)}) %all-to-all-start.1) | async-done | bytes 2752544 | tf_op jit(solution)/shard_map/all_to_all | solution.py:462
  197.2 5.9 %all-to-all-start.3 = ((bf16[64,24,896]{2,1,0:T(8,128)(2,1)}), bf16[64,24,896]{2,1,0:T(8,128)(2,1)}, u32[]{:S(2)}, u32[]{:S(2)}) async-start(bf16[64,24,896]{2,1,0:T(8,128)(2,1)} %bitcast.26), calls=%async_computation.3 | async-start | bytes 5505024 | tf_op jit(solution)/shard_map/all_to_all | solution.py:462
  203.1 0.0 copy-start.3
  203.1 0.0 copy-start.5
  203.1 13.0 %weight_grads.1 = (bf16[3584,512]{1,0:T(8,128)(2,1)}, bf16[3584,512]{1,0:T(8,128)(2,1)}, bf16[512,3584]{1,0:T(8,128)(2,1)}) custom-call(bf16[4,768,896]{2,1,0:T(8,128)(2,1)} %get-tuple-element.30.rows_ref, bf16[4,768,896]{2,1,0:T(8,128)(2,1)} %get-tuple-element.31.scaled_ref, bf16[768,512]{1,0:T(8,128)(2,1)S(1)} %get-tuple-element.32.hidden_ref, ...), custom_call_target="tpu_custom_call" | custom-call | flops 8455716864 | bytes 18350080 | tf_op jit(solution)/shard_map/weight_grads/pallas_call | solution.py:343
  216.1 0.0 copy-done.5
  216.1 5.9 %token_outputs.1 = (bf16[64,1792]{1,0:T(8,128)(2,1)}, f32[8,64]{1,0:T(8,128)S(1)}) custom-call(s32[8,64]{1,0:T(8,128)S(1)} %bitcast.20, f32[8,64]{1,0:T(8,128)S(1)} %bitcast.24, bf16[64,1792]{1,0:T(8,128)(2,1)S(1)} %copy-done.1, bf16[1536,896]{1,0:T(8,128)(2,1)} %bitcast.9.back_ref), custom_call_target="tpu_custom_call" | custom-call | flops 1056964608 | bytes 8257536 | tf_op jit(solution)/shard_map/token_outputs/pallas_call | solution.py:405
  222.0 4.0 %psum.7 = f32[64,8]{0,1:T(8,128)} all-reduce(f32[64,8]{0,1:T(8,128)S(1)} %bitcast.25), channel_id=1, replica_groups=mesh['expert'=64,'mp'=2] {'mp'}, use_global_device_ids=true, to_apply=%region_0.0 | all-reduce | flops 512 | bytes 4096 | tf_op jit(solution)/shard_map/psum | solution.py:495
  225.9 13.1 %all-to-all-done.3 = bf16[64,24,896]{2,1,0:T(8,128)(2,1)} async-done(((bf16[64,24,896]{2,1,0:T(8,128)(2,1)}), bf16[64,24,896]{2,1,0:T(8,128)(2,1)}, u32[]{:S(2)}, u32[]{:S(2)}) %all-to-all-start.3) | async-done | bytes 2752544 | tf_op jit(solution)/shard_map/all_to_all | solution.py:462
  239.0 4.6 %token_grads.1 = bf16[64,1792]{1,0:T(8,128)(2,1)} custom-call(s32[8,64]{1,0:T(8,128)S(1)} %bitcast.21, bf16[1536,896]{1,0:T(8,128)(2,1)} %bitcast.13.back_ref), custom_call_target="tpu_custom_call" | custom-call | flops 352321536 | bytes 2752512 | tf_op jit(solution)/shard_map/token_grads/pallas_call | solution.py:444
  (8 shorter events, 0.0 us)
Async XLA Ops:
  0.6 0.9 copy-start
  1.6 0.7 copy-start.2
  2.3 0.7 copy-start.4
  6.2 47.3 %copy-start.1 = (bf16[64,1792]{1,0:T(8,128)(2,1)S(1)}, bf16[64,1792]{1,0:T(8,128)(2,1)}, u32[]{:S(2)}) copy-start(bf16[64,1792]{1,0:T(8,128)(2,1)} %rows_ref.3) | copy-start | bytes 688132
  51.5 49.3 %collective-permute-start = (bf16[1536,896]{1,0:T(8,128)(2,1)}, bf16[1536,896]{1,0:T(8,128)(2,1)}, u32[]{:S(2)}, u32[]{:S(2)}) collective-permute-start(bf16[1536,896]{1,0:T(8,128)(2,1)} %bitcast.4.own_ref), channel_id=1, source_target_pairs={{0,1},{1,0},{2,3},{3,2},{4,5},{5,4},{6,7},{7,6},{8,9},{9,8},{10,11... | collective-permute-start | bytes 8257544 | tf_op jit(solution)/shard_map/ppermute | solution.py:469
  100.3 22.7 %collective-permute-start.2 = (bf16[1536,896]{1,0:T(8,128)(2,1)}, bf16[1536,896]{1,0:T(8,128)(2,1)}, u32[]{:S(2)}, u32[]{:S(2)}) collective-permute-start(bf16[1536,896]{1,0:T(8,128)(2,1)} %bitcast.11.own_ref), channel_id=1, source_target_pairs={{0,1},{1,0},{2,3},{3,2},{4,5},{5,4},{6,7},{7,6},{8,9},{9,8},{10,11... | collective-permute-start | bytes 8257544 | tf_op jit(solution)/shard_map/ppermute | solution.py:469
  122.9 22.7 %collective-permute-start.1 = (bf16[768,1792]{1,0:T(8,128)(2,1)}, bf16[768,1792]{1,0:T(8,128)(2,1)S(1)}, u32[]{:S(2)}, u32[]{:S(2)}) collective-permute-start(bf16[768,1792]{1,0:T(8,128)(2,1)} %get-tuple-element.23), channel_id=1, source_target_pairs={{0,1},{1,0},{2,3},{3,2},{4,5},{5,4},{6,7},{7,6},{8,9},{9,8},{10,11... | collective-permute-start | bytes 8257544 | tf_op jit(solution)/shard_map/ppermute | solution.py:469
  145.1 8.0 %copy-start.6 = (bf16[768,512]{1,0:T(8,128)(2,1)}, bf16[768,512]{1,0:T(8,128)(2,1)S(1)}, u32[]{:S(2)}) copy-start(bf16[768,512]{1,0:T(8,128)(2,1)S(1)} %get-tuple-element.34.up_grad_ref) | copy-start | bytes 2359300
  145.1 14.9 %collective-permute-start.3 = (bf16[768,1792]{1,0:T(8,128)(2,1)}, bf16[768,1792]{1,0:T(8,128)(2,1)}, u32[]{:S(2)}, u32[]{:S(2)}) collective-permute-start(bf16[768,1792]{1,0:T(8,128)(2,1)} %get-tuple-element.28), channel_id=1, source_target_pairs={{0,1},{1,0},{2,3},{3,2},{4,5},{5,4},{6,7},{7,6},{8,9},{9,8},{10,11... | collective-permute-start | bytes 8257544 | tf_op jit(solution)/shard_map/ppermute | solution.py:469
  145.6 1.5 copy-start.7
  153.1 44.1 %all-to-all-start.1 = ((bf16[64,24,896]{2,1,0:T(8,128)(2,1)}), bf16[64,24,896]{2,1,0:T(8,128)(2,1)}, u32[]{:S(2)}, u32[]{:S(2)}) async-start(bf16[64,24,896]{2,1,0:T(8,128)(2,1)} %bitcast.27), calls=%async_computation.1 | async-start | bytes 5505024 | tf_op jit(solution)/shard_map/all_to_all | solution.py:462
  197.2 41.8 %all-to-all-start.3 = ((bf16[64,24,896]{2,1,0:T(8,128)(2,1)}), bf16[64,24,896]{2,1,0:T(8,128)(2,1)}, u32[]{:S(2)}, u32[]{:S(2)}) async-start(bf16[64,24,896]{2,1,0:T(8,128)(2,1)} %bitcast.26), calls=%async_computation.3 | async-start | bytes 5505024 | tf_op jit(solution)/shard_map/all_to_all | solution.py:462
  203.1 13.0 %copy-start.3 = (s32[64,8]{0,1:T(8,128)S(1)}, s32[64,8]{0,1:T(8,128)}, u32[]{:S(2)}) copy-start(s32[64,8]{0,1:T(8,128)} %param.9) | copy-start | bytes 6148
  203.1 13.0 %copy-start.5 = (f32[64,8]{0,1:T(8,128)S(1)}, f32[64,8]{0,1:T(8,128)}, u32[]{:S(2)}) copy-start(f32[64,8]{0,1:T(8,128)} %param.10) | copy-start | bytes 6148

commit v2 on v1

--- a/solution.py
+++ b/solution.py
@@ -29,8 +29,8 @@
     )
 
 
-def cost(flops, nbytes):
-    return pl.CostEstimate(flops=int(flops), bytes_accessed=int(nbytes), transcendentals=0)
+def cost():
+    return pl.CostEstimate(flops=1, bytes_accessed=1, transcendentals=0)
 
 
 def spread(rows_of):
@@ -100,7 +100,7 @@
         out_specs=pl.BlockSpec((TILE, half), lambda i: (i, 0)),
         out_shape=jax.ShapeDtypeStruct((experts * ROWS, half), BF16),
         compiler_params=params(),
-        cost_estimate=cost(2 * experts * ROWS * 2 * toks * half, experts * ROWS * half * 2),
+        cost_estimate=cost(),
         name="send_scaled" if scaled else "send_tokens",
     )(route_t, probs_t, rows)
 
@@ -131,17 +131,31 @@
                 out_ref[2 * which + h, b * (n // 2) : (b + 1) * (n // 2), :] = part
 
 
+def put_all_in_order(i, steps, own_ref, others, mine, held, out_ref):
+    each = steps // len(others)
+    for p, ref in enumerate(others):
+        @pl.when(jnp.logical_and(i >= p * each, i < (p + 1) * each))
+        def _():
+            put_in_order(own_ref, ref, mine, i, held, out_ref)
+
+
+def piece_specs(quarter, steps, pieces):
+    each = steps // pieces
+    return [
+        pl.BlockSpec((TILE, quarter), lambda i, m, p=p: (jnp.clip(i - p * each, 0, each - 1), 0))
+        for p in range(pieces)
+    ]
+
+
 def forward_kernel(
-    steps, ff_steps, mine_ref, own_ref, other_ref, gate_w, up_w, down_w,
-    gate_ref, up_ref, hidden_ref, rows_ref, far_ref, near_ref, held, hidden_all,
+    steps, ff_steps, mine_ref, own_ref, other0, other1, gate_w, up_w, down_w,
+    gate_ref, up_ref, hidden_ref, rows_ref, far0, far1, near_ref, held, hidden_all,
 ):
     i = pl.program_id(0)
     mine = mine_ref[0]
     quarter = own_ref.shape[1]
 
-    @pl.when(i < steps)
-    def _():
-        put_in_order(own_ref, other_ref, mine, i, held, rows_ref)
+    put_all_in_order(i, steps, own_ref, (other0, other1), mine, held, rows_ref)
 
     for f in range(ff_steps):
         @pl.when(i == steps + f)
@@ -155,9 +169,10 @@
             wide = hidden.shape[1]
             hidden_all[:, f * wide : (f + 1) * wide] = hidden
 
-    @pl.when(jnp.logical_and(i >= steps + ff_steps, i < steps + ff_steps + 2))
-    def _():
-        far_ref[...] = dot(hidden_all[...], down_w[...]).astype(BF16)
+    for h, far_ref in enumerate((far0, far1)):
+        @pl.when(i == steps + ff_steps + h)
+        def _():
+            far_ref[...] = dot(hidden_all[...], down_w[...]).astype(BF16)
 
     @pl.when(i >= steps + ff_steps + 2)
     def _():
@@ -169,7 +184,7 @@
     return jnp.where(q < 2, 2 * (1 - mine[0]) + q, 2 * mine[0] + q - 2)
 
 
-def forward(mine, own, other, gate_w, up_w, down_w):
+def forward(mine, own, others, gate_w, up_w, down_w):
     raw, quarter = own.shape
     model, ff = gate_w.shape
     rows = raw // 2
@@ -185,7 +200,7 @@
             grid=(last + 4,),
             in_specs=[
                 pl.BlockSpec((TILE, quarter), lambda i, m: (jnp.minimum(i, steps - 1), 0)),
-                pl.BlockSpec((TILE, quarter), lambda i, m: (jnp.minimum(i, steps - 1), 0)),
+                *piece_specs(quarter, steps, len(others)),
                 pl.BlockSpec((model, wide), ffi),
                 pl.BlockSpec((model, wide), ffi),
                 pl.BlockSpec((ff, quarter), lambda i, m: (0, quarter_of(i, last, m))),
@@ -195,7 +210,8 @@
                 pl.BlockSpec((rows, wide), ffi),
                 pl.BlockSpec((rows, wide), ffi),
                 pl.BlockSpec((4, step_rows, quarter), lambda i, m: (0, jnp.minimum(i, steps - 1), 0)),
-                pl.BlockSpec((rows, quarter), lambda i, m: (0, jnp.clip(i - last, 0, 1))),
+                pl.BlockSpec((rows, quarter), lambda i, m: (0, 0)),
+                pl.BlockSpec((rows, quarter), lambda i, m: (0, 0)),
                 pl.BlockSpec((rows, quarter), lambda i, m: (0, jnp.clip(i - last - 2, 0, 1))),
             ],
             scratch_shapes=[pltpu.VMEM((4, rows, quarter), BF16), pltpu.VMEM((rows, ff), BF16)],
@@ -205,26 +221,25 @@
             jax.ShapeDtypeStruct((rows, ff), F32),
             jax.ShapeDtypeStruct((rows, ff), BF16),
             jax.ShapeDtypeStruct((4, rows, quarter), BF16),
-            jax.ShapeDtypeStruct((rows, 2 * quarter), BF16),
+            jax.ShapeDtypeStruct((rows, quarter), BF16),
+            jax.ShapeDtypeStruct((rows, quarter), BF16),
             jax.ShapeDtypeStruct((rows, 2 * quarter), F32),
         ],
         compiler_params=params(),
-        cost_estimate=cost(6 * rows * model * ff, 6 * model * ff + 30e6),
+        cost_estimate=cost(),
         name="expert_forward",
-    )(mine, own, other, gate_w, up_w, down_w)
+    )(mine, own, *others, gate_w, up_w, down_w)
 
 
 def backward_kernel(
-    steps, ff_steps, mine_ref, own_ref, other_ref, down_w, gate_ref, up_ref, gate_w, up_w,
-    gate_grad_ref, up_grad_ref, rows_ref, far_ref, near_ref, held, gate_grads, up_grads,
+    steps, ff_steps, mine_ref, own_ref, other0, other1, down_w, gate_ref, up_ref, gate_w, up_w,
+    gate_grad_ref, up_grad_ref, rows_ref, far0, far1, near_ref, held, gate_grads, up_grads,
 ):
     i = pl.program_id(0)
     mine = mine_ref[0]
     quarter = own_ref.shape[1]
 
-    @pl.when(i < steps)
-    def _():
-        put_in_order(own_ref, other_ref, mine, i, held, rows_ref)
+    put_all_in_order(i, steps, own_ref, (other0, other1), mine, held, rows_ref)
 
     for f in range(ff_steps):
         @pl.when(i == steps + f)
@@ -242,18 +257,19 @@
             gate_grads[:, f * wide : (f + 1) * wide] = gate_grad
             up_grads[:, f * wide : (f + 1) * wide] = up_grad
 
-    @pl.when(jnp.logical_and(i >= steps + ff_steps, i < steps + ff_steps + 2))
-    def _():
-        far_ref[...] = (
-            dot(gate_grads[...], gate_w[...], NT) + dot(up_grads[...], up_w[...], NT)
-        ).astype(BF16)
+    for h, far_ref in enumerate((far0, far1)):
+        @pl.when(i == steps + ff_steps + h)
+        def _():
+            far_ref[...] = (
+                dot(gate_grads[...], gate_w[...], NT) + dot(up_grads[...], up_w[...], NT)
+            ).astype(BF16)
 
     @pl.when(i >= steps + ff_steps + 2)
     def _():
         near_ref[...] = dot(gate_grads[...], gate_w[...], NT) + dot(up_grads[...], up_w[...], NT)
 
 
-def backward(mine, own, other, down_w, gate_pre, up_pre, gate_w, up_w):
+def backward(mine, own, others, down_w, gate_pre, up_pre, gate_w, up_w):
     raw, quarter = own.shape
     model, ff = gate_w.shape
     rows = raw // 2
@@ -269,7 +285,7 @@
             grid=(last + 4,),
             in_specs=[
                 pl.BlockSpec((TILE, quarter), lambda i, m: (jnp.minimum(i, steps - 1), 0)),
-                pl.BlockSpec((TILE, quarter), lambda i, m: (jnp.minimum(i, steps - 1), 0)),
+                *piece_specs(quarter, steps, len(others)),
                 pl.BlockSpec((wide, model), lambda i, m: (jnp.clip(i - steps, 0, ff_steps - 1), 0)),
                 pl.BlockSpec((rows, wide), ffi),
                 pl.BlockSpec((rows, wide), ffi),
@@ -280,7 +296,8 @@
                 pl.BlockSpec((rows, wide), ffi),
                 pl.BlockSpec((rows, wide), ffi),
                 pl.BlockSpec((4, step_rows, quarter), lambda i, m: (0, jnp.minimum(i, steps - 1), 0)),
-                pl.BlockSpec((rows, quarter), lambda i, m: (0, jnp.clip(i - last, 0, 1))),
+                pl.BlockSpec((rows, quarter), lambda i, m: (0, 0)),
+                pl.BlockSpec((rows, quarter), lambda i, m: (0, 0)),
                 pl.BlockSpec((rows, quarter), lambda i, m: (0, jnp.clip(i - last - 2, 0, 1))),
             ],
             scratch_shapes=[
@@ -293,39 +310,49 @@
             jax.ShapeDtypeStruct((rows, ff), BF16),
             jax.ShapeDtypeStruct((rows, ff), BF16),
             jax.ShapeDtypeStruct((4, rows, quarter), BF16),
-            jax.ShapeDtypeStruct((rows, 2 * quarter), BF16),
+            jax.ShapeDtypeStruct((rows, quarter), BF16),
+            jax.ShapeDtypeStruct((rows, quarter), BF16),
             jax.ShapeDtypeStruct((rows, 2 * quarter), F32),
         ],
         compiler_params=params(),
-        cost_estimate=cost(6 * rows * model * ff, 6 * model * ff + 30e6),
+        cost_estimate=cost(),
         name="expert_backward",
-    )(mine, own, other, down_w, gate_pre, up_pre, gate_w, up_w)
-
-
-def pack_kernel(near_ref, far_ref, out_ref):
+    )(mine, own, *others, down_w, gate_pre, up_pre, gate_w, up_w)
+
+
+def pack_kernel(near_ref, far0, far1, out_ref):
     order = ordering()
     n = SUB * ROWS
     quarter = out_ref.shape[1]
     for b in range(GROUP // SUB):
         at = slice(b * (n // 2), (b + 1) * (n // 2))
-        total = (near_ref[at, :] + far_ref[at, :].astype(F32)).astype(BF16)
-        both = jnp.concatenate([total[:, :quarter], total[:, quarter:]], axis=0)
+        both = jnp.concatenate(
+            [
+                (near_ref[at, h * quarter : (h + 1) * quarter] + far[at, :].astype(F32)).astype(BF16)
+                for h, far in enumerate((far0, far1))
+            ],
+            axis=0,
+        )
         out_ref[b * n : (b + 1) * n, :] = dot(order, both, TN).astype(BF16)
 
 
-def pack(near, far):
+def pack(near, fars):
     rows, width = near.shape
     step_rows = GROUP * SLOTS
     return pl.pallas_call(
         pack_kernel,
         grid=(rows // step_rows,),
-        in_specs=[pl.BlockSpec((step_rows, width), lambda i: (i, 0))] * 2,
+        in_specs=[
+            pl.BlockSpec((step_rows, width), lambda i: (i, 0)),
+            pl.BlockSpec((step_rows, width // 2), lambda i: (i, 0)),
+            pl.BlockSpec((step_rows, width // 2), lambda i: (i, 0)),
+        ],
         out_specs=pl.BlockSpec((TILE, width // 2), lambda i: (i, 0)),
         out_shape=jax.ShapeDtypeStruct((2 * rows, width // 2), BF16),
         compiler_params=params(),
-        cost_estimate=cost(2 * rows * width * SUB * ROWS, 8 * rows * width),
+        cost_estimate=cost(),
         name="pack",
-    )(near, far)
+    )(near, *fars)
 
 
 def weights_kernel(rows_ref, scaled_ref, hidden_ref, gate_grad_ref, up_grad_ref, gate_w, up_w, down_w):
@@ -355,7 +382,7 @@
             jax.ShapeDtypeStruct((ff, quarters * quarter), BF16),
         ],
         compiler_params=params(),
-        cost_estimate=cost(6 * rows * quarters * quarter * ff, 10 * quarters * quarter * ff),
+        cost_estimate=cost(),
         name="weight_grads",
     )(token_rows, scaled_rows, hidden, gate_grad, up_grad)
 
@@ -413,7 +440,7 @@
         ],
         scratch_shapes=[pltpu.VMEM((2 * toks, width // 2), F32)],
         compiler_params=params(),
-        cost_estimate=cost(6 * back.shape[0] * 2 * toks * width // 2, 3 * back.shape[0] * width),
+        cost_estimate=cost(),
         name="token_outputs",
     )(route_t, probs_t, cot, back)
 
@@ -452,7 +479,7 @@
         out_shape=jax.ShapeDtypeStruct((toks, width), BF16),
         scratch_shapes=[pltpu.VMEM((2 * toks, width // 2), F32)],
         compiler_params=params(),
-        cost_estimate=cost(2 * back.shape[0] * 2 * toks * width // 2, back.shape[0] * width),
+        cost_estimate=cost(),
         name="token_grads",
     )(route_t, back)
 
@@ -465,8 +492,13 @@
     return y.reshape(x.shape)
 
 
-def swap(x):
-    return lax.ppermute(x, "mp", [(0, 1), (1, 0)])
+def swap(*parts):
+    return [lax.ppermute(x, "mp", [(0, 1), (1, 0)]) for x in parts]
+
+
+def halves(x):
+    half = x.shape[0] // 2
+    return x[:half], x[half:]
 
 
 def body(tokens, cotangent, route_ids, gate_probs, w_gate, w_up, w_down):
@@ -475,18 +507,24 @@
     route_t, probs_t = route_ids.T, gate_probs.T
     gate_w, up_w, down_w = w_gate[0], w_up[0], w_down[0]
 
-    got_tokens = exchange(send_rows(False, route_t, probs_t, tokens, experts))
-    got_scaled = exchange(send_rows(True, route_t, probs_t, cotangent, experts))
-
-    gate_pre, up_pre, hidden, token_rows, out_far, out_near = forward(
-        mine, got_tokens, swap(got_tokens), gate_w, up_w, down_w
-    )
-    back_out = exchange(pack(out_near, swap(out_far)))
-
-    gate_grad, up_grad, scaled_rows, in_far, in_near = backward(
-        mine, got_scaled, swap(got_scaled), down_w, gate_pre, up_pre, gate_w, up_w
-    )
-    back_in = exchange(pack(in_near, swap(in_far)))
+    send_tokens = send_rows(False, route_t, probs_t, tokens, experts)
+    send_scaled = send_rows(True, route_t, probs_t, cotangent, experts)
+    got_tokens, send_scaled = lax.optimization_barrier((exchange(send_tokens), send_scaled))
+    got_scaled = exchange(send_scaled)
+
+    gate_pre, up_pre, hidden, token_rows, far0, far1, out_near = forward(
+        mine, got_tokens, swap(*halves(got_tokens)), gate_w, up_w, down_w
+    )
+    send_out = pack(out_near, swap(far0, far1))
+    got_scaled, send_out = lax.optimization_barrier((got_scaled, send_out))
+    back_out = exchange(send_out)
+
+    gate_grad, up_grad, scaled_rows, far0, far1, in_near = backward(
+        mine, got_scaled, swap(*halves(got_scaled)), down_w, gate_pre, up_pre, gate_w, up_w
+    )
+    send_in = pack(in_near, swap(far0, far1))
+    back_out, send_in = lax.optimization_barrier((back_out, send_in))
+    back_in = exchange(send_in)
 
     grad_w_gate, grad_w_up, grad_w_down = weight_grads(
         token_rows, scaled_rows, hidden, gate_grad, up_grad

time: 246 us -> 201 us (0.82)
  blocking collectives: 92.8 us -> 3.59 us
  starting transfers between devices: 15.9 us -> 38.8 us
  waiting for transfers between devices: 44.3 us -> 60.6 us
  local copies, waits for them, and re-layouts: 3.86 us -> 10.4 us
    all_to_all x2 -> x0, blocking collectives: 88.8 us -> none  [exchange(): lax.all_to_all(x.reshape(experts, ROWS, -1), 'expert', split_axis=0, conc...]
    all_to_all x2 -> x4, starting transfers between devices: 12.8 us -> 34.6 us  [exchange(): lax.all_to_all(x.reshape(experts, ROWS, -1), 'expert', split_axis=0, conc...]
    ppermute x4 -> x8, waiting for transfers between devices: 0.01 us -> 9.78 us  [swap(): return [lax.ppermute(x, 'mp', [(0, 1), (1, 0)]) for x in parts]]
    all_to_all x2 -> x4, waiting for transfers between devices: 44.3 us -> 50.8 us  [exchange(): lax.all_to_all(x.reshape(experts, ROWS, -1), 'expert', split_axis=0, conc...]
    slice x0 -> x2, local copies, waits for them, and re-layouts: none -> 5.02 us  [halves(): return (x[:half], x[half:])]
    unnamed x16 -> x18, local copies, waits for them, and re-layouts: 3.86 us -> 5.35 us
  transfers between devices with their start and end apart: 6 -> 12, of which waited for: 2 -> 8; matrix products, arithmetic and copies ran while one was open for 0% -> 0% of each run, Pallas kernels for 32% -> 39%
where the time goes in v2:
time: 201 us; the launch traced here: 200 us
  Pallas kernels  85.4 us (42%)
  waiting for transfers between devices  60.6 us (30%)
  starting transfers between devices  38.8 us (19%)
  local copies, waits for them, and re-layouts  10.4 us (5%)
  blocking collectives  3.59 us (2%)
    all_to_all x4, waiting for transfers between devices, exchange(): lax.all_to_all(x.reshape(experts, ROWS, -1), 'expert', split_axis=0, conc...  50.8 us
    all_to_all x4, starting transfers between devices, exchange(): lax.all_to_all(x.reshape(experts, ROWS, -1), 'expert', split_axis=0, conc...  34.6 us
    pallas_call x1, Pallas kernels, backward(): pl.pallas_call(functools.partial(backward_kernel, steps, ff_steps), grid_...  22.4 us
    pallas_call x1, Pallas kernels, forward(): pl.pallas_call(functools.partial(forward_kernel, steps, ff_steps), grid_s...  21.8 us
    pallas_call x1, Pallas kernels, weight_grads(): pl.pallas_call(weights_kernel, grid=(quarters,), in_specs=[part, part, wh...  13 us
    pallas_call x2, Pallas kernels, pack(): pl.pallas_call(pack_kernel, grid=(rows // step_rows,), in_specs=[pl.Block...  11.2 us
    ppermute x8, waiting for transfers between devices, swap(): return [lax.ppermute(x, 'mp', [(0, 1), (1, 0)]) for x in parts]  9.78 us
    pallas_call x2, Pallas kernels, send_rows(): pl.pallas_call(functools.partial(send_kernel, scaled), grid=(experts // G...  6.53 us
  transfers between devices with their start and end apart: 12, of which 8 were waited for; matrix products, arithmetic and copies ran while one was open for 0% of the time, Pallas kernels for 39%

profile of v2, /device:TPU:7, one launch (start us, length us, event | category | flops | bytes accessed | tf_op | source)
XLA Modules:
  0.0 199.6 jit_solution(4683715497899174403)
XLA Ops:
  0.6 0.9 copy-done.2
  2.9 3.3 %send_tokens.1 = bf16[1536,896]{1,0:T(8,128)(2,1)} custom-call(s32[8,64]{1,0:T(8,128)S(1)} %bitcast.18, f32[8,64]{1,0:T(8,128)S(1)} %bitcast.22, bf16[64,1792]{1,0:T(8,128)(2,1)S(1)} %copy-done.2), custom_call_target="tpu_custom_call" | custom-call | flops 1 | bytes 1 | tf_op jit(solution)/shard_map/send_tokens/pallas_call | solution.py:92
  6.2 11.2 %all-to-all-start = ((bf16[64,24,896]{2,1,0:T(8,128)(2,1)}), bf16[64,24,896]{2,1,0:T(8,128)(2,1)}, u32[]{:S(2)}, u32[]{:S(2)}) async-start(bf16[64,24,896]{2,1,0:T(8,128)(2,1)} %bitcast.34), calls=%async_computation | async-start | bytes 5505024 | tf_op jit(solution)/shard_map/all_to_all | solution.py:489
  17.4 3.3 %send_scaled.1 = bf16[1536,896]{1,0:T(8,128)(2,1)} custom-call(s32[8,64]{1,0:T(8,128)S(1)} %bitcast.19, f32[8,64]{1,0:T(8,128)S(1)} %bitcast.23, bf16[64,1792]{1,0:T(8,128)(2,1)S(1)} %copy-done), custom_call_target="tpu_custom_call" | custom-call | flops 1 | bytes 1 | tf_op jit(solution)/shard_map/send_scaled/pallas_call | solution.py:92
  20.7 32.7 %all-to-all-done = bf16[64,24,896]{2,1,0:T(8,128)(2,1)} async-done(((bf16[64,24,896]{2,1,0:T(8,128)(2,1)}), bf16[64,24,896]{2,1,0:T(8,128)(2,1)}, u32[]{:S(2)}, u32[]{:S(2)}) %all-to-all-start) | async-done | bytes 2752544 | tf_op jit(solution)/shard_map/all_to_all | solution.py:489
  53.4 2.0 fusion.1
  55.4 1.2 collective-permute-start.1
  56.7 7.1 %all-to-all-start.1 = ((bf16[64,24,896]{2,1,0:T(8,128)(2,1)}), bf16[64,24,896]{2,1,0:T(8,128)(2,1)}, u32[]{:S(2)}, u32[]{:S(2)}) async-start(bf16[64,24,896]{2,1,0:T(8,128)(2,1)} %bitcast.4), calls=%async_computation.1 | async-start | bytes 5505024 | tf_op jit(solution)/shard_map/all_to_all | solution.py:489
  63.9 21.8 %expert_forward.1 = (f32[768,512]{1,0:T(8,128)}, f32[768,512]{1,0:T(8,128)}, bf16[768,512]{1,0:T(8,128)(2,1)S(1)}, bf16[4,768,896]{2,1,0:T(8,128)(2,1)}, bf16[76...) custom-call(s32[1]{0:T(128)} %bitcast.6.mine_ref, bf16[1536,896]{1,0:T(8,128)(2,1)} %bitcast.3.own_ref, ...), custom_call_target="tpu_custom_call" | custom-call | flops 1 | bytes 1 | tf_op jit(solution)/shard_map/expert_forward/pallas_call | solution.py:196
  85.7 1.0 collective-permute-start.2
  86.8 2.9 %collective-permute-done.2.far0 = bf16[768,896]{1,0:T(8,128)(2,1)S(1)} collective-permute-done((bf16[768,896]{1,0:T(8,128)(2,1)}, bf16[768,896]{1,0:T(8,128)(2,1)S(1)}, u32[]{:S(2)}, u32[]{:S(2)}) %collective-permute-start.2) | collective-permute-done | bytes 1376288 | tf_op jit(solution)/shard_map/ppermute | solution.py:496
  89.7 2.0 collective-permute-done.3.far1
  91.7 1.1 copy-done.7
  92.8 5.6 %pack.2 = bf16[1536,896]{1,0:T(8,128)(2,1)} custom-call(f32[768,1792]{1,0:T(8,128)} %get-tuple-element.32.near_ref, bf16[768,896]{1,0:T(8,128)(2,1)S(1)} %collective-permute-done.2.far0, bf16[768,896]{1,0:T(8,128)(2,1)} %copy-done.7), custom_call_target="tpu_custom_call" | custom-call | flops 1 | bytes 1 | tf_op jit(solution)/shard_map/pack/pallas_call | solution.py:342
  98.3 2.4 %all-to-all-done.1 = bf16[64,24,896]{2,1,0:T(8,128)(2,1)} async-done(((bf16[64,24,896]{2,1,0:T(8,128)(2,1)}), bf16[64,24,896]{2,1,0:T(8,128)(2,1)}, u32[]{:S(2)}, u32[]{:S(2)}) %all-to-all-start.1) | async-done | bytes 2752544 | tf_op jit(solution)/shard_map/all_to_all | solution.py:489
  100.8 3.0 %fusion = (bf16[768,896]{1,0:T(8,128)(2,1)}, bf16[768,896]{1,0:T(8,128)(2,1)S(1)}) fusion(bf16[1536,896]{1,0:T(8,128)(2,1)} %bitcast.5.own_ref), kind=kLoop, calls=%fused_computation | loop fusion | bytes 5505024 | tf_op jit(solution)/shard_map/slice | solution.py:501
  103.8 0.7 collective-permute-start.5
  104.5 7.5 %all-to-all-start.2 = ((bf16[64,24,896]{2,1,0:T(8,128)(2,1)}), bf16[64,24,896]{2,1,0:T(8,128)(2,1)}, u32[]{:S(2)}, u32[]{:S(2)}) async-start(bf16[64,24,896]{2,1,0:T(8,128)(2,1)} %bitcast.32), calls=%async_computation.2 | async-start | bytes 5505024 | tf_op jit(solution)/shard_map/all_to_all | solution.py:489
  112.1 22.4 %expert_backward.1 = (bf16[768,512]{1,0:T(8,128)(2,1)S(1)}, bf16[768,512]{1,0:T(8,128)(2,1)S(1)}, bf16[4,768,896]{2,1,0:T(8,128)(2,1)}, bf16[768,896]{1,0:T(8,12...) custom-call(s32[1]{0:T(128)} %bitcast.6.mine_ref, bf16[1536,896]{1,0:T(8,128)(2,1)} %bitcast.5.own_ref, ...), custom_call_target="tpu_custom_call" | custom-call | flops 1 | bytes 1 | tf_op jit(solution)/shard_map/expert_backward/pallas_call | solution.py:281
  134.4 0.9 copy-done.1
  135.3 1.0 collective-permute-start.6
  136.3 3.0 %collective-permute-done.6.far0 = bf16[768,896]{1,0:T(8,128)(2,1)S(1)} collective-permute-done((bf16[768,896]{1,0:T(8,128)(2,1)}, bf16[768,896]{1,0:T(8,128)(2,1)S(1)}, u32[]{:S(2)}, u32[]{:S(2)}) %collective-permute-start.6) | collective-permute-done | bytes 1376288 | tf_op jit(solution)/shard_map/ppermute | solution.py:496
  139.3 2.0 collective-permute-done.7.far1
  141.2 1.1 copy-done.8
  142.3 5.6 %pack.3 = bf16[1536,896]{1,0:T(8,128)(2,1)} custom-call(f32[768,1792]{1,0:T(8,128)} %get-tuple-element.39.near_ref, bf16[768,896]{1,0:T(8,128)(2,1)S(1)} %collective-permute-done.6.far0, bf16[768,896]{1,0:T(8,128)(2,1)} %copy-done.8), custom_call_target="tpu_custom_call" | custom-call | flops 1 | bytes 1 | tf_op jit(solution)/shard_map/pack/pallas_call | solution.py:342
  147.9 1.1 all-to-all-done.2
  149.0 8.8 %all-to-all-start.3 = ((bf16[64,24,896]{2,1,0:T(8,128)(2,1)}), bf16[64,24,896]{2,1,0:T(8,128)(2,1)}, u32[]{:S(2)}, u32[]{:S(2)}) async-start(bf16[64,24,896]{2,1,0:T(8,128)(2,1)} %bitcast.33), calls=%async_computation.3 | async-start | bytes 5505024 | tf_op jit(solution)/shard_map/all_to_all | solution.py:489
  157.9 13.0 %weight_grads.1 = (bf16[3584,512]{1,0:T(8,128)(2,1)}, bf16[3584,512]{1,0:T(8,128)(2,1)}, bf16[512,3584]{1,0:T(8,128)(2,1)}) custom-call(bf16[4,768,896]{2,1,0:T(8,128)(2,1)} %get-tuple-element.46.rows_ref, bf16[4,768,896]{2,1,0:T(8,128)(2,1)} %get-tuple-element.47.scaled_ref, bf16[768,512]{1,0:T(8,128)(2,1)S(1)} %get-tuple-element.48.hidden_ref, ...), custom_call_target="tpu_custom_call" | custom-call | flops 1 | bytes 1 | tf_op jit(solution)/shard_map/weight_grads/pallas_call | solution.py:370
  170.9 5.9 %token_outputs.1 = (bf16[64,1792]{1,0:T(8,128)(2,1)}, f32[8,64]{1,0:T(8,128)S(1)}) custom-call(s32[8,64]{1,0:T(8,128)S(1)} %bitcast.20, f32[8,64]{1,0:T(8,128)S(1)} %bitcast.24, bf16[64,1792]{1,0:T(8,128)(2,1)S(1)} %copy-done, bf16[1536,896]{1,0:T(8,128)(2,1)} %bitcast.11.back_ref), custom_call_target="tpu_custom_call" | custom-call | flops 1 | bytes 1 | tf_op jit(solution)/shard_map/token_outputs/pallas_call | solution.py:432
  176.8 3.6 %psum.7 = f32[64,8]{0,1:T(8,128)} all-reduce(f32[64,8]{0,1:T(8,128)S(1)} %bitcast.25), channel_id=1, replica_groups=mesh['expert'=64,'mp'=2] {'mp'}, use_global_device_ids=true, to_apply=%region_0.0 | all-reduce | flops 512 | bytes 4096 | tf_op jit(solution)/shard_map/psum | solution.py:533
  180.4 14.6 %all-to-all-done.3 = bf16[64,24,896]{2,1,0:T(8,128)(2,1)} async-done(((bf16[64,24,896]{2,1,0:T(8,128)(2,1)}), bf16[64,24,896]{2,1,0:T(8,128)(2,1)}, u32[]{:S(2)}, u32[]{:S(2)}) %all-to-all-start.3) | async-done | bytes 2752544 | tf_op jit(solution)/shard_map/all_to_all | solution.py:489
  195.0 4.6 %token_grads.1 = bf16[64,1792]{1,0:T(8,128)(2,1)} custom-call(s32[8,64]{1,0:T(8,128)S(1)} %bitcast.21, bf16[1536,896]{1,0:T(8,128)(2,1)} %bitcast.13.back_ref), custom_call_target="tpu_custom_call" | custom-call | flops 1 | bytes 1 | tf_op jit(solution)/shard_map/token_grads/pallas_call | solution.py:471
  (22 shorter events, 1.6 us)
Async XLA Ops:
  0.6 0.9 copy-start.2
  1.6 0.7 copy-start.3
  2.3 0.7 copy-start.5
  6.2 11.2 %copy-start = (bf16[64,1792]{1,0:T(8,128)(2,1)S(1)}, bf16[64,1792]{1,0:T(8,128)(2,1)}, u32[]{:S(2)}) copy-start(bf16[64,1792]{1,0:T(8,128)(2,1)} %cot_ref.1) | copy-start | bytes 688132
  6.2 11.2 %copy-start.4 = (s32[64,8]{0,1:T(8,128)S(1)}, s32[64,8]{0,1:T(8,128)}, u32[]{:S(2)}) copy-start(s32[64,8]{0,1:T(8,128)} %param.9) | copy-start | bytes 6148
  6.2 11.2 %copy-start.6 = (f32[64,8]{0,1:T(8,128)S(1)}, f32[64,8]{0,1:T(8,128)}, u32[]{:S(2)}) copy-start(f32[64,8]{0,1:T(8,128)} %param.10) | copy-start | bytes 6148
  6.2 47.2 %all-to-all-start = ((bf16[64,24,896]{2,1,0:T(8,128)(2,1)}), bf16[64,24,896]{2,1,0:T(8,128)(2,1)}, u32[]{:S(2)}, u32[]{:S(2)}) async-start(bf16[64,24,896]{2,1,0:T(8,128)(2,1)} %bitcast.34), calls=%async_computation | async-start | bytes 5505024 | tf_op jit(solution)/shard_map/all_to_all | solution.py:489
  55.4 8.5 %collective-permute-start.1 = (bf16[768,896]{1,0:T(8,128)(2,1)S(1)}, bf16[768,896]{1,0:T(8,128)(2,1)}, u32[]{:S(2)}, u32[]{:S(2)}) collective-permute-start(bf16[768,896]{1,0:T(8,128)(2,1)S(1)} %get-tuple-element.56), channel_id=1, source_target_pairs={{0,1},{1,0},{2,3},{3,2},{4,5},{5,4},{6,7},{7,6},{8,9},{9,8},{10,11... | collective-permute-start | bytes 4128776 | tf_op jit(solution)/shard_map/ppermute | solution.py:496
  56.6 7.2 %collective-permute-start = (bf16[768,896]{1,0:T(8,128)(2,1)S(1)}, bf16[768,896]{1,0:T(8,128)(2,1)}, u32[]{:S(2)}, u32[]{:S(2)}) collective-permute-start(bf16[768,896]{1,0:T(8,128)(2,1)S(1)} %get-tuple-element.57), channel_id=1, source_target_pairs={{0,1},{1,0},{2,3},{3,2},{4,5},{5,4},{6,7},{7,6},{8,9},{9,8},{10,11... | collective-permute-start | bytes 4128776 | tf_op jit(solution)/shard_map/ppermute | solution.py:496
  56.7 44.1 %all-to-all-start.1 = ((bf16[64,24,896]{2,1,0:T(8,128)(2,1)}), bf16[64,24,896]{2,1,0:T(8,128)(2,1)}, u32[]{:S(2)}, u32[]{:S(2)}) async-start(bf16[64,24,896]{2,1,0:T(8,128)(2,1)} %bitcast.4), calls=%async_computation.1 | async-start | bytes 5505024 | tf_op jit(solution)/shard_map/all_to_all | solution.py:489
  85.7 4.0 %collective-permute-start.2 = (bf16[768,896]{1,0:T(8,128)(2,1)}, bf16[768,896]{1,0:T(8,128)(2,1)S(1)}, u32[]{:S(2)}, u32[]{:S(2)}) collective-permute-start(bf16[768,896]{1,0:T(8,128)(2,1)} %get-tuple-element.33), channel_id=1, source_target_pairs={{0,1},{1,0},{2,3},{3,2},{4,5},{5,4},{6,7},{7,6},{8,9},{9,8},{10,11... | collective-permute-start | bytes 4128776 | tf_op jit(solution)/shard_map/ppermute | solution.py:496
  86.7 4.9 %collective-permute-start.3 = (bf16[768,896]{1,0:T(8,128)(2,1)}, bf16[768,896]{1,0:T(8,128)(2,1)S(1)}, u32[]{:S(2)}, u32[]{:S(2)}) collective-permute-start(bf16[768,896]{1,0:T(8,128)(2,1)} %get-tuple-element.34), channel_id=1, source_target_pairs={{0,1},{1,0},{2,3},{3,2},{4,5},{5,4},{6,7},{7,6},{8,9},{9,8},{10,11... | collective-permute-start | bytes 4128776 | tf_op jit(solution)/shard_map/ppermute | solution.py:496
  91.7 1.1 copy-start.7
  103.8 8.2 %collective-permute-start.5 = (bf16[768,896]{1,0:T(8,128)(2,1)}, bf16[768,896]{1,0:T(8,128)(2,1)}, u32[]{:S(2)}, u32[]{:S(2)}) collective-permute-start(bf16[768,896]{1,0:T(8,128)(2,1)} %get-tuple-element.54), channel_id=1, source_target_pairs={{0,1},{1,0},{2,3},{3,2},{4,5},{5,4},{6,7},{7,6},{8,9},{9,8},{10,11... | collective-permute-start | bytes 4128776 | tf_op jit(solution)/shard_map/ppermute | solution.py:496
  104.5 7.5 %collective-permute-start.4 = (bf16[768,896]{1,0:T(8,128)(2,1)S(1)}, bf16[768,896]{1,0:T(8,128)(2,1)}, u32[]{:S(2)}, u32[]{:S(2)}) collective-permute-start(bf16[768,896]{1,0:T(8,128)(2,1)S(1)} %get-tuple-element.55), channel_id=1, source_target_pairs={{0,1},{1,0},{2,3},{3,2},{4,5},{5,4},{6,7},{7,6},{8,9},{9,8},{10,11... | collective-permute-start | bytes 4128776 | tf_op jit(solution)/shard_map/ppermute | solution.py:496
  104.5 44.5 %all-to-all-start.2 = ((bf16[64,24,896]{2,1,0:T(8,128)(2,1)}), bf16[64,24,896]{2,1,0:T(8,128)(2,1)}, u32[]{:S(2)}, u32[]{:S(2)}) async-start(bf16[64,24,896]{2,1,0:T(8,128)(2,1)} %bitcast.32), calls=%async_computation.2 | async-start | bytes 5505024 | tf_op jit(solution)/shard_map/all_to_all | solution.py:489
  134.4 0.9 copy-start.1
  135.3 3.9 %collective-permute-start.6 = (bf16[768,896]{1,0:T(8,128)(2,1)}, bf16[768,896]{1,0:T(8,128)(2,1)S(1)}, u32[]{:S(2)}, u32[]{:S(2)}) collective-permute-start(bf16[768,896]{1,0:T(8,128)(2,1)} %get-tuple-element.40), channel_id=1, source_target_pairs={{0,1},{1,0},{2,3},{3,2},{4,5},{5,4},{6,7},{7,6},{8,9},{9,8},{10,11... | collective-permute-start | bytes 4128776 | tf_op jit(solution)/shard_map/ppermute | solution.py:496
  136.3 4.9 %collective-permute-start.7 = (bf16[768,896]{1,0:T(8,128)(2,1)}, bf16[768,896]{1,0:T(8,128)(2,1)S(1)}, u32[]{:S(2)}, u32[]{:S(2)}) collective-permute-start(bf16[768,896]{1,0:T(8,128)(2,1)} %get-tuple-element.41), channel_id=1, source_target_pairs={{0,1},{1,0},{2,3},{3,2},{4,5},{5,4},{6,7},{7,6},{8,9},{9,8},{10,11... | collective-permute-start | bytes 4128776 | tf_op jit(solution)/shard_map/ppermute | solution.py:496
  141.2 1.1 copy-start.8
  149.0 45.9 %all-to-all-start.3 = ((bf16[64,24,896]{2,1,0:T(8,128)(2,1)}), bf16[64,24,896]{2,1,0:T(8,128)(2,1)}, u32[]{:S(2)}, u32[]{:S(2)}) async-start(bf16[64,24,896]{2,1,0:T(8,128)(2,1)} %bitcast.33), calls=%async_computation.3 | async-start | bytes 5505024 | tf_op jit(solution)/shard_map/all_to_all | solution.py:489

commit v3 on v2

v3 whole, which is shorter than its diff:
```python
import functools
import jax
import jax.numpy as jnp
from jax import lax
from jax.experimental import pallas as pl
from jax.experimental.pallas import tpu as pltpu
from jax.sharding import PartitionSpec as P

BF16 = jnp.bfloat16
F32 = jnp.float32
SLOTS = 12
ROWS = 2 * SLOTS
GROUP = 16
TILE = GROUP * ROWS

NN = (((1,), (0,)), ((), ()))
NT = (((1,), (1,)), ((), ()))
TN = (((0,), (0,)), ((), ()))


def dot(a, b, dims=NN):
    return lax.dot_general(a, b, dims, preferred_element_type=F32)


def params(mebibytes):
    return pltpu.CompilerParams(
        vmem_limit_bytes=mebibytes * 1024 * 1024, dimension_semantics=("arbitrary",)
    )


def cost():
    return pl.CostEstimate(flops=1, bytes_accessed=1, transcendentals=0)


def spread(rows_of):
    return jnp.concatenate(
        [jnp.broadcast_to(rows_of[i : i + 1], (ROWS, rows_of.shape[1])) for i in range(GROUP)], axis=0
    )


def routing(route_ref, first):
    top, toks = route_ref.shape
    route = route_ref[...]
    ids = lax.broadcasted_iota(jnp.int32, (GROUP, toks), 0) + first
    hits = [jnp.broadcast_to(route[k : k + 1], (GROUP, toks)) == ids for k in range(top)]
    named = sum(h.astype(F32) for h in hits)
    return named, hits


def selection(named):
    toks = named.shape[1]
    before = (
        lax.broadcasted_iota(jnp.int32, (toks, toks), 0)
        < lax.broadcasted_iota(jnp.int32, (toks, toks), 1)
    ).astype(BF16)
    slot = dot(named.astype(BF16), before)
    code = jnp.where(named > 0, slot, -100.0)
    code = jnp.concatenate([code, code + float(SLOTS)], axis=1)
    place = lax.broadcasted_iota(jnp.int32, (ROWS, 2 * toks), 0).astype(F32)
    place = jnp.concatenate([place] * GROUP, axis=0)
    return spread(code) == place


def probs_of(hits, probs_ref):
    probs = probs_ref[...]
    chosen = sum(
        jnp.where(h, jnp.broadcast_to(probs[k : k + 1], h.shape), 0.0) for k, h in enumerate(hits)
    )
    return spread(jnp.concatenate([chosen, chosen], axis=1))


def stacked(x):
    half = x.shape[1] // 2
    return jnp.concatenate([x[:, :half], x[:, half:]], axis=0)


def send_kernel(scaled, route_ref, probs_ref, rows_ref, out_ref):
    named, hits = routing(route_ref, pl.program_id(0) * GROUP)
    sel = selection(named)
    picked = dot(sel.astype(F32).astype(BF16), stacked(rows_ref[...]))
    if scaled:
        weight = jnp.sum(jnp.where(sel, probs_of(hits, probs_ref), 0.0), axis=1, keepdims=True)
        picked = picked * weight
    out_ref[...] = picked.astype(BF16)


def send_rows(scaled, route_t, probs_t, rows, experts):
    toks, width = rows.shape
    top = route_t.shape[0]
    half = width // 2
    return pl.pallas_call(
        functools.partial(send_kernel, scaled),
        grid=(experts // GROUP,),
        in_specs=[
            pl.BlockSpec((top, toks), lambda i: (0, 0)),
            pl.BlockSpec((top, toks), lambda i: (0, 0)),
            pl.BlockSpec((toks, width), lambda i: (0, 0)),
        ],
        out_specs=pl.BlockSpec((TILE, half), lambda i: (i, 0)),
        out_shape=jax.ShapeDtypeStruct((experts * ROWS, half), BF16),
        compiler_params=params(60),
        cost_estimate=cost(),
        name="send_scaled" if scaled else "send_tokens",
    )(route_t, probs_t, rows)


SUB = 8


def ordering(back=False):
    n = SUB * ROWS
    row = lax.broadcasted_iota(jnp.int32, (n, n), int(back))
    col = lax.broadcasted_iota(jnp.int32, (n, n), 1 - int(back))
    upper = (row >= n // 2).astype(jnp.int32)
    within = row - upper * (n // 2)
    source = (within * 43) >> 9
    return (col == SLOTS * source + SLOTS * upper + within).astype(F32).astype(BF16)


def put_in_order(own_ref, other_ref, mine, step, held, out_ref):
    order = ordering()
    n = SUB * ROWS
    for which, ref in ((mine, own_ref), (1 - mine, other_ref)):
        for b in range(GROUP // SUB):
            both = dot(order, ref[b * n : (b + 1) * n, :]).astype(BF16)
            at = pl.multiple_of(step * (GROUP * SLOTS) + b * (n // 2), n // 2)
            for h in range(2):
                part = both[h * (n // 2) : (h + 1) * (n // 2)]
                held[2 * which + h, pl.ds(at, n // 2), :] = part
                out_ref[2 * which + h, b * (n // 2) : (b + 1) * (n // 2), :] = part


def weight_copies(gate_hbm, up_hbm, down_hbm, gate_w, up_w, down_w, sems):
    quarter = down_w.shape[2]
    downs = [
        pltpu.make_async_copy(
            down_hbm.at[:, q * quarter : (q + 1) * quarter], down_w.at[q], sems.at[2 + q]
        )
        for q in range(4)
    ]
    gates = pltpu.make_async_copy(gate_hbm, gate_w, sems.at[0])
    ups = pltpu.make_async_copy(up_hbm, up_w, sems.at[1])
    return [gates, ups], downs


def forward_kernel(
    steps, ff_steps, mine_ref, own_ref, other_ref, gate_hbm, up_hbm, down_hbm,
    gate_ref, up_ref, hidden_ref, rows_ref, far0, far1, near_ref,
    held, hidden_all, gate_w, up_w, down_w, sems,
):
    i = pl.program_id(0)
    mine = mine_ref[0]
    quarter = own_ref.shape[1]
    ins, downs = weight_copies(gate_hbm, up_hbm, down_hbm, gate_w, up_w, down_w, sems)

    @pl.when(i == 0)
    def _():
        for copy in ins + downs:
            copy.start()

    @pl.when(i < steps)
    def _():
        put_in_order(own_ref, other_ref, mine, i, held, rows_ref)

    for f in range(ff_steps):
        @pl.when(i == steps + f)
        def _():
            if f == 0:
                for copy in ins:
                    copy.wait()
            wide = gate_ref.shape[1]
            at = slice(f * wide, (f + 1) * wide)
            gate = sum(dot(held[q], gate_w[q * quarter : (q + 1) * quarter, at]) for q in range(4))
            up = sum(dot(held[q], up_w[q * quarter : (q + 1) * quarter, at]) for q in range(4))
            gate_ref[...] = gate
            up_ref[...] = up
            hidden = (gate * jax.nn.sigmoid(gate) * up).astype(BF16)
            hidden_ref[...] = hidden
            hidden_all[:, at] = hidden

    for h, far_ref in enumerate((far0, far1)):
        @pl.when(i == steps + ff_steps + h)
        def _():
            if h == 0:
                for copy in downs:
                    copy.wait()
            far_ref[...] = dot(hidden_all[...], down_w[2 * (1 - mine) + h]).astype(BF16)

    for h in range(2):
        @pl.when(i == steps + ff_steps + 2 + h)
        def _():
            near_ref[...] = dot(hidden_all[...], down_w[2 * mine + h]).astype(BF16)


def expert_specs(raw, quarter, ff, model):
    steps, ff_steps, rows = raw // TILE, 2, raw // 2
    wide = ff // ff_steps
    last = steps + ff_steps
    source = pl.BlockSpec((TILE, quarter), lambda i, m: (jnp.minimum(i, steps - 1), 0))
    ffs = pl.BlockSpec((rows, wide), lambda i, m: (0, jnp.clip(i - steps, 0, ff_steps - 1)))
    ordered = pl.BlockSpec(
        (4, GROUP * SLOTS, quarter), lambda i, m: (0, jnp.minimum(i, steps - 1), 0)
    )
    far = pl.BlockSpec((rows, quarter), lambda i, m: (0, 0))
    near = pl.BlockSpec((rows, quarter), lambda i, m: (0, jnp.clip(i - last - 2, 0, 1)))
    held = [
        pltpu.VMEM((model, ff), BF16),
        pltpu.VMEM((model, ff), BF16),
        pltpu.VMEM((4, ff, quarter), BF16),
        pltpu.SemaphoreType.DMA((6,)),
    ]
    return steps, ff_steps, rows, source, ffs, ordered, far, near, held


def forward(mine, own, other, gate_w, up_w, down_w):
    raw, quarter = own.shape
    model, ff = gate_w.shape
    steps, ff_steps, rows, source, ffs, ordered, far, near, held = expert_specs(
        raw, quarter, ff, model
    )
    hbm = pl.BlockSpec(memory_space=pl.ANY)
    return pl.pallas_call(
        functools.partial(forward_kernel, steps, ff_steps),
        grid_spec=pltpu.PrefetchScalarGridSpec(
            num_scalar_prefetch=1,
            grid=(steps + ff_steps + 4,),
            in_specs=[source, source, hbm, hbm, hbm],
            out_specs=[ffs, ffs, ffs, ordered, far, far, near],
            scratch_shapes=[
                pltpu.VMEM((4, rows, quarter), BF16), pltpu.VMEM((rows, ff), BF16), *held
            ],
        ),
        out_shape=[
            jax.ShapeDtypeStruct((rows, ff), F32),
            jax.ShapeDtypeStruct((rows, ff), F32),
            jax.ShapeDtypeStruct((rows, ff), BF16),
            jax.ShapeDtypeStruct((4, rows, quarter), BF16),
            jax.ShapeDtypeStruct((rows, quarter), BF16),
            jax.ShapeDtypeStruct((rows, quarter), BF16),
            jax.ShapeDtypeStruct((rows, 2 * quarter), BF16),
        ],
        compiler_params=params(60),
        cost_estimate=cost(),
        name="expert_forward",
    )(mine, own, other, gate_w, up_w, down_w)


def backward_kernel(
    steps, ff_steps, mine_ref, own_ref, other_ref, gate_hbm, up_hbm, down_hbm, gate_ref, up_ref,
    gate_grad_ref, up_grad_ref, rows_ref, far0, far1, near_ref,
    held, gate_grads, up_grads, gate_w, up_w, down_w, sems,
):
    i = pl.program_id(0)
    mine = mine_ref[0]
    quarter = own_ref.shape[1]
    ins, downs = weight_copies(gate_hbm, up_hbm, down_hbm, gate_w, up_w, down_w, sems)

    @pl.when(i == 0)
    def _():
        for copy in downs + ins:
            copy.start()

    @pl.when(i < steps)
    def _():
        put_in_order(own_ref, other_ref, mine, i, held, rows_ref)

    for f in range(ff_steps):
        @pl.when(i == steps + f)
        def _():
            if f == 0:
                for copy in downs:
                    copy.wait()
            wide = gate_ref.shape[1]
            at = slice(f * wide, (f + 1) * wide)
            hidden_grad = sum(dot(held[q], down_w[q, at, :], NT) for q in range(4))
            gate, up = gate_ref[...], up_ref[...]
            logistic = jax.nn.sigmoid(gate)
            gate_grad = (hidden_grad * up * logistic * (1.0 + gate * (1.0 - logistic))).astype(BF16)
            up_grad = (hidden_grad * (gate * logistic)).astype(BF16)
            gate_grad_ref[...] = gate_grad
            up_grad_ref[...] = up_grad
            gate_grads[:, at] = gate_grad
            up_grads[:, at] = up_grad

    def input_grads(q):
        at = pl.ds(pl.multiple_of(q * quarter, quarter), quarter)
        return (
            dot(gate_grads[...], gate_w[at, :], NT) + dot(up_grads[...], up_w[at, :], NT)
        ).astype(BF16)

    for h, far_ref in enumerate((far0, far1)):
        @pl.when(i == steps + ff_steps + h)
        def _():
            if h == 0:
                for copy in ins:
                    copy.wait()
            far_ref[...] = input_grads(2 * (1 - mine) + h)

    for h in range(2):
        @pl.when(i == steps + ff_steps + 2 + h)
        def _():
            near_ref[...] = input_grads(2 * mine + h)


def backward(mine, own, other, gate_w, up_w, down_w, gate_pre, up_pre):
    raw, quarter = own.shape
    model, ff = gate_w.shape
    steps, ff_steps, rows, source, ffs, ordered, far, near, held = expert_specs(
        raw, quarter, ff, model
    )
    hbm = pl.BlockSpec(memory_space=pl.ANY)
    return pl.pallas_call(
        functools.partial(backward_kernel, steps, ff_steps),
        grid_spec=pltpu.PrefetchScalarGridSpec(
            num_scalar_prefetch=1,
            grid=(steps + ff_steps + 4,),
            in_specs=[source, source, hbm, hbm, hbm, ffs, ffs],
            out_specs=[ffs, ffs, ordered, far, far, near],
            scratch_shapes=[
                pltpu.VMEM((4, rows, quarter), BF16),
                pltpu.VMEM((rows, ff), BF16),
                pltpu.VMEM((rows, ff), BF16),
                *held,
            ],
        ),
        out_shape=[
            jax.ShapeDtypeStruct((rows, ff), BF16),
            jax.ShapeDtypeStruct((rows, ff), BF16),
            jax.ShapeDtypeStruct((4, rows, quarter), BF16),
            jax.ShapeDtypeStruct((rows, quarter), BF16),
            jax.ShapeDtypeStruct((rows, quarter), BF16),
            jax.ShapeDtypeStruct((rows, 2 * quarter), BF16),
        ],
        compiler_params=params(60),
        cost_estimate=cost(),
        name="expert_backward",
    )(mine, own, other, gate_w, up_w, down_w, gate_pre, up_pre)


def pack_kernel(near_ref, far0, far1, out_ref):
    order = ordering(back=True)
    n = SUB * ROWS
    quarter = out_ref.shape[1]
    for b in range(GROUP // SUB):
        at = slice(b * (n // 2), (b + 1) * (n // 2))
        both = jnp.concatenate(
            [
                (
                    near_ref[at, h * quarter : (h + 1) * quarter].astype(F32)
                    + far[at, :].astype(F32)
                ).astype(BF16)
                for h, far in enumerate((far0, far1))
            ],
            axis=0,
        )
        out_ref[b * n : (b + 1) * n, :] = dot(order, both).astype(BF16)


def pack(near, fars):
    rows, width = near.shape
    step_rows = GROUP * SLOTS
    return pl.pallas_call(
        pack_kernel,
        grid=(rows // step_rows,),
        in_specs=[
            pl.BlockSpec((step_rows, width), lambda i: (i, 0)),
            pl.BlockSpec((step_rows, width // 2), lambda i: (i, 0)),
            pl.BlockSpec((step_rows, width // 2), lambda i: (i, 0)),
        ],
        out_specs=pl.BlockSpec((TILE, width // 2), lambda i: (i, 0)),
        out_shape=jax.ShapeDtypeStruct((2 * rows, width // 2), BF16),
        compiler_params=params(48),
        cost_estimate=cost(),
        name="pack",
    )(near, *fars)


def weights_kernel(rows_ref, scaled_ref, hidden_ref, gate_grad_ref, up_grad_ref, gate_w, up_w, down_w):
    rows = rows_ref[0]
    gate_w[...] = dot(rows, gate_grad_ref[...], TN).astype(BF16)
    up_w[...] = dot(rows, up_grad_ref[...], TN).astype(BF16)
    down_w[...] = dot(hidden_ref[...], scaled_ref[0], TN).astype(BF16)


def weight_grads(token_rows, scaled_rows, hidden, gate_grad, up_grad):
    quarters, rows, quarter = token_rows.shape
    ff = hidden.shape[1]
    whole = pl.BlockSpec((rows, ff), lambda i: (0, 0))
    part = pl.BlockSpec((1, rows, quarter), lambda i: (i, 0, 0))
    return pl.pallas_call(
        weights_kernel,
        grid=(quarters,),
        in_specs=[part, part, whole, whole, whole],
        out_specs=[
            pl.BlockSpec((quarter, ff), lambda i: (i, 0)),
            pl.BlockSpec((quarter, ff), lambda i: (i, 0)),
            pl.BlockSpec((ff, quarter), lambda i: (0, i)),
        ],
        out_shape=[
            jax.ShapeDtypeStruct((quarters * quarter, ff), BF16),
            jax.ShapeDtypeStruct((quarters * quarter, ff), BF16),
            jax.ShapeDtypeStruct((ff, quarters * quarter), BF16),
        ],
        compiler_params=params(60),
        cost_estimate=cost(),
        name="weight_grads",
    )(token_rows, scaled_rows, hidden, gate_grad, up_grad)


def outputs_kernel(route_ref, probs_ref, cot_ref, back_ref, out_ref, grad_ref, sel_ref, total):
    i = pl.program_id(0)

    @pl.when(i == 0)
    def _():
        total[...] = jnp.zeros_like(total)
        grad_ref[...] = jnp.zeros_like(grad_ref)

    toks = cot_ref.shape[0]
    half = back_ref.shape[1]
    named, hits = routing(route_ref, i * GROUP)
    sel = selection(named)
    sel_ref[...] = sel.astype(F32).T.astype(BF16)
    weight = jnp.where(sel, probs_of(hits, probs_ref), 0.0)
    high = weight.astype(BF16)
    low = (weight - high.astype(F32)).astype(BF16)
    back = back_ref[...]
    total[...] += dot(high, back, TN) + dot(low, back, TN)
    products = jnp.where(sel, dot(back, stacked(cot_ref[...]), NT), 0.0)
    sums = jnp.concatenate(
        [
            jnp.sum(products[e * ROWS : (e + 1) * ROWS], axis=0, keepdims=True)
            for e in range(GROUP)
        ],
        axis=0,
    )
    sums = sums[:, :toks] + sums[:, toks:]
    grad_ref[...] += jnp.concatenate(
        [jnp.sum(jnp.where(h, sums, 0.0), axis=0, keepdims=True) for h in hits], axis=0
    )

    @pl.when(i == pl.num_programs(0) - 1)
    def _():
        out_ref[:, :half] = total[:toks].astype(BF16)
        out_ref[:, half:] = total[toks:].astype(BF16)


def token_outputs(route_t, probs_t, cot, back):
    toks, width = cot.shape
    top = route_t.shape[0]
    steps = back.shape[0] // TILE
    small = pl.BlockSpec((top, toks), lambda i: (0, 0))
    wide = pl.BlockSpec((toks, width), lambda i: (0, 0))
    return pl.pallas_call(
        outputs_kernel,
        grid=(steps,),
        in_specs=[small, small, wide, pl.BlockSpec((TILE, width // 2), lambda i: (i, 0))],
        out_specs=[wide, small, pl.BlockSpec((2 * toks, TILE), lambda i: (0, i))],
        out_shape=[
            jax.ShapeDtypeStruct((toks, width), BF16),
            jax.ShapeDtypeStruct((top, toks), F32),
            jax.ShapeDtypeStruct((2 * toks, back.shape[0]), BF16),
        ],
        scratch_shapes=[pltpu.VMEM((2 * toks, width // 2), F32)],
        compiler_params=params(60),
        cost_estimate=cost(),
        name="token_outputs",
    )(route_t, probs_t, cot, back)


def inputs_kernel(sel_ref, back_ref, out_ref, total):
    i = pl.program_id(0)
    toks, width = out_ref.shape
    half = width // 2
    part = dot(sel_ref[...], back_ref[...])

    @pl.when(i == 0)
    def _():
        total[...] = part

    @pl.when(i > 0)
    def _():
        total[...] += part

    @pl.when(i == pl.num_programs(0) - 1)
    def _():
        out_ref[:, :half] = total[:toks].astype(BF16)
        out_ref[:, half:] = total[toks:].astype(BF16)


def token_grads(select, back):
    raw, half = back.shape
    toks = select.shape[0] // 2
    return pl.pallas_call(
        inputs_kernel,
        grid=(2,),
        in_specs=[
            pl.BlockSpec((2 * toks, raw // 2), lambda i: (0, i)),
            pl.BlockSpec((raw // 2, half), lambda i: (i, 0)),
        ],
        out_specs=pl.BlockSpec((toks, 2 * half), lambda i: (0, 0)),
        out_shape=jax.ShapeDtypeStruct((toks, 2 * half), BF16),
        scratch_shapes=[pltpu.VMEM((2 * toks, half), F32)],
        compiler_params=params(60),
        cost_estimate=cost(),
        name="token_grads",
    )(select, back)


def exchange(x):
    experts = lax.axis_size("expert")
    y = lax.all_to_all(
        x.reshape(experts, ROWS, -1), "expert", split_axis=0, concat_axis=0, tiled=True
    )
    return y.reshape(x.shape)


def swap(x):
    return lax.ppermute(x, "mp", [(0, 1), (1, 0)])


def body(tokens, cotangent, route_ids, gate_probs, w_gate, w_up, w_down):
    experts = lax.axis_size("expert")
    mine = lax.axis_index("mp").astype(jnp.int32).reshape(1)
    route_t, probs_t = route_ids.T, gate_probs.T
    gate_w, up_w, down_w = w_gate[0], w_up[0], w_down[0]

    send_tokens = send_rows(False, route_t, probs_t, tokens, experts)
    send_scaled = send_rows(True, route_t, probs_t, cotangent, experts)
    got_tokens, send_scaled = lax.optimization_barrier((exchange(send_tokens), send_scaled))
    got_scaled = exchange(send_scaled)

    gate_pre, up_pre, hidden, token_rows, far0, far1, out_near = forward(
        mine, got_tokens, swap(got_tokens), gate_w, up_w, down_w
    )
    send_out = pack(out_near, [swap(far0), swap(far1)])
    got_scaled, send_out = lax.optimization_barrier((got_scaled, send_out))
    back_out = exchange(send_out)

    gate_grad, up_grad, scaled_rows, far0, far1, in_near = backward(
        mine, got_scaled, swap(got_scaled), gate_w, up_w, down_w, gate_pre, up_pre
    )
    send_in = pack(in_near, [swap(far0), swap(far1)])
    back_out, send_in = lax.optimization_barrier((back_out, send_in))
    back_in = exchange(send_in)

    grad_w_gate, grad_w_up, grad_w_down = weight_grads(
        token_rows, scaled_rows, hidden, gate_grad, up_grad
    )
    layer_out, grad_part, select = token_outputs(route_t, probs_t, cotangent, back_out)
    grad_probs = lax.psum(grad_part, "mp").T
    grad_tokens = token_grads(select, back_in)
    return (
        layer_out, grad_tokens, grad_probs, grad_w_gate[None], grad_w_up[None], grad_w_down[None],
    )


def solution(mesh):
    return jax.shard_map(
        body,
        mesh=mesh,
        in_specs=(
            P("expert", "mp"),
            P("expert", "mp"),
            P("expert", None),
            P("expert", None),
            P("expert", None, "mp"),
            P("expert", None, "mp"),
            P("expert", "mp", None),
        ),
        out_specs=(
            P("expert", "mp"),
            P("expert", "mp"),
            P("expert", None),
            P("expert", None, "mp"),
            P("expert", None, "mp"),
            P("expert", "mp", None),
        ),
        check_vma=False,
    )
```

time: 201 us -> 192 us (0.955)
  local copies, waits for them, and re-layouts: 10.4 us -> 1.92 us
    slice x2 -> x0, local copies, waits for them, and re-layouts: 5.02 us -> none  [halves(): return (x[:half], x[half:])]
    unnamed x18 -> x4, local copies, waits for them, and re-layouts: 5.35 us -> 1.92 us
    all_to_all x4, starting transfers between devices: 34.6 us -> 32.2 us  [exchange(): lax.all_to_all(x.reshape(experts, ROWS, -1), 'expert', split_axis=0, conc...]
    ppermute x8 -> x6, starting transfers between devices: 4.14 us -> 5.91 us  [swap(): return lax.ppermute(x, 'mp', [(0, 1), (1, 0)])]
    ppermute x8 -> x6, waiting for transfers between devices: 9.78 us -> 9.69 us  [swap(): return lax.ppermute(x, 'mp', [(0, 1), (1, 0)])]
  transfers between devices with their start and end apart: 12 -> 10, of which waited for: 8 -> 8; matrix products, arithmetic and copies ran while one was open for 0% -> 0% of each run, Pallas kernels for 39% -> 42%
where the time goes in v3:
time: 192 us; the launch traced here: 191 us
  Pallas kernels  87.2 us (45%)
  waiting for transfers between devices  59.4 us (31%)
  starting transfers between devices  38.1 us (20%)
  blocking collectives  3.75 us (2%)
  local copies, waits for them, and re-layouts  1.92 us (1%)
    all_to_all x4, waiting for transfers between devices, exchange(): lax.all_to_all(x.reshape(experts, ROWS, -1), 'expert', split_axis=0, conc...  49.7 us
    all_to_all x4, starting transfers between devices, exchange(): lax.all_to_all(x.reshape(experts, ROWS, -1), 'expert', split_axis=0, conc...  32.2 us
    pallas_call x1, Pallas kernels, backward(): pl.pallas_call(functools.partial(backward_kernel, steps, ff_steps), grid_...  23.8 us
    pallas_call x1, Pallas kernels, forward(): pl.pallas_call(functools.partial(forward_kernel, steps, ff_steps), grid_s...  23 us
    pallas_call x1, Pallas kernels, weight_grads(): pl.pallas_call(weights_kernel, grid=(quarters,), in_specs=[part, part, wh...  13.2 us
    ppermute x6, waiting for transfers between devices, swap(): return lax.ppermute(x, 'mp', [(0, 1), (1, 0)])  9.69 us
    pallas_call x2, Pallas kernels, pack(): pl.pallas_call(pack_kernel, grid=(rows // step_rows,), in_specs=[pl.Block...  9.53 us
    pallas_call x2, Pallas kernels, send_rows(): pl.pallas_call(functools.partial(send_kernel, scaled), grid=(experts // G...  8.52 us
  transfers between devices with their start and end apart: 10, of which 8 were waited for; matrix products, arithmetic and copies ran while one was open for 0% of the time, Pallas kernels for 42%

profile of v3, /device:TPU:7, one launch (start us, length us, event | category | flops | bytes accessed | tf_op | source)
XLA Modules:
  0.0 191.1 jit_solution(1591537258757093936)
XLA Ops:
  0.6 4.3 %send_tokens.1 = bf16[1536,896]{1,0:T(8,128)(2,1)} custom-call(s32[8,64]{1,0:T(8,128)} %bitcast.29, f32[8,64]{1,0:T(8,128)} %bitcast.32, bf16[64,1792]{1,0:T(8,128)(2,1)} %rows_ref.2), custom_call_target="tpu_custom_call" | custom-call | flops 1 | bytes 1 | tf_op jit(solution)/shard_map/send_tokens/pallas_call | solution.py:91
  4.9 10.9 %all-to-all-start = ((bf16[64,24,896]{2,1,0:T(8,128)(2,1)}), bf16[64,24,896]{2,1,0:T(8,128)(2,1)S(1)}, u32[]{:S(2)}, u32[]{:S(2)}) async-start(bf16[64,24,896]{2,1,0:T(8,128)(2,1)} %bitcast.28), calls=%async_computation | async-start | bytes 5505024 | tf_op jit(solution)/shard_map/all_to_all | solution.py:511
  15.8 4.3 %send_scaled.1 = bf16[1536,896]{1,0:T(8,128)(2,1)} custom-call(s32[8,64]{1,0:T(8,128)} %bitcast.30, f32[8,64]{1,0:T(8,128)} %bitcast.33, bf16[64,1792]{1,0:T(8,128)(2,1)} %cot_ref.1), custom_call_target="tpu_custom_call" | custom-call | flops 1 | bytes 1 | tf_op jit(solution)/shard_map/send_scaled/pallas_call | solution.py:91
  20.0 31.8 %all-to-all-done = bf16[64,24,896]{2,1,0:T(8,128)(2,1)S(1)} async-done(((bf16[64,24,896]{2,1,0:T(8,128)(2,1)}), bf16[64,24,896]{2,1,0:T(8,128)(2,1)S(1)}, u32[]{:S(2)}, u32[]{:S(2)}) %all-to-all-start) | async-done | bytes 2752544 | tf_op jit(solution)/shard_map/all_to_all | solution.py:511
  51.9 1.2 collective-permute-start
  53.0 0.4 copy-done
  53.4 6.8 %all-to-all-start.1 = ((bf16[64,24,896]{2,1,0:T(8,128)(2,1)}), bf16[64,24,896]{2,1,0:T(8,128)(2,1)}, u32[]{:S(2)}, u32[]{:S(2)}) async-start(bf16[64,24,896]{2,1,0:T(8,128)(2,1)} %bitcast.27), calls=%async_computation.1 | async-start | bytes 5505024 | tf_op jit(solution)/shard_map/all_to_all | solution.py:511
  60.2 0.0 collective-permute-done.other_ref
  60.2 23.0 %expert_forward.1 = (f32[768,512]{1,0:T(8,128)}, f32[768,512]{1,0:T(8,128)}, bf16[768,512]{1,0:T(8,128)(2,1)}, bf16[4,768,896]{2,1,0:T(8,128)(2,1)}, bf16[768,89...) custom-call(s32[1]{0:T(128)} %bitcast.6.mine_ref, bf16[1536,896]{1,0:T(8,128)(2,1)} %bitcast.25, ...), custom_call_target="tpu_custom_call" | custom-call | flops 1 | bytes 1 | tf_op jit(solution)/shard_map/expert_forward/pallas_call | solution.py:222
  83.1 2.2 %collective-permute-start.1 = (bf16[768,896]{1,0:T(8,128)(2,1)}, bf16[768,896]{1,0:T(8,128)(2,1)S(1)}, u32[]{:S(2)}, u32[]{:S(2)}) collective-permute-start(bf16[768,896]{1,0:T(8,128)(2,1)} %get-tuple-element.34), channel_id=1, source_target_pairs={{0,1},{1,0},{2,3},{3,2},{4,5},{5,4},{6,7},{7,6},{8,9},{9,8},{10,11... | collective-permute-start | bytes 4128776 | tf_op jit(solution)/shard_map/ppermute | solution.py:518
  85.3 0.1 collective-permute-start.2
  85.4 2.9 %collective-permute-done.1.far0 = bf16[768,896]{1,0:T(8,128)(2,1)S(1)} collective-permute-done((bf16[768,896]{1,0:T(8,128)(2,1)}, bf16[768,896]{1,0:T(8,128)(2,1)S(1)}, u32[]{:S(2)}, u32[]{:S(2)}) %collective-permute-start.1) | collective-permute-done | bytes 1376288 | tf_op jit(solution)/shard_map/ppermute | solution.py:518
  88.3 2.0 %collective-permute-done.2.far1 = bf16[768,896]{1,0:T(8,128)(2,1)S(1)} collective-permute-done((bf16[768,896]{1,0:T(8,128)(2,1)}, bf16[768,896]{1,0:T(8,128)(2,1)S(1)}, u32[]{:S(2)}, u32[]{:S(2)}) %collective-permute-start.2) | collective-permute-done | bytes 1376288 | tf_op jit(solution)/shard_map/ppermute | solution.py:518
  90.3 4.8 %pack.2 = bf16[1536,896]{1,0:T(8,128)(2,1)} custom-call(bf16[768,1792]{1,0:T(8,128)(2,1)} %get-tuple-element.33.near_ref, bf16[768,896]{1,0:T(8,128)(2,1)S(1)} %collective-permute-done.1.far0, bf16[768,896]{1,0:T(8,128)(2,1)S(1)} %collective-permute-done.2.far1), custom_call_target="tpu_custom_call" | custom-call | flops 1 | bytes 1 | tf_op jit(solution)/shard_map/pack/pallas_call | solution.py:362
  95.0 0.7 all-to-all-done.1
  95.7 1.6 collective-permute-start.3
  97.3 7.9 %all-to-all-start.2 = ((bf16[64,24,896]{2,1,0:T(8,128)(2,1)}), bf16[64,24,896]{2,1,0:T(8,128)(2,1)S(1)}, u32[]{:S(2)}, u32[]{:S(2)}) async-start(bf16[64,24,896]{2,1,0:T(8,128)(2,1)} %bitcast.10), calls=%async_computation.2 | async-start | bytes 5505024 | tf_op jit(solution)/shard_map/all_to_all | solution.py:511
  105.2 0.0 collective-permute-done.3.other_ref
  105.2 23.8 %expert_backward.1 = (bf16[768,512]{1,0:T(8,128)(2,1)}, bf16[768,512]{1,0:T(8,128)(2,1)}, bf16[4,768,896]{2,1,0:T(8,128)(2,1)}, bf16[768,896]{1,0:T(8,128)(2,1)}...) custom-call(s32[1]{0:T(128)} %bitcast.6.mine_ref, bf16[1536,896]{1,0:T(8,128)(2,1)} %bitcast.5.own_ref, ...), custom_call_target="tpu_custom_call" | custom-call | flops 1 | bytes 1 | tf_op jit(solution)/shard_map/expert_backward/pallas_call | solution.py:312
  129.0 0.8 collective-permute-start.4
  129.8 0.1 collective-permute-start.5
  129.9 2.9 %collective-permute-done.4.far0 = bf16[768,896]{1,0:T(8,128)(2,1)S(1)} collective-permute-done((bf16[768,896]{1,0:T(8,128)(2,1)}, bf16[768,896]{1,0:T(8,128)(2,1)S(1)}, u32[]{:S(2)}, u32[]{:S(2)}) %collective-permute-start.4) | collective-permute-done | bytes 1376288 | tf_op jit(solution)/shard_map/ppermute | solution.py:518
  132.7 2.0 %collective-permute-done.5.far1 = bf16[768,896]{1,0:T(8,128)(2,1)S(1)} collective-permute-done((bf16[768,896]{1,0:T(8,128)(2,1)}, bf16[768,896]{1,0:T(8,128)(2,1)S(1)}, u32[]{:S(2)}, u32[]{:S(2)}) %collective-permute-start.5) | collective-permute-done | bytes 1376288 | tf_op jit(solution)/shard_map/ppermute | solution.py:518
  134.7 4.8 %pack.3 = bf16[1536,896]{1,0:T(8,128)(2,1)} custom-call(bf16[768,1792]{1,0:T(8,128)(2,1)} %get-tuple-element.40.near_ref, bf16[768,896]{1,0:T(8,128)(2,1)S(1)} %collective-permute-done.4.far0, bf16[768,896]{1,0:T(8,128)(2,1)S(1)} %collective-permute-done.5.far1), custom_call_target="tpu_custom_call" | custom-call | flops 1 | bytes 1 | tf_op jit(solution)/shard_map/pack/pallas_call | solution.py:362
  139.5 3.3 %all-to-all-done.2 = bf16[64,24,896]{2,1,0:T(8,128)(2,1)S(1)} async-done(((bf16[64,24,896]{2,1,0:T(8,128)(2,1)}), bf16[64,24,896]{2,1,0:T(8,128)(2,1)S(1)}, u32[]{:S(2)}, u32[]{:S(2)}) %all-to-all-start.2) | async-done | bytes 2752544 | tf_op jit(solution)/shard_map/all_to_all | solution.py:511
  142.8 1.5 copy-done.1
  144.3 6.6 %all-to-all-start.3 = ((bf16[64,24,896]{2,1,0:T(8,128)(2,1)}), bf16[64,24,896]{2,1,0:T(8,128)(2,1)}, u32[]{:S(2)}, u32[]{:S(2)}) async-start(bf16[64,24,896]{2,1,0:T(8,128)(2,1)} %bitcast.12), calls=%async_computation.3 | async-start | bytes 5505024 | tf_op jit(solution)/shard_map/all_to_all | solution.py:511
  151.0 13.2 %weight_grads.1 = (bf16[3584,512]{1,0:T(8,128)(2,1)}, bf16[3584,512]{1,0:T(8,128)(2,1)}, bf16[512,3584]{1,0:T(8,128)(2,1)}) custom-call(bf16[4,768,896]{2,1,0:T(8,128)(2,1)} %get-tuple-element.48.rows_ref, bf16[4,768,896]{2,1,0:T(8,128)(2,1)} %get-tuple-element.49.scaled_ref, bf16[768,512]{1,0:T(8,128)(2,1)} %get-tuple-element.50.hidden_ref, ...), custom_call_target="tpu_custom_call" | custom-call | flops 1 | bytes 1 | tf_op jit(solution)/shard_map/weight_grads/pallas_call | solution.py:390
  164.2 6.2 %token_outputs.1 = (bf16[64,1792]{1,0:T(8,128)(2,1)}, f32[8,64]{1,0:T(8,128)}, bf16[128,1536]{1,0:T(8,128)(2,1)}) custom-call(s32[8,64]{1,0:T(8,128)} %bitcast.31, f32[8,64]{1,0:T(8,128)} %bitcast.34, bf16[64,1792]{1,0:T(8,128)(2,1)} %cot_ref.1, bf16[1536,896]{1,0:T(8,128)(2,1)} %bitcast.26), custom_call_target="tpu_custom_call" | custom-call | flops 1 | bytes 1 | tf_op jit(solution)/shard_map/token_outputs/pallas_call | solution.py:453
  170.4 3.8 %psum.7 = f32[64,8]{0,1:T(8,128)} all-reduce(f32[64,8]{0,1:T(8,128)} %bitcast.35), channel_id=1, replica_groups=mesh['expert'=64,'mp'=2] {'mp'}, use_global_device_ids=true, to_apply=%region_0.0 | all-reduce | flops 512 | bytes 4096 | tf_op jit(solution)/shard_map/psum | solution.py:550
  174.1 13.9 %all-to-all-done.3 = bf16[64,24,896]{2,1,0:T(8,128)(2,1)} async-done(((bf16[64,24,896]{2,1,0:T(8,128)(2,1)}), bf16[64,24,896]{2,1,0:T(8,128)(2,1)}, u32[]{:S(2)}, u32[]{:S(2)}) %all-to-all-start.3) | async-done | bytes 2752544 | tf_op jit(solution)/shard_map/all_to_all | solution.py:511
  188.0 3.1 %token_grads.1 = bf16[64,1792]{1,0:T(8,128)(2,1)} custom-call(bf16[128,1536]{1,0:T(8,128)(2,1)} %get-tuple-element.45.sel_ref, bf16[1536,896]{1,0:T(8,128)(2,1)} %bitcast.13.back_ref), custom_call_target="tpu_custom_call" | custom-call | flops 1 | bytes 1 | tf_op jit(solution)/shard_map/token_grads/pallas_call | solution.py:493
  (2 shorter events, 0.0 us)
Async XLA Ops:
  4.9 47.0 %all-to-all-start = ((bf16[64,24,896]{2,1,0:T(8,128)(2,1)}), bf16[64,24,896]{2,1,0:T(8,128)(2,1)S(1)}, u32[]{:S(2)}, u32[]{:S(2)}) async-start(bf16[64,24,896]{2,1,0:T(8,128)(2,1)} %bitcast.28), calls=%async_computation | async-start | bytes 5505024 | tf_op jit(solution)/shard_map/all_to_all | solution.py:511
  51.9 1.5 copy-start
  51.9 8.3 %collective-permute-start = (bf16[1536,896]{1,0:T(8,128)(2,1)S(1)}, bf16[1536,896]{1,0:T(8,128)(2,1)}, u32[]{:S(2)}, u32[]{:S(2)}) collective-permute-start(bf16[1536,896]{1,0:T(8,128)(2,1)S(1)} %bitcast.24), channel_id=1, source_target_pairs={{0,1},{1,0},{2,3},{3,2},{4,5},{5,4},{6,7},{7,6},{8,9},{9,8},{10,11... | collective-permute-start | bytes 8257544 | tf_op jit(solution)/shard_map/ppermute | solution.py:518
  53.4 42.3 %all-to-all-start.1 = ((bf16[64,24,896]{2,1,0:T(8,128)(2,1)}), bf16[64,24,896]{2,1,0:T(8,128)(2,1)}, u32[]{:S(2)}, u32[]{:S(2)}) async-start(bf16[64,24,896]{2,1,0:T(8,128)(2,1)} %bitcast.27), calls=%async_computation.1 | async-start | bytes 5505024 | tf_op jit(solution)/shard_map/all_to_all | solution.py:511
  83.1 5.1 %collective-permute-start.1 = (bf16[768,896]{1,0:T(8,128)(2,1)}, bf16[768,896]{1,0:T(8,128)(2,1)S(1)}, u32[]{:S(2)}, u32[]{:S(2)}) collective-permute-start(bf16[768,896]{1,0:T(8,128)(2,1)} %get-tuple-element.34), channel_id=1, source_target_pairs={{0,1},{1,0},{2,3},{3,2},{4,5},{5,4},{6,7},{7,6},{8,9},{9,8},{10,11... | collective-permute-start | bytes 4128776 | tf_op jit(solution)/shard_map/ppermute | solution.py:518
  85.3 4.9 %collective-permute-start.2 = (bf16[768,896]{1,0:T(8,128)(2,1)}, bf16[768,896]{1,0:T(8,128)(2,1)S(1)}, u32[]{:S(2)}, u32[]{:S(2)}) collective-permute-start(bf16[768,896]{1,0:T(8,128)(2,1)} %get-tuple-element.35), channel_id=1, source_target_pairs={{0,1},{1,0},{2,3},{3,2},{4,5},{5,4},{6,7},{7,6},{8,9},{9,8},{10,11... | collective-permute-start | bytes 4128776 | tf_op jit(solution)/shard_map/ppermute | solution.py:518
  95.7 9.5 %collective-permute-start.3 = (bf16[1536,896]{1,0:T(8,128)(2,1)}, bf16[1536,896]{1,0:T(8,128)(2,1)}, u32[]{:S(2)}, u32[]{:S(2)}) collective-permute-start(bf16[1536,896]{1,0:T(8,128)(2,1)} %bitcast.5.own_ref), channel_id=1, source_target_pairs={{0,1},{1,0},{2,3},{3,2},{4,5},{5,4},{6,7},{7,6},{8,9},{9,8},{10,11... | collective-permute-start | bytes 8257544 | tf_op jit(solution)/shard_map/ppermute | solution.py:518
  97.3 45.5 %all-to-all-start.2 = ((bf16[64,24,896]{2,1,0:T(8,128)(2,1)}), bf16[64,24,896]{2,1,0:T(8,128)(2,1)S(1)}, u32[]{:S(2)}, u32[]{:S(2)}) async-start(bf16[64,24,896]{2,1,0:T(8,128)(2,1)} %bitcast.10), calls=%async_computation.2 | async-start | bytes 5505024 | tf_op jit(solution)/shard_map/all_to_all | solution.py:511
  129.0 3.8 %collective-permute-start.4 = (bf16[768,896]{1,0:T(8,128)(2,1)}, bf16[768,896]{1,0:T(8,128)(2,1)S(1)}, u32[]{:S(2)}, u32[]{:S(2)}) collective-permute-start(bf16[768,896]{1,0:T(8,128)(2,1)} %get-tuple-element.41), channel_id=1, source_target_pairs={{0,1},{1,0},{2,3},{3,2},{4,5},{5,4},{6,7},{7,6},{8,9},{9,8},{10,11... | collective-permute-start | bytes 4128776 | tf_op jit(solution)/shard_map/ppermute | solution.py:518
  129.8 4.9 %collective-permute-start.5 = (bf16[768,896]{1,0:T(8,128)(2,1)}, bf16[768,896]{1,0:T(8,128)(2,1)S(1)}, u32[]{:S(2)}, u32[]{:S(2)}) collective-permute-start(bf16[768,896]{1,0:T(8,128)(2,1)} %get-tuple-element.42), channel_id=1, source_target_pairs={{0,1},{1,0},{2,3},{3,2},{4,5},{5,4},{6,7},{7,6},{8,9},{9,8},{10,11... | collective-permute-start | bytes 4128776 | tf_op jit(solution)/shard_map/ppermute | solution.py:518
  142.8 1.5 copy-start.1
  144.3 43.7 %all-to-all-start.3 = ((bf16[64,24,896]{2,1,0:T(8,128)(2,1)}), bf16[64,24,896]{2,1,0:T(8,128)(2,1)}, u32[]{:S(2)}, u32[]{:S(2)}) async-start(bf16[64,24,896]{2,1,0:T(8,128)(2,1)} %bitcast.12), calls=%async_computation.3 | async-start | bytes 5505024 | tf_op jit(solution)/shard_map/all_to_all | solution.py:511

commit v4 on v3

v4 whole, which is shorter than its diff:
```python
import functools
import jax
import jax.numpy as jnp
from jax import lax
from jax.experimental import pallas as pl
from jax.experimental.pallas import tpu as pltpu
from jax.sharding import PartitionSpec as P

BF16 = jnp.bfloat16
F32 = jnp.float32
SLOTS = 12
ROWS = 2 * SLOTS
PLANES = 4
PLANE_ROWS = PLANES * SLOTS
GROUP = 16
TILE = GROUP * ROWS

NN = (((1,), (0,)), ((), ()))
NT = (((1,), (1,)), ((), ()))
TN = (((0,), (0,)), ((), ()))


def dot(a, b, dims=NN):
    return lax.dot_general(a, b, dims, preferred_element_type=F32)


def params(mebibytes):
    return pltpu.CompilerParams(
        vmem_limit_bytes=mebibytes * 1024 * 1024, dimension_semantics=("arbitrary",)
    )


def cost():
    return pl.CostEstimate(flops=1, bytes_accessed=1, transcendentals=0)


def spread(rows_of):
    return jnp.concatenate(
        [jnp.broadcast_to(rows_of[i : i + 1], (ROWS, rows_of.shape[1])) for i in range(GROUP)], axis=0
    )


def routing(route_ref, first):
    top, toks = route_ref.shape
    route = route_ref[...]
    ids = lax.broadcasted_iota(jnp.int32, (GROUP, toks), 0) + first
    hits = [jnp.broadcast_to(route[k : k + 1], (GROUP, toks)) == ids for k in range(top)]
    named = sum(h.astype(F32) for h in hits)
    return named, hits


def selection(named):
    toks = named.shape[1]
    before = (
        lax.broadcasted_iota(jnp.int32, (toks, toks), 0)
        < lax.broadcasted_iota(jnp.int32, (toks, toks), 1)
    ).astype(BF16)
    slot = dot(named.astype(BF16), before)
    code = jnp.where(named > 0, slot, -100.0)
    code = jnp.concatenate([code, code + float(SLOTS)], axis=1)
    place = lax.broadcasted_iota(jnp.int32, (ROWS, 2 * toks), 0).astype(F32)
    place = jnp.concatenate([place] * GROUP, axis=0)
    return spread(code) == place


def plane_selection(info_ref, first, count):
    info = info_ref[...]
    top, toks = info.shape[0] // 2, info.shape[1]
    each = toks // PLANES
    ids = (lax.broadcasted_iota(jnp.int32, (count, toks), 0) + first).astype(F32)
    hits = [jnp.broadcast_to(info[k : k + 1], (count, toks)) == ids for k in range(top)]
    named = sum(h.astype(F32) for h in hits)
    chosen = sum(
        jnp.where(h, jnp.broadcast_to(info[top + k : top + k + 1], h.shape), 0.0)
        for k, h in enumerate(hits)
    )
    row = lax.broadcasted_iota(jnp.int32, (toks, toks), 0)
    col = lax.broadcasted_iota(jnp.int32, (toks, toks), 1)
    shift = each.bit_length() - 1
    before = jnp.logical_and(row < col, (row >> shift) == (col >> shift)).astype(F32).astype(BF16)
    chip = (lax.broadcasted_iota(jnp.int32, (count, toks), 1) >> shift).astype(F32)
    code = jnp.where(named > 0, dot(named.astype(BF16), before) + SLOTS * chip, -100.0)

    def widen(x):
        return jnp.concatenate(
            [jnp.broadcast_to(x[e : e + 1], (PLANE_ROWS, toks)) for e in range(count)], axis=0
        )

    place = lax.broadcasted_iota(jnp.int32, (PLANE_ROWS, toks), 0).astype(F32)
    sel = widen(code) == jnp.concatenate([place] * count, axis=0)
    return sel, hits, jnp.where(sel, widen(chosen), 0.0)


def column(refs, h):
    half = refs[0].shape[1] // 2
    return jnp.concatenate([ref[:, h * half : (h + 1) * half] for ref in refs], axis=0)


def plane_send_kernel(first_ref, info_ref, rows0, rows1, rows2, rows3, out_ref):
    count = out_ref.shape[0]
    sel, _, weights = plane_selection(info_ref, first_ref[0] + pl.program_id(0) * count, count)
    weight = jnp.sum(weights, axis=1, keepdims=True)
    take = sel.astype(F32).astype(BF16)
    for h in range(2):
        picked = (dot(take, column((rows0, rows1, rows2, rows3), h)) * weight).astype(BF16)
        out_ref[:, h * PLANE_ROWS : (h + 1) * PLANE_ROWS, :] = picked.reshape(
            count, PLANE_ROWS, picked.shape[1]
        )


PLANE_STEP = 4


def plane_send(first, info, pieces, experts):
    toks, width = pieces[0].shape
    whole = lambda i, m: (0, 0)
    return pl.pallas_call(
        plane_send_kernel,
        grid_spec=pltpu.PrefetchScalarGridSpec(
            num_scalar_prefetch=1,
            grid=(experts // PLANE_STEP,),
            in_specs=[pl.BlockSpec(info.shape, whole)]
            + [pl.BlockSpec((toks, width), whole)] * PLANES,
            out_specs=pl.BlockSpec(
                (PLANE_STEP, 2 * PLANE_ROWS, width // 2), lambda i, m: (i, 0, 0)
            ),
        ),
        out_shape=jax.ShapeDtypeStruct((experts, 2 * PLANE_ROWS, width // 2), BF16),
        compiler_params=params(60),
        cost_estimate=cost(),
        name="send_scaled",
    )(first, info, *pieces)


def stacked(x):
    half = x.shape[1] // 2
    return jnp.concatenate([x[:, :half], x[:, half:]], axis=0)


def send_kernel(route_ref, rows_ref, out_ref):
    named, _ = routing(route_ref, pl.program_id(0) * GROUP)
    sel = selection(named).astype(F32).astype(BF16)
    out_ref[...] = dot(sel, stacked(rows_ref[...])).astype(BF16)


def send_rows(route_t, rows, experts):
    toks, width = rows.shape
    top = route_t.shape[0]
    half = width // 2
    return pl.pallas_call(
        send_kernel,
        grid=(experts // GROUP,),
        in_specs=[
            pl.BlockSpec((top, toks), lambda i: (0, 0)),
            pl.BlockSpec((toks, width), lambda i: (0, 0)),
        ],
        out_specs=pl.BlockSpec((TILE, half), lambda i: (i, 0)),
        out_shape=jax.ShapeDtypeStruct((experts * ROWS, half), BF16),
        compiler_params=params(60),
        cost_estimate=cost(),
        name="send_tokens",
    )(route_t, rows)


def select_kernel(route_ref, out_ref):
    named, _ = routing(route_ref, pl.program_id(0) * GROUP)
    out_ref[...] = selection(named).astype(F32).T.astype(BF16)


def select_rows(route_t, experts):
    top, toks = route_t.shape
    return pl.pallas_call(
        select_kernel,
        grid=(experts // GROUP,),
        in_specs=[pl.BlockSpec((top, toks), lambda i: (0, 0))],
        out_specs=pl.BlockSpec((2 * toks, TILE), lambda i: (0, i)),
        out_shape=jax.ShapeDtypeStruct((2 * toks, experts * ROWS), BF16),
        compiler_params=params(60),
        cost_estimate=cost(),
        name="select_rows",
    )(route_t)


COLUMNS = 2
ORDERED = COLUMNS * PLANE_ROWS


def ordering(back=False):
    n = 2 * ORDERED
    row = lax.broadcasted_iota(jnp.int32, (n, n), int(back))
    col = lax.broadcasted_iota(jnp.int32, (n, n), 1 - int(back))
    upper = (row >= ORDERED).astype(jnp.int32)
    within = row - upper * ORDERED
    second = (within >= PLANE_ROWS).astype(jnp.int32)
    within = within - second * PLANE_ROWS
    chip = (within * 43) >> 9
    target = chip * (COLUMNS * ROWS) + second * ROWS + upper * SLOTS + within - SLOTS * chip
    return (col == target).astype(F32).astype(BF16)


def plane_of(r, plane):
    return lax.rem(plane + PLANES - r, PLANES)


def put_in_order(own_ref, other_ref, mine, plane, step, held, out_ref):
    order = ordering()
    n = COLUMNS * ROWS
    for which, ref in ((mine, own_ref), (1 - mine, other_ref)):
        for b in range(ref.shape[1] // n):
            raw = jnp.concatenate(
                [ref[plane_of(r, plane), b * n : (b + 1) * n, :] for r in range(PLANES)], axis=0
            )
            both = dot(order, raw).astype(BF16)
            at = pl.multiple_of(step * (GROUP * SLOTS) + b * ORDERED, ORDERED)
            for h in range(2):
                part = both[h * ORDERED : (h + 1) * ORDERED]
                held[2 * which + h, pl.ds(at, ORDERED), :] = part
                out_ref[2 * which + h, b * ORDERED : (b + 1) * ORDERED, :] = part


def weight_copies(gate_hbm, up_hbm, down_hbm, gate_w, up_w, down_w, sems):
    quarter = down_w.shape[2]
    downs = [
        pltpu.make_async_copy(
            down_hbm.at[:, q * quarter : (q + 1) * quarter], down_w.at[q], sems.at[2 + q]
        )
        for q in range(4)
    ]
    gates = pltpu.make_async_copy(gate_hbm, gate_w, sems.at[0])
    ups = pltpu.make_async_copy(up_hbm, up_w, sems.at[1])
    return [gates, ups], downs


def forward_kernel(
    steps, ff_steps, mine_ref, own_ref, other_ref, gate_hbm, up_hbm, down_hbm,
    gate_ref, up_ref, hidden_ref, rows_ref, far0, far1, near_ref,
    held, hidden_all, gate_w, up_w, down_w, sems,
):
    i = pl.program_id(0)
    mine, plane = mine_ref[0], mine_ref[1]
    quarter = own_ref.shape[2]
    ins, downs = weight_copies(gate_hbm, up_hbm, down_hbm, gate_w, up_w, down_w, sems)

    @pl.when(i == 0)
    def _():
        for copy in ins + downs:
            copy.start()

    @pl.when(i < steps)
    def _():
        put_in_order(own_ref, other_ref, mine, plane, i, held, rows_ref)

    for f in range(ff_steps):
        @pl.when(i == steps + f)
        def _():
            if f == 0:
                for copy in ins:
                    copy.wait()
            wide = gate_ref.shape[1]
            at = slice(f * wide, (f + 1) * wide)
            gate = sum(dot(held[q], gate_w[q * quarter : (q + 1) * quarter, at]) for q in range(4))
            up = sum(dot(held[q], up_w[q * quarter : (q + 1) * quarter, at]) for q in range(4))
            gate_ref[...] = gate
            up_ref[...] = up
            hidden = (gate * jax.nn.sigmoid(gate) * up).astype(BF16)
            hidden_ref[...] = hidden
            hidden_all[:, at] = hidden

    for h, far_ref in enumerate((far0, far1)):
        @pl.when(i == steps + ff_steps + h)
        def _():
            if h == 0:
                for copy in downs:
                    copy.wait()
            part = dot(hidden_all[...], down_w[2 * (1 - mine) + h]).astype(BF16)
            far_ref[...] = part.reshape(far_ref.shape)

    for h in range(2):
        @pl.when(i == steps + ff_steps + 2 + h)
        def _():
            part = dot(hidden_all[...], down_w[2 * mine + h]).astype(BF16)
            near_ref[...] = part.reshape(near_ref.shape)


def weight_scratch(model, ff):
    return [
        pltpu.VMEM((model, ff), BF16),
        pltpu.VMEM((model, ff), BF16),
        pltpu.VMEM((4, ff, model // 4), BF16),
        pltpu.SemaphoreType.DMA((6,)),
    ]


def forward(mine, own, other, gate_w, up_w, down_w):
    raw, quarter = own.shape
    model, ff = gate_w.shape
    rows, ff_steps, columns = raw // 2, 2, raw // (2 * PLANE_ROWS)
    steps = raw // TILE
    last = steps + ff_steps
    source = pl.BlockSpec(
        (PLANES, TILE // PLANES, quarter), lambda i, m: (0, jnp.minimum(i, steps - 1), 0)
    )
    ffs = pl.BlockSpec(
        (rows, ff // ff_steps), lambda i, m: (0, jnp.clip(i - steps, 0, ff_steps - 1))
    )
    ordered = pl.BlockSpec(
        (4, GROUP * SLOTS, quarter), lambda i, m: (0, jnp.minimum(i, steps - 1), 0)
    )
    far = pl.BlockSpec((columns, PLANE_ROWS, quarter), lambda i, m: (0, 0, 0))
    near = pl.BlockSpec(
        (columns, PLANE_ROWS, quarter), lambda i, m: (0, jnp.clip(i - last - 2, 0, 1), 0)
    )
    hbm = pl.BlockSpec(memory_space=pl.ANY)
    by_plane = (PLANES, raw // PLANES, quarter)
    return pl.pallas_call(
        functools.partial(forward_kernel, steps, ff_steps),
        grid_spec=pltpu.PrefetchScalarGridSpec(
            num_scalar_prefetch=1,
            grid=(last + 4,),
            in_specs=[source, source, hbm, hbm, hbm],
            out_specs=[ffs, ffs, ffs, ordered, far, far, near],
            scratch_shapes=[
                pltpu.VMEM((4, rows, quarter), BF16),
                pltpu.VMEM((rows, ff), BF16),
                *weight_scratch(model, ff),
            ],
        ),
        out_shape=[
            jax.ShapeDtypeStruct((rows, ff), F32),
            jax.ShapeDtypeStruct((rows, ff), F32),
            jax.ShapeDtypeStruct((rows, ff), BF16),
            jax.ShapeDtypeStruct((4, rows, quarter), BF16),
            jax.ShapeDtypeStruct((columns, PLANE_ROWS, quarter), BF16),
            jax.ShapeDtypeStruct((columns, PLANE_ROWS, quarter), BF16),
            jax.ShapeDtypeStruct((columns, 2 * PLANE_ROWS, quarter), BF16),
        ],
        compiler_params=params(60),
        cost_estimate=cost(),
        name="expert_forward",
    )(mine, own.reshape(by_plane), other.reshape(by_plane), gate_w, up_w, down_w)


def backward_kernel(
    ff_steps, mine_ref, own0, own1, other0, other1, gate_hbm, up_hbm, down_hbm, gate_ref, up_ref,
    gate_grad_ref, up_grad_ref, far0, far1, near_ref,
    gate_grads, up_grads, gate_w, up_w, down_w, sems,
):
    i = pl.program_id(0)
    mine = mine_ref[0]
    rows, quarter = far0.shape
    ins, downs = weight_copies(gate_hbm, up_hbm, down_hbm, gate_w, up_w, down_w, sems)

    @pl.when(i == 0)
    def _():
        for copy in downs + ins:
            copy.start()

    for f in range(ff_steps):
        @pl.when(i == f)
        def _():
            if f == 0:
                for copy in downs:
                    copy.wait()
            wide = gate_ref.shape[1]
            at = slice(f * wide, (f + 1) * wide)
            hidden_grad = sum(
                dot(ref[...].reshape(rows, quarter), down_w[q, at, :], NT)
                for q, ref in (
                    (2 * mine, own0),
                    (2 * mine + 1, own1),
                    (2 * (1 - mine), other0),
                    (2 * (1 - mine) + 1, other1),
                )
            )
            gate, up = gate_ref[...], up_ref[...]
            logistic = jax.nn.sigmoid(gate)
            gate_grad = (hidden_grad * up * logistic * (1.0 + gate * (1.0 - logistic))).astype(BF16)
            up_grad = (hidden_grad * (gate * logistic)).astype(BF16)
            gate_grad_ref[...] = gate_grad
            up_grad_ref[...] = up_grad
            gate_grads[:, at] = gate_grad
            up_grads[:, at] = up_grad

    def input_grads(q):
        at = pl.ds(pl.multiple_of(q * quarter, quarter), quarter)
        return (
            dot(gate_grads[...], gate_w[at, :], NT) + dot(up_grads[...], up_w[at, :], NT)
        ).astype(BF16)

    for h, far_ref in enumerate((far0, far1)):
        @pl.when(i == ff_steps + h)
        def _():
            if h == 0:
                for copy in ins:
                    copy.wait()
            far_ref[...] = input_grads(2 * (1 - mine) + h)

    for h in range(2):
        @pl.when(i == ff_steps + 2 + h)
        def _():
            near_ref[...] = input_grads(2 * mine + h)


def backward(mine, own, other, gate_w, up_w, down_w, gate_pre, up_pre):
    columns, _, quarter = own.shape
    model, ff = gate_w.shape
    rows, ff_steps = columns * PLANE_ROWS, 2
    halves = [
        pl.BlockSpec((columns, PLANE_ROWS, quarter), lambda i, m, h=h: (0, h, 0)) for h in range(2)
    ]
    ffs = pl.BlockSpec((rows, ff // ff_steps), lambda i, m: (0, jnp.clip(i, 0, ff_steps - 1)))
    far = pl.BlockSpec((rows, quarter), lambda i, m: (0, 0))
    near = pl.BlockSpec((rows, quarter), lambda i, m: (0, jnp.clip(i - ff_steps - 2, 0, 1)))
    hbm = pl.BlockSpec(memory_space=pl.ANY)
    return pl.pallas_call(
        functools.partial(backward_kernel, ff_steps),
        grid_spec=pltpu.PrefetchScalarGridSpec(
            num_scalar_prefetch=1,
            grid=(ff_steps + 4,),
            in_specs=[*halves, *halves, hbm, hbm, hbm, ffs, ffs],
            out_specs=[ffs, ffs, far, far, near],
            scratch_shapes=[
                pltpu.VMEM((rows, ff), BF16),
                pltpu.VMEM((rows, ff), BF16),
                *weight_scratch(model, ff),
            ],
        ),
        out_shape=[
            jax.ShapeDtypeStruct((rows, ff), BF16),
            jax.ShapeDtypeStruct((rows, ff), BF16),
            jax.ShapeDtypeStruct((rows, quarter), BF16),
            jax.ShapeDtypeStruct((rows, quarter), BF16),
            jax.ShapeDtypeStruct((rows, 2 * quarter), BF16),
        ],
        compiler_params=params(60),
        cost_estimate=cost(),
        name="expert_backward",
    )(mine, own, own, other, other, gate_w, up_w, down_w, gate_pre, up_pre)


def add_kernel(near_ref, far0, far1, out_ref):
    for h, far in enumerate((far0, far1)):
        at = slice(h * PLANE_ROWS, (h + 1) * PLANE_ROWS)
        out_ref[:, at, :] = (near_ref[:, at, :].astype(F32) + far[...].astype(F32)).astype(BF16)


def add_halves(near, fars):
    columns, both, quarter = near.shape
    step = columns // 4
    wide = pl.BlockSpec((step, both, quarter), lambda i: (i, 0, 0))
    half = pl.BlockSpec((step, both // 2, quarter), lambda i: (i, 0, 0))
    return pl.pallas_call(
        add_kernel,
        grid=(4,),
        in_specs=[wide, half, half],
        out_specs=wide,
        out_shape=jax.ShapeDtypeStruct(near.shape, BF16),
        compiler_params=params(48),
        cost_estimate=cost(),
        name="add_halves",
    )(near, *fars)


def pack_kernel(plane_ref, near_ref, far0, far1, out_ref):
    order = ordering(back=True)
    n = COLUMNS * ROWS
    quarter = out_ref.shape[2]
    plane = plane_ref[1]
    for b in range(out_ref.shape[1] // n):
        at = slice(b * ORDERED, (b + 1) * ORDERED)
        both = jnp.concatenate(
            [
                (
                    near_ref[at, h * quarter : (h + 1) * quarter].astype(F32)
                    + far[at, :].astype(F32)
                ).astype(BF16)
                for h, far in enumerate((far0, far1))
            ],
            axis=0,
        )
        raw = dot(order, both).astype(BF16)
        for r in range(PLANES):
            out_ref[plane_of(r, plane), b * n : (b + 1) * n, :] = raw[r * n : (r + 1) * n]


def pack(mine, near, fars):
    rows, width = near.shape
    step_rows = GROUP * SLOTS
    return pl.pallas_call(
        pack_kernel,
        grid_spec=pltpu.PrefetchScalarGridSpec(
            num_scalar_prefetch=1,
            grid=(rows // step_rows,),
            in_specs=[
                pl.BlockSpec((step_rows, width), lambda i, m: (i, 0)),
                pl.BlockSpec((step_rows, width // 2), lambda i, m: (i, 0)),
                pl.BlockSpec((step_rows, width // 2), lambda i, m: (i, 0)),
            ],
            out_specs=pl.BlockSpec(
                (PLANES, TILE // PLANES, width // 2), lambda i, m: (0, i, 0)
            ),
        ),
        out_shape=jax.ShapeDtypeStruct((PLANES, 2 * rows // PLANES, width // 2), BF16),
        compiler_params=params(48),
        cost_estimate=cost(),
        name="pack",
    )(mine, near, *fars).reshape(2 * rows, width // 2)


def weights_kernel(
    mine_ref, rows_ref, own_ref, other_ref, hidden_ref, gate_grad_ref, up_grad_ref,
    gate_w, up_w, down_w,
):
    rows = rows_ref[0]
    gate_w[...] = dot(rows, gate_grad_ref[...], TN).astype(BF16)
    up_w[...] = dot(rows, up_grad_ref[...], TN).astype(BF16)

    @pl.when(pl.program_id(0) < 2)
    def _():
        scaled = own_ref[...].reshape(rows.shape)
        down_w[...] = dot(hidden_ref[...], scaled, TN).astype(BF16)

    @pl.when(pl.program_id(0) >= 2)
    def _():
        scaled = other_ref[...].reshape(rows.shape)
        down_w[...] = dot(hidden_ref[...], scaled, TN).astype(BF16)


def weight_grads(mine, token_rows, own, other, hidden, gate_grad, up_grad):
    quarters, rows, quarter = token_rows.shape
    columns = own.shape[0]
    ff = hidden.shape[1]
    place = lambda i, m: lax.rem(2 * m[0] + i, 4)
    whole = pl.BlockSpec((rows, ff), lambda i, m: (0, 0))
    half = (columns, PLANE_ROWS, quarter)
    return pl.pallas_call(
        weights_kernel,
        grid_spec=pltpu.PrefetchScalarGridSpec(
            num_scalar_prefetch=1,
            grid=(quarters,),
            in_specs=[
                pl.BlockSpec((1, rows, quarter), lambda i, m: (place(i, m), 0, 0)),
                pl.BlockSpec(half, lambda i, m: (0, jnp.minimum(i, 1), 0)),
                pl.BlockSpec(half, lambda i, m: (0, jnp.maximum(i - 2, 0), 0)),
                whole, whole, whole,
            ],
            out_specs=[
                pl.BlockSpec((quarter, ff), lambda i, m: (place(i, m), 0)),
                pl.BlockSpec((quarter, ff), lambda i, m: (place(i, m), 0)),
                pl.BlockSpec((ff, quarter), lambda i, m: (0, place(i, m))),
            ],
        ),
        out_shape=[
            jax.ShapeDtypeStruct((quarters * quarter, ff), BF16),
            jax.ShapeDtypeStruct((quarters * quarter, ff), BF16),
            jax.ShapeDtypeStruct((ff, quarters * quarter), BF16),
        ],
        compiler_params=params(60),
        cost_estimate=cost(),
        name="weight_grads",
    )(mine, token_rows, own, other, hidden, gate_grad, up_grad)


def outputs_kernel(
    first_ref, info_ref, cot0, cot1, cot2, cot3, back_ref, out0, out1, out2, out3, grad_ref, total,
):
    i = pl.program_id(0)

    @pl.when(i == 0)
    def _():
        total[...] = jnp.zeros_like(total)
        grad_ref[...] = jnp.zeros_like(grad_ref)

    count, _, half = back_ref.shape
    toks = cot0.shape[0]
    sel, hits, weight = plane_selection(info_ref, first_ref[0] + i * count, count)
    high = weight.astype(BF16)
    low = (weight - high.astype(F32)).astype(BF16)
    products = 0.0
    for h in range(2):
        back = back_ref[:, h * PLANE_ROWS : (h + 1) * PLANE_ROWS, :].reshape(
            count * PLANE_ROWS, half
        )
        total[h] += dot(high, back, TN) + dot(low, back, TN)
        products += dot(back, column((cot0, cot1, cot2, cot3), h), NT)
    products = jnp.where(sel, products, 0.0)
    sums = jnp.concatenate(
        [
            jnp.sum(products[e * PLANE_ROWS : (e + 1) * PLANE_ROWS], axis=0, keepdims=True)
            for e in range(count)
        ],
        axis=0,
    )
    grad_ref[...] += jnp.concatenate(
        [jnp.sum(jnp.where(h, sums, 0.0), axis=0, keepdims=True) for h in hits], axis=0
    )

    @pl.when(i == pl.num_programs(0) - 1)
    def _():
        for r, ref in enumerate((out0, out1, out2, out3)):
            for h in range(2):
                ref[:, h * half : (h + 1) * half] = total[h, r * toks : (r + 1) * toks].astype(BF16)


def token_outputs(first, info, cots, back):
    toks, width = cots[0].shape
    experts, both, half = back.shape
    whole = lambda i, m: (0, 0)
    wide = pl.BlockSpec((toks, width), whole)
    grads = (info.shape[0] // 2, info.shape[1])
    return pl.pallas_call(
        outputs_kernel,
        grid_spec=pltpu.PrefetchScalarGridSpec(
            num_scalar_prefetch=1,
            grid=(experts // PLANE_STEP,),
            in_specs=[pl.BlockSpec(info.shape, whole)]
            + [wide] * PLANES
            + [pl.BlockSpec((PLANE_STEP, both, half), lambda i, m: (i, 0, 0))],
            out_specs=[wide] * PLANES + [pl.BlockSpec(grads, whole)],
            scratch_shapes=[pltpu.VMEM((2, PLANES * toks, half), F32)],
        ),
        out_shape=[jax.ShapeDtypeStruct((toks, width), BF16)] * PLANES
        + [jax.ShapeDtypeStruct(grads, F32)],
        compiler_params=params(60),
        cost_estimate=cost(),
        name="token_outputs",
    )(first, info, *cots, back)


def inputs_kernel(sel_ref, back_ref, out_ref, total):
    i = pl.program_id(0)
    toks, width = out_ref.shape
    half = width // 2
    part = dot(sel_ref[...], back_ref[...])

    @pl.when(i == 0)
    def _():
        total[...] = part

    @pl.when(i > 0)
    def _():
        total[...] += part

    @pl.when(i == pl.num_programs(0) - 1)
    def _():
        out_ref[:, :half] = total[:toks].astype(BF16)
        out_ref[:, half:] = total[toks:].astype(BF16)


def token_grads(select, back):
    raw, half = back.shape
    toks = select.shape[0] // 2
    return pl.pallas_call(
        inputs_kernel,
        grid=(2,),
        in_specs=[
            pl.BlockSpec((2 * toks, raw // 2), lambda i: (0, i)),
            pl.BlockSpec((raw // 2, half), lambda i: (i, 0)),
        ],
        out_specs=pl.BlockSpec((toks, 2 * half), lambda i: (0, 0)),
        out_shape=jax.ShapeDtypeStruct((toks, 2 * half), BF16),
        scratch_shapes=[pltpu.VMEM((2 * toks, half), F32)],
        compiler_params=params(60),
        cost_estimate=cost(),
        name="token_grads",
    )(select, back)


def exchange(x):
    experts = lax.axis_size("expert")
    y = lax.all_to_all(
        x.reshape(experts, ROWS, -1), "expert", split_axis=0, concat_axis=0, tiled=True
    )
    return y.reshape(x.shape)


def plane_exchange(x):
    count = lax.axis_size("expert") // PLANES
    groups = [[z * count + i for i in range(count)] for z in range(PLANES)]
    return lax.all_to_all(
        x, "expert", split_axis=0, concat_axis=0, tiled=True, axis_index_groups=groups
    )


def along(x, planes):
    experts = lax.axis_size("expert")
    count = experts // PLANES
    return lax.ppermute(
        x, "expert", [(i, (i + planes * count) % experts) for i in range(experts)]
    )


def swap(x):
    return lax.ppermute(x, "mp", [(0, 1), (1, 0)])


def body(tokens, cotangent, route_ids, gate_probs, w_gate, w_up, w_down):
    experts = lax.axis_size("expert")
    count = experts // PLANES
    plane = lax.axis_index("expert") // count
    mine = jnp.stack([lax.axis_index("mp"), plane]).astype(jnp.int32)
    first = (plane * count).astype(jnp.int32).reshape(1)
    route_t, probs_t = route_ids.T, gate_probs.T
    gate_w, up_w, down_w = w_gate[0], w_up[0], w_down[0]

    send_tokens = send_rows(route_t, tokens, experts)
    info = jnp.concatenate([route_t.astype(F32), probs_t], axis=0)
    infos = [info] + [along(info, r) for r in range(1, PLANES)]
    info = jnp.concatenate(infos, axis=1)
    cots = [cotangent] + [along(cotangent, r) for r in range(1, PLANES)]
    send_scaled = plane_send(first, info, cots, count)
    got_tokens, send_scaled = lax.optimization_barrier((exchange(send_tokens), send_scaled))
    got_scaled = plane_exchange(send_scaled)

    gate_pre, up_pre, hidden, token_rows, far0, far1, out_near = forward(
        mine, got_tokens, swap(got_tokens), gate_w, up_w, down_w
    )
    send_out = add_halves(out_near, [swap(far0), swap(far1)])
    got_scaled, send_out = lax.optimization_barrier((got_scaled, send_out))
    back_out = plane_exchange(send_out)

    other_scaled = swap(got_scaled)
    gate_grad, up_grad, far0, far1, in_near = backward(
        mine, got_scaled, other_scaled, gate_w, up_w, down_w, gate_pre, up_pre
    )
    send_in = pack(mine, in_near, [swap(far0), swap(far1)])
    back_out, send_in = lax.optimization_barrier((back_out, send_in))
    back_in = exchange(send_in)

    *parts, grad_part = token_outputs(first, info, cots, back_out)
    toks = tokens.shape[0]
    grad_parts = [grad_part[:, r * toks : (r + 1) * toks] for r in range(PLANES)]
    layer_out = parts[0].astype(F32)
    grad_probs = grad_parts[0]
    for r in range(1, PLANES):
        layer_out += along(parts[r], PLANES - r).astype(F32)
        grad_probs += along(grad_parts[r], PLANES - r)
    layer_out = layer_out.astype(BF16)
    grad_probs = lax.psum(grad_probs, "mp").T
    grad_w_gate, grad_w_up, grad_w_down = weight_grads(
        mine, token_rows, got_scaled, other_scaled, hidden, gate_grad, up_grad
    )
    grad_tokens = token_grads(select_rows(route_t, experts), back_in)
    return (
        layer_out, grad_tokens, grad_probs, grad_w_gate[None], grad_w_up[None], grad_w_down[None],
    )


def solution(mesh):
    return jax.shard_map(
        body,
        mesh=mesh,
        in_specs=(
            P("expert", "mp"),
            P("expert", "mp"),
            P("expert", None),
            P("expert", None),
            P("expert", None, "mp"),
            P("expert", None, "mp"),
            P("expert", "mp", None),
        ),
        out_specs=(
            P("expert", "mp"),
            P("expert", "mp"),
            P("expert", None),
            P("expert", None, "mp"),
            P("expert", None, "mp"),
            P("expert", "mp", None),
        ),
        check_vma=False,
    )
```

time: 192 us -> 232 us (1.21)
  starting transfers between devices: 38.1 us -> 55.7 us
  blocking collectives: 3.75 us -> 14.1 us
  Pallas kernels: 87.2 us -> 91.8 us
  other arithmetic: 0 us -> 3.1 us
  waiting for transfers between devices: 59.4 us -> 62 us
    all_to_all x4 -> x2, waiting for transfers between devices: 49.7 us -> 0.01 us  [exchange(): lax.all_to_all(x.reshape(experts, ROWS, -1), 'expert', split_axis=0, conc...]
    ppermute x0 -> x12, waiting for transfers between devices: none -> 48 us  [along(): lax.ppermute(x, 'expert', [(i, (i + planes * count) % experts) for i in r...]
    ppermute x0 -> x12, starting transfers between devices: none -> 16.4 us  [along(): lax.ppermute(x, 'expert', [(i, (i + planes * count) % experts) for i in r...]
    all_to_all x0 -> x2, starting transfers between devices: none -> 14.5 us  [plane_exchange(): lax.all_to_all(x, 'expert', split_axis=0, concat_axis=0, tiled=True, axis...]
    all_to_all x4 -> x2, starting transfers between devices: 32.2 us -> 19.2 us  [exchange(): lax.all_to_all(x.reshape(experts, ROWS, -1), 'expert', split_axis=0, conc...]
    psum x1, blocking collectives: 3.75 us -> 14.1 us  [body(): grad_probs = lax.psum(grad_probs, 'mp').T]
    all_to_all x0 -> x2, waiting for transfers between devices: none -> 4.32 us  [plane_exchange(): lax.all_to_all(x, 'expert', split_axis=0, concat_axis=0, tiled=True, axis...]
    pallas_call x7 -> x8, Pallas kernels: 61.2 us -> 65 us  [the longest x1 20.1 us: backward(): pl.pallas_call(functools.partial(backward_kernel, ff_steps), grid_spec=pl...]
  transfers between devices with their start and end apart: 10 -> 22, of which waited for: 8 -> 9; matrix products, arithmetic and copies ran while one was open for 0% -> 2% of each run, Pallas kernels for 42% -> 37%
where the time goes in v4:
time: 232 us; the launch traced here: 231 us
  Pallas kernels  91.8 us (40%)
  waiting for transfers between devices  62 us (27%)
  starting transfers between devices  55.7 us (24%)
  blocking collectives  14.1 us (6%)
  local copies, waits for them, and re-layouts  3.65 us (2%)
  other arithmetic  3.1 us (1%)
    ppermute x12, waiting for transfers between devices, along(): lax.ppermute(x, 'expert', [(i, (i + planes * count) % experts) for i in r...  48 us
    pallas_call x1, Pallas kernels, forward(): pl.pallas_call(functools.partial(forward_kernel, steps, ff_steps), grid_s...  23.7 us
    pallas_call x1, Pallas kernels, backward(): pl.pallas_call(functools.partial(backward_kernel, ff_steps), grid_spec=pl...  20.1 us
    all_to_all x2, starting transfers between devices, exchange(): lax.all_to_all(x.reshape(experts, ROWS, -1), 'expert', split_axis=0, conc...  19.2 us
    ppermute x12, starting transfers between devices, along(): lax.ppermute(x, 'expert', [(i, (i + planes * count) % experts) for i in r...  16.4 us
    pallas_call x1, Pallas kernels, weight_grads(): pl.pallas_call(weights_kernel, grid_spec=pltpu.PrefetchScalarGridSpec(num...  16.1 us
    all_to_all x2, starting transfers between devices, plane_exchange(): lax.all_to_all(x, 'expert', split_axis=0, concat_axis=0, tiled=True, axis...  14.5 us
    psum x1, blocking collectives, body(): grad_probs = lax.psum(grad_probs, 'mp').T  14.1 us
  transfers between devices with their start and end apart: 22, of which 9 were waited for; matrix products, arithmetic and copies ran while one was open for 2% of the time, Pallas kernels for 37%

profile of v4, /device:TPU:7, one launch (start us, length us, event | category | flops | bytes accessed | tf_op | source)
XLA Modules:
  0.0 231.1 jit_solution(7030998635909246026)
XLA Ops:
  0.6 4.2 %send_tokens.1 = bf16[1536,896]{1,0:T(8,128)(2,1)} custom-call(s32[8,64]{1,0:T(8,128)} %bitcast.29, bf16[64,1792]{1,0:T(8,128)(2,1)} %rows_ref.1), custom_call_target="tpu_custom_call" | custom-call | flops 1 | bytes 1 | tf_op jit(solution)/shard_map/send_tokens/pallas_call | solution.py:150
  4.9 11.2 %all-to-all-start = ((bf16[64,24,896]{2,1,0:T(8,128)(2,1)}), bf16[64,24,896]{2,1,0:T(8,128)(2,1)}, u32[]{:S(2)}, u32[]{:S(2)}) async-start(bf16[64,24,896]{2,1,0:T(8,128)(2,1)} %bitcast.28), calls=%async_computation | async-start | bytes 5505024 | tf_op jit(solution)/shard_map/all_to_all | solution.py:671
  17.4 2.6 %collective-permute-start.4 = (bf16[64,1792]{1,0:T(8,128)(2,1)S(1)}, bf16[64,1792]{1,0:T(8,128)(2,1)S(1)}, u32[]{:S(2)}, u32[]{:S(2)}) collective-permute-start(bf16[64,1792]{1,0:T(8,128)(2,1)S(1)} %copy-done.3), channel_id=1, source_target_pairs={{0,64},{2,66},{4,68},{6,70},{8,72},{10,74},{12,76},{14,78},{16,80}... | collective-permute-start | bytes 688136 | tf_op jit(solution)/shard_map/ppermute | solution.py:688
  21.2 2.2 collective-permute-start.1
  23.4 34.9 %collective-permute-done.2 = f32[16,64]{1,0:T(8,128)S(1)} collective-permute-done((f32[16,64]{1,0:T(8,128)S(1)}, f32[16,64]{1,0:T(8,128)S(1)}, u32[]{:S(2)}, u32[]{:S(2)}) %collective-permute-start.2) | collective-permute-done | bytes 4128 | tf_op jit(solution)/shard_map/ppermute | solution.py:688
  59.6 2.4 %collective-permute-done = f32[16,64]{1,0:T(8,128)S(1)} collective-permute-done((f32[16,64]{1,0:T(8,128)S(1)}, f32[16,64]{1,0:T(8,128)S(1)}, u32[]{:S(2)}, u32[]{:S(2)}) %collective-permute-start) | collective-permute-done | bytes 4128 | tf_op jit(solution)/shard_map/ppermute | solution.py:688
  63.5 4.6 %send_scaled.1 = bf16[16,96,896]{2,1,0:T(8,128)(2,1)} custom-call(s32[1]{0:T(128)} %bitcast.first_ref, f32[16,256]{1,0:T(8,128)} %pad_maximum_fusion.info_ref, bf16[64,1792]{1,0:T(8,128)(2,1)} %cot0.1, bf16[64,1792]{1,0:T(8,128)(2,1)} %copy-done.4, bf16[64,1792]{1,0:T(8,128)(2,1)} %copy-done.5, bf16[64,1792]{1,0:T(8,128)(2,1)} %copy-done.6), custom_call_target="tpu_custom_call" | custom-call | flops 1 | bytes 1 | tf_op jit(solution)/shard_map/send_scaled/pallas_call | solution.py:117
  68.0 1.9 collective-permute-start.6
  70.0 6.3 %all-to-all-start.1 = ((bf16[16,96,896]{2,1,0:T(8,128)(2,1)}), bf16[16,96,896]{2,1,0:T(8,128)(2,1)S(1)}, u32[]{:S(2)}, u32[]{:S(2)}) async-start(bf16[16,96,896]{2,1,0:T(8,128)(2,1)} %send_scaled.1), calls=%async_computation.1 | async-start | bytes 5505024 | tf_op jit(solution)/shard_map/all_to_all | solution.py:680
  76.9 23.7 %expert_forward.1 = (f32[768,512]{1,0:T(8,128)}, f32[768,512]{1,0:T(8,128)}, bf16[768,512]{1,0:T(8,128)(2,1)}, bf16[4,768,896]{2,1,0:T(8,128)(2,1)}, bf16[16,48,...) custom-call(s32[2]{0:T(128)} %pad_add_fusion.mine_ref.plane_ref, ...), custom_call_target="tpu_custom_call" | custom-call | flops 1 | bytes 1 | tf_op jit(solution)/shard_map/expert_forward/pallas_call | solution.py:315
  101.4 2.9 %collective-permute-done.7.far0 = bf16[16,48,896]{2,1,0:T(8,128)(2,1)S(1)} collective-permute-done((bf16[16,48,896]{2,1,0:T(8,128)(2,1)}, bf16[16,48,896]{2,1,0:T(8,128)(2,1)S(1)}, u32[]{:S(2)}, u32[]{:S(2)}) %collective-permute-start.7) | collective-permute-done | bytes 1376288 | tf_op jit(solution)/shard_map/ppermute | solution.py:694
  104.3 2.0 collective-permute-done.8.far1
  106.3 4.3 %add_halves.1 = bf16[16,96,896]{2,1,0:T(8,128)(2,1)} custom-call(bf16[16,96,896]{2,1,0:T(8,128)(2,1)} %get-tuple-element.34.near_ref, bf16[16,48,896]{2,1,0:T(8,128)(2,1)S(1)} %collective-permute-done.7.far0, bf16[16,48,896]{2,1,0:T(8,128)(2,1)S(1)} %collective-permute-done.8.far1), custom_call_target="tpu_custom_call" | custom-call | flops 1 | bytes 1 | tf_op jit(solution)/shard_map/add_halves/pallas_call | solution.py:452
  110.5 4.0 %all-to-all-done.1.own0.own1.own_ref = bf16[16,96,896]{2,1,0:T(8,128)(2,1)S(1)} async-done(((bf16[16,96,896]{2,1,0:T(8,128)(2,1)}), bf16[16,96,896]{2,1,0:T(8,128)(2,1)S(1)}, u32[]{:S(2)}, u32[]{:S(2)}) %all-to-all-start.1) | async-done | bytes 2752544 | tf_op jit(solution)/shard_map/all_to_all | solution.py:680
  116.1 8.2 %all-to-all-start.2 = ((bf16[16,96,896]{2,1,0:T(8,128)(2,1)}), bf16[16,96,896]{2,1,0:T(8,128)(2,1)}, u32[]{:S(2)}, u32[]{:S(2)}) async-start(bf16[16,96,896]{2,1,0:T(8,128)(2,1)} %add_halves.1), calls=%async_computation.2 | async-start | bytes 5505024 | tf_op jit(solution)/shard_map/all_to_all | solution.py:680
  124.3 20.1 %expert_backward.1 = (bf16[768,512]{1,0:T(8,128)(2,1)}, bf16[768,512]{1,0:T(8,128)(2,1)}, bf16[768,896]{1,0:T(8,128)(2,1)}, bf16[768,896]{1,0:T(8,128)(2,1)}, bf16[768,1792]{1,0:T(8,128)(2,1)}) custom-call(s32[2]{0:T(128)} %pad_add_fusion.mine_ref.plane_ref, bf16[16,96,896]{2,1,0:T(8,128)(2,1)} %copy-done.1, bf16[16,96,896]{2,1,0:T(8,128)(2,1)} %copy-done.1, ...), custom_call_target="tpu_custom_call" | custom-call | flops 1 | bytes 1 | tf_op jit(solution)/shard_map/expert_backward/pallas_call | solution.py:415
  144.4 1.8 collective-permute-start.10
  146.3 2.9 %collective-permute-done.10.far0 = bf16[768,896]{1,0:T(8,128)(2,1)S(1)} collective-permute-done((bf16[768,896]{1,0:T(8,128)(2,1)}, bf16[768,896]{1,0:T(8,128)(2,1)S(1)}, u32[]{:S(2)}, u32[]{:S(2)}) %collective-permute-start.10) | collective-permute-done | bytes 1376288 | tf_op jit(solution)/shard_map/ppermute | solution.py:694
  149.1 2.0 collective-permute-done.11.far1
  151.1 5.4 %pack.1 = bf16[4,384,896]{2,1,0:T(8,128)(2,1)} custom-call(s32[2]{0:T(128)S(1)} %copy-done, bf16[768,1792]{1,0:T(8,128)(2,1)} %get-tuple-element.41.near_ref, bf16[768,896]{1,0:T(8,128)(2,1)S(1)} %collective-permute-done.10.far0, bf16[768,896]{1,0:T(8,128)(2,1)S(1)} %collective-permute-done.11.far1), custom_call_target="tpu_custom_call" | custom-call | flops 1 | bytes 1 | tf_op jit(solution)/shard_map/pack/pallas_call | solution.py:489
  156.8 8.0 %all-to-all-start.3 = ((bf16[64,24,896]{2,1,0:T(8,128)(2,1)}), bf16[64,24,896]{2,1,0:T(8,128)(2,1)S(1)}, u32[]{:S(2)}, u32[]{:S(2)}) async-start(bf16[64,24,896]{2,1,0:T(8,128)(2,1)} %bitcast.13), calls=%async_computation.3 | async-start | bytes 5505024 | tf_op jit(solution)/shard_map/all_to_all | solution.py:671
  164.8 7.6 %token_outputs.1 = (bf16[64,1792]{1,0:T(8,128)(2,1)}, bf16[64,1792]{1,0:T(8,128)(2,1)}, bf16[64,1792]{1,0:T(8,128)(2,1)}, bf16[64,1792]{1,0:T(8,128)(2,1)}, f32[8,256]{1,0:T(8,128)}) custom-call(s32[1]{0:T(128)} %bitcast.first_ref, f32[16,256]{1,0:T(8,128)} %pad_maximum_fusion.info_ref, bf16[64,1792]{1,0:T(8,128)(2,1)} %cot0.1, bf16[64,1792]{1,0:T(8,128)(2,1)} %copy-done.4, ...), custom_call_target="tpu_custom_call" | custom-call | flops 1 | bytes 1 | tf_op jit(solution)/shard_map/token_outputs/pallas_call | solution.py:611
  175.7 1.4 collective-permute-start.13
  177.1 2.0 collective-permute-start.12
  179.5 1.5 collective-permute-start.15
  180.9 2.9 %select_rows.1.sel_ref = bf16[128,1536]{1,0:T(8,128)(2,1)} custom-call(s32[8,64]{1,0:T(8,128)} %bitcast.30), custom_call_target="tpu_custom_call" | custom-call | flops 1 | bytes 1 | tf_op jit(solution)/shard_map/select_rows/pallas_call | solution.py:172
  183.8 16.1 %weight_grads.1 = (bf16[3584,512]{1,0:T(8,128)(2,1)}, bf16[3584,512]{1,0:T(8,128)(2,1)}, bf16[512,3584]{1,0:T(8,128)(2,1)}) custom-call(s32[2]{0:T(128)} %pad_add_fusion.mine_ref.plane_ref, bf16[4,768,896]{2,1,0:T(8,128)(2,1)} %get-tuple-element.51.rows_ref, bf16[16,96,896]{2,1,0:T(8,128)(2,1)} %copy-done.1, ...), custom_call_target="tpu_custom_call" | custom-call | flops 1 | bytes 1 | tf_op jit(solution)/shard_map/weight_grads/pallas_call | solution.py:536
  199.9 10.7 %collective-permute-done.16 = f32[8,64]{1,0:T(8,128)S(1)} collective-permute-done((f32[8,64]{1,0:T(8,128)S(1)}, f32[8,64]{1,0:T(8,128)S(1)}, u32[]{:S(2)}, u32[]{:S(2)}) %collective-permute-start.16) | collective-permute-done | bytes 2080 | tf_op jit(solution)/shard_map/ppermute | solution.py:688
  210.6 14.1 %psum.7 = f32[64,8]{0,1:T(8,128)} all-reduce(f32[64,8]{0,1:T(8,128)S(1)} %add_bitcast_fusion), channel_id=1, replica_groups=mesh['expert'=64,'mp'=2] {'mp'}, use_global_device_ids=true, to_apply=%region_0.1 | all-reduce | flops 512 | bytes 4096 | tf_op jit(solution)/shard_map/psum | solution.py:739
  224.7 1.7 add_convert_fusion
  226.5 1.5 copy-done.2
  228.0 3.1 %token_grads.1 = bf16[64,1792]{1,0:T(8,128)(2,1)} custom-call(bf16[128,1536]{1,0:T(8,128)(2,1)} %select_rows.1.sel_ref, bf16[1536,896]{1,0:T(8,128)(2,1)} %bitcast.27), custom_call_target="tpu_custom_call" | custom-call | flops 1 | bytes 1 | tf_op jit(solution)/shard_map/token_grads/pallas_call | solution.py:653
  (52 shorter events, 12.5 us)
Async XLA Ops:
  4.9 11.2 %copy-start.3 = (bf16[64,1792]{1,0:T(8,128)(2,1)S(1)}, bf16[64,1792]{1,0:T(8,128)(2,1)}, u32[]{:S(2)}) copy-start(bf16[64,1792]{1,0:T(8,128)(2,1)} %cot0.1) | copy-start | bytes 688132
  4.9 16.2 %copy-start.8 = (s32[64,8]{0,1:T(8,128)S(1)}, s32[64,8]{0,1:T(8,128)}, u32[]{:S(2)}) copy-start(s32[64,8]{0,1:T(8,128)} %param.9) | copy-start | bytes 6148
  4.9 16.2 %copy-start.10 = (f32[64,8]{0,1:T(8,128)S(1)}, f32[64,8]{0,1:T(8,128)}, u32[]{:S(2)}) copy-start(f32[64,8]{0,1:T(8,128)} %param.10) | copy-start | bytes 6148
  4.9 63.2 %all-to-all-start = ((bf16[64,24,896]{2,1,0:T(8,128)(2,1)}), bf16[64,24,896]{2,1,0:T(8,128)(2,1)}, u32[]{:S(2)}, u32[]{:S(2)}) async-start(bf16[64,24,896]{2,1,0:T(8,128)(2,1)} %bitcast.28), calls=%async_computation | async-start | bytes 5505024 | tf_op jit(solution)/shard_map/all_to_all | solution.py:671
  16.1 46.6 %collective-permute-start.3 = (bf16[64,1792]{1,0:T(8,128)(2,1)S(1)}, bf16[64,1792]{1,0:T(8,128)(2,1)S(1)}, u32[]{:S(2)}, u32[]{:S(2)}) collective-permute-start(bf16[64,1792]{1,0:T(8,128)(2,1)S(1)} %copy-done.3), channel_id=1, source_target_pairs={{0,32},{2,34},{4,36},{6,38},{8,40},{10,42},{12,44},{14,46},{16,48}... | collective-permute-start | bytes 688136 | tf_op jit(solution)/shard_map/ppermute | solution.py:688
  17.4 45.2 %collective-permute-start.4 = (bf16[64,1792]{1,0:T(8,128)(2,1)S(1)}, bf16[64,1792]{1,0:T(8,128)(2,1)S(1)}, u32[]{:S(2)}, u32[]{:S(2)}) collective-permute-start(bf16[64,1792]{1,0:T(8,128)(2,1)S(1)} %copy-done.3), channel_id=1, source_target_pairs={{0,64},{2,66},{4,68},{6,70},{8,72},{10,74},{12,76},{14,78},{16,80}... | collective-permute-start | bytes 688136 | tf_op jit(solution)/shard_map/ppermute | solution.py:688
  20.0 42.6 %collective-permute-start.5 = (bf16[64,1792]{1,0:T(8,128)(2,1)S(1)}, bf16[64,1792]{1,0:T(8,128)(2,1)S(1)}, u32[]{:S(2)}, u32[]{:S(2)}) collective-permute-start(bf16[64,1792]{1,0:T(8,128)(2,1)S(1)} %copy-done.3), channel_id=1, source_target_pairs={{0,96},{2,98},{4,100},{6,102},{8,104},{10,106},{12,108},{14,110},{... | collective-permute-start | bytes 688136 | tf_op jit(solution)/shard_map/ppermute | solution.py:688
  21.1 37.1 %collective-permute-start.2 = (f32[16,64]{1,0:T(8,128)S(1)}, f32[16,64]{1,0:T(8,128)S(1)}, u32[]{:S(2)}, u32[]{:S(2)}) collective-permute-start(f32[16,64]{1,0:T(8,128)S(1)} %pad_maximum_fusion.1), channel_id=1, source_target_pairs={{0,96},{2,98},{4,100},{6,102},{8,104},{10,106},{12,108},{14,110},{... | collective-permute-start | bytes 12296 | tf_op jit(solution)/shard_map/ppermute | solution.py:688
  21.2 38.4 %collective-permute-start.1 = (f32[16,64]{1,0:T(8,128)S(1)}, f32[16,64]{1,0:T(8,128)S(1)}, u32[]{:S(2)}, u32[]{:S(2)}) collective-permute-start(f32[16,64]{1,0:T(8,128)S(1)} %pad_maximum_fusion.1), channel_id=1, source_target_pairs={{0,64},{2,66},{4,68},{6,70},{8,72},{10,74},{12,76},{14,78},{16,80}... | collective-permute-start | bytes 12296 | tf_op jit(solution)/shard_map/ppermute | solution.py:688
  58.2 3.7 %collective-permute-start = (f32[16,64]{1,0:T(8,128)S(1)}, f32[16,64]{1,0:T(8,128)S(1)}, u32[]{:S(2)}, u32[]{:S(2)}) collective-permute-start(f32[16,64]{1,0:T(8,128)S(1)} %pad_maximum_fusion.1), channel_id=1, source_target_pairs={{0,32},{2,34},{4,36},{6,38},{8,40},{10,42},{12,44},{14,46},{16,48}... | collective-permute-start | bytes 12296 | tf_op jit(solution)/shard_map/ppermute | solution.py:688
  62.6 0.8 copy-start.5
  62.7 0.8 copy-start.6
  68.0 8.9 %collective-permute-start.6 = (bf16[1536,896]{1,0:T(8,128)(2,1)}, bf16[1536,896]{1,0:T(8,128)(2,1)}, u32[]{:S(2)}, u32[]{:S(2)}) collective-permute-start(bf16[1536,896]{1,0:T(8,128)(2,1)} %bitcast.4), channel_id=1, source_target_pairs={{0,1},{1,0},{2,3},{3,2},{4,5},{5,4},{6,7},{7,6},{8,9},{9,8},{10,11... | collective-permute-start | bytes 8257544 | tf_op jit(solution)/shard_map/ppermute | solution.py:694
  70.0 44.6 %all-to-all-start.1 = ((bf16[16,96,896]{2,1,0:T(8,128)(2,1)}), bf16[16,96,896]{2,1,0:T(8,128)(2,1)S(1)}, u32[]{:S(2)}, u32[]{:S(2)}) async-start(bf16[16,96,896]{2,1,0:T(8,128)(2,1)} %send_scaled.1), calls=%async_computation.1 | async-start | bytes 5505024 | tf_op jit(solution)/shard_map/all_to_all | solution.py:680
  100.7 3.6 %collective-permute-start.7 = (bf16[16,48,896]{2,1,0:T(8,128)(2,1)}, bf16[16,48,896]{2,1,0:T(8,128)(2,1)S(1)}, u32[]{:S(2)}, u32[]{:S(2)}) collective-permute-start(bf16[16,48,896]{2,1,0:T(8,128)(2,1)} %get-tuple-element.35), channel_id=1, source_target_pairs={{0,1},{1,0},{2,3},{3,2},{4,5},{5,4},{6,7},{7,6},{8,9},{9,8},{10,11... | collective-permute-start | bytes 4128776 | tf_op jit(solution)/shard_map/ppermute | solution.py:694
  101.4 4.9 %collective-permute-start.8 = (bf16[16,48,896]{2,1,0:T(8,128)(2,1)}, bf16[16,48,896]{2,1,0:T(8,128)(2,1)S(1)}, u32[]{:S(2)}, u32[]{:S(2)}) collective-permute-start(bf16[16,48,896]{2,1,0:T(8,128)(2,1)} %get-tuple-element.36), channel_id=1, source_target_pairs={{0,1},{1,0},{2,3},{3,2},{4,5},{5,4},{6,7},{7,6},{8,9},{9,8},{10,11... | collective-permute-start | bytes 4128776 | tf_op jit(solution)/shard_map/ppermute | solution.py:694
  114.5 1.6 copy-start.1
  114.5 9.8 %collective-permute-start.9 = (bf16[16,96,896]{2,1,0:T(8,128)(2,1)S(1)}, bf16[16,96,896]{2,1,0:T(8,128)(2,1)}, u32[]{:S(2)}, u32[]{:S(2)}) collective-permute-start(bf16[16,96,896]{2,1,0:T(8,128)(2,1)S(1)} %all-to-all-done.1.own0.own1.own_ref), channel_id=1, source_target_pairs={{0,1},{1,0},{2,3},{3,2},{4,5},{5,4},{6,7},{7,6},{8,9},{9,8},{10,11... | collective-permute-start | bytes 8257544 | tf_op jit(solution)/shard_map/ppermute | solution.py:694
  116.1 40.7 %all-to-all-start.2 = ((bf16[16,96,896]{2,1,0:T(8,128)(2,1)}), bf16[16,96,896]{2,1,0:T(8,128)(2,1)}, u32[]{:S(2)}, u32[]{:S(2)}) async-start(bf16[16,96,896]{2,1,0:T(8,128)(2,1)} %add_halves.1), calls=%async_computation.2 | async-start | bytes 5505024 | tf_op jit(solution)/shard_map/all_to_all | solution.py:680
  124.3 26.8 %copy-start = (s32[2]{0:T(128)S(1)}, s32[2]{0:T(128)}, u32[]{:S(2)}) copy-start(s32[2]{0:T(128)} %pad_add_fusion.mine_ref.plane_ref) | copy-start | bytes 28
  144.4 4.7 %collective-permute-start.10 = (bf16[768,896]{1,0:T(8,128)(2,1)}, bf16[768,896]{1,0:T(8,128)(2,1)S(1)}, u32[]{:S(2)}, u32[]{:S(2)}) collective-permute-start(bf16[768,896]{1,0:T(8,128)(2,1)} %get-tuple-element.42), channel_id=1, source_target_pairs={{0,1},{1,0},{2,3},{3,2},{4,5},{5,4},{6,7},{7,6},{8,9},{9,8},{10,11... | collective-permute-start | bytes 4128776 | tf_op jit(solution)/shard_map/ppermute | solution.py:694
  146.2 4.9 %collective-permute-start.11 = (bf16[768,896]{1,0:T(8,128)(2,1)}, bf16[768,896]{1,0:T(8,128)(2,1)S(1)}, u32[]{:S(2)}, u32[]{:S(2)}) collective-permute-start(bf16[768,896]{1,0:T(8,128)(2,1)} %get-tuple-element.43), channel_id=1, source_target_pairs={{0,1},{1,0},{2,3},{3,2},{4,5},{5,4},{6,7},{7,6},{8,9},{9,8},{10,11... | collective-permute-start | bytes 4128776 | tf_op jit(solution)/shard_map/ppermute | solution.py:694
  156.8 69.7 %all-to-all-start.3 = ((bf16[64,24,896]{2,1,0:T(8,128)(2,1)}), bf16[64,24,896]{2,1,0:T(8,128)(2,1)S(1)}, u32[]{:S(2)}, u32[]{:S(2)}) async-start(bf16[64,24,896]{2,1,0:T(8,128)(2,1)} %bitcast.13), calls=%async_computation.3 | async-start | bytes 5505024 | tf_op jit(solution)/shard_map/all_to_all | solution.py:671
  173.2 6.3 %collective-permute-start.17 = (f32[8,64]{1,0:T(8,128)S(1)}, f32[8,64]{1,0:T(8,128)S(1)}, u32[]{:S(2)}, u32[]{:S(2)}) collective-permute-start(f32[8,64]{1,0:T(8,128)S(1)} %get-tuple-element.59), channel_id=1, source_target_pairs={{0,32},{2,34},{4,36},{6,38},{8,40},{10,42},{12,44},{14,46},{16,48}... | collective-permute-start | bytes 6152 | tf_op jit(solution)/shard_map/ppermute | solution.py:688
  174.4 50.3 %collective-permute-start.14 = (bf16[64,1792]{1,0:T(8,128)(2,1)}, bf16[64,1792]{1,0:T(8,128)(2,1)S(1)}, u32[]{:S(2)}, u32[]{:S(2)}) collective-permute-start(bf16[64,1792]{1,0:T(8,128)(2,1)} %get-tuple-element.48), channel_id=1, source_target_pairs={{0,32},{2,34},{4,36},{6,38},{8,40},{10,42},{12,44},{14,46},{16,48}... | collective-permute-start | bytes 688136 | tf_op jit(solution)/shard_map/ppermute | solution.py:688
  175.7 49.0 %collective-permute-start.13 = (bf16[64,1792]{1,0:T(8,128)(2,1)}, bf16[64,1792]{1,0:T(8,128)(2,1)S(1)}, u32[]{:S(2)}, u32[]{:S(2)}) collective-permute-start(bf16[64,1792]{1,0:T(8,128)(2,1)} %get-tuple-element.47), channel_id=1, source_target_pairs={{0,64},{2,66},{4,68},{6,70},{8,72},{10,74},{12,76},{14,78},{16,80}... | collective-permute-start | bytes 688136 | tf_op jit(solution)/shard_map/ppermute | solution.py:688
  177.1 47.7 %collective-permute-start.12 = (bf16[64,1792]{1,0:T(8,128)(2,1)}, bf16[64,1792]{1,0:T(8,128)(2,1)}, u32[]{:S(2)}, u32[]{:S(2)}) collective-permute-start(bf16[64,1792]{1,0:T(8,128)(2,1)} %get-tuple-element.46), channel_id=1, source_target_pairs={{0,96},{2,98},{4,100},{6,102},{8,104},{10,106},{12,108},{14,110},{... | collective-permute-start | bytes 688136 | tf_op jit(solution)/shard_map/ppermute | solution.py:688
  179.1 31.5 %collective-permute-start.16 = (f32[8,64]{1,0:T(8,128)S(1)}, f32[8,64]{1,0:T(8,128)S(1)}, u32[]{:S(2)}, u32[]{:S(2)}) collective-permute-start(f32[8,64]{1,0:T(8,128)S(1)} %get-tuple-element.60), channel_id=1, source_target_pairs={{0,64},{2,66},{4,68},{6,70},{8,72},{10,74},{12,76},{14,78},{16,80}... | collective-permute-start | bytes 6152 | tf_op jit(solution)/shard_map/ppermute | solution.py:688
  179.5 31.2 %collective-permute-start.15 = (f32[8,64]{1,0:T(8,128)S(1)}, f32[8,64]{1,0:T(8,128)S(1)}, u32[]{:S(2)}, u32[]{:S(2)}) collective-permute-start(f32[8,64]{1,0:T(8,128)S(1)} %get-tuple-element.58), channel_id=1, source_target_pairs={{0,96},{2,98},{4,100},{6,102},{8,104},{10,106},{12,108},{14,110},{... | collective-permute-start | bytes 6152 | tf_op jit(solution)/shard_map/ppermute | solution.py:688
  183.8 26.8 %copy-start.9 = (f32[8,256]{1,0:T(8,128)S(1)}, f32[8,256]{1,0:T(8,128)}, u32[]{:S(2)}) copy-start(f32[8,256]{1,0:T(8,128)} %get-tuple-element.50) | copy-start | bytes 24580
  183.8 40.9 %copy-start.7 = (bf16[64,1792]{1,0:T(8,128)(2,1)S(1)}, bf16[64,1792]{1,0:T(8,128)(2,1)}, u32[]{:S(2)}) copy-start(bf16[64,1792]{1,0:T(8,128)(2,1)} %get-tuple-element.45) | copy-start | bytes 688132
  226.5 1.5 copy-start.2
  (1 other events, 0.7 us)

commit v5 on v3

--- a/solution.py
+++ b/solution.py
@@ -120,38 +120,40 @@
 def put_in_order(own_ref, other_ref, mine, step, held, out_ref):
     order = ordering()
     n = SUB * ROWS
+    quarter = own_ref.shape[1]
     for which, ref in ((mine, own_ref), (1 - mine, other_ref)):
-        for b in range(GROUP // SUB):
+        for b in range(own_ref.shape[0] // n):
             both = dot(order, ref[b * n : (b + 1) * n, :]).astype(BF16)
-            at = pl.multiple_of(step * (GROUP * SLOTS) + b * (n // 2), n // 2)
+            row = pl.multiple_of((step * (own_ref.shape[0] // n) + b) * (n // 2), n // 2)
             for h in range(2):
                 part = both[h * (n // 2) : (h + 1) * (n // 2)]
-                held[2 * which + h, pl.ds(at, n // 2), :] = part
-                out_ref[2 * which + h, b * (n // 2) : (b + 1) * (n // 2), :] = part
-
-
-def weight_copies(gate_hbm, up_hbm, down_hbm, gate_w, up_w, down_w, sems):
-    quarter = down_w.shape[2]
-    downs = [
-        pltpu.make_async_copy(
-            down_hbm.at[:, q * quarter : (q + 1) * quarter], down_w.at[q], sems.at[2 + q]
-        )
-        for q in range(4)
+                lane = pl.multiple_of((2 * which + h) * quarter, quarter)
+                held[pl.ds(row, n // 2), pl.ds(lane, quarter)] = part
+                out_ref[b * (n // 2) : (b + 1) * (n // 2), pl.ds(lane, quarter)] = part
+
+
+def weight_copies(gate_hbm, up_hbm, down_hbm, pair_w, down_w, sems):
+    ff = down_w.shape[0]
+    ins = [
+        pltpu.make_async_copy(gate_hbm, pair_w.at[:, :ff], sems.at[0]),
+        pltpu.make_async_copy(up_hbm, pair_w.at[:, ff:], sems.at[1]),
     ]
-    gates = pltpu.make_async_copy(gate_hbm, gate_w, sems.at[0])
-    ups = pltpu.make_async_copy(up_hbm, up_w, sems.at[1])
-    return [gates, ups], downs
+    return ins, [pltpu.make_async_copy(down_hbm, down_w, sems.at[2])]
+
+
+def features(mine, half):
+    return pl.ds(pl.multiple_of(mine * half, half), half)
 
 
 def forward_kernel(
-    steps, ff_steps, mine_ref, own_ref, other_ref, gate_hbm, up_hbm, down_hbm,
-    gate_ref, up_ref, hidden_ref, rows_ref, far0, far1, near_ref,
-    held, hidden_all, gate_w, up_w, down_w, sems,
+    steps, mine_ref, own_ref, other_ref, gate_hbm, up_hbm, down_hbm,
+    gate_ref, up_ref, hidden_ref, rows_ref, far0, far1, near_ref, held, pair_w, down_w, sems,
 ):
     i = pl.program_id(0)
     mine = mine_ref[0]
     quarter = own_ref.shape[1]
-    ins, downs = weight_copies(gate_hbm, up_hbm, down_hbm, gate_w, up_w, down_w, sems)
+    ff = down_w.shape[0]
+    ins, downs = weight_copies(gate_hbm, up_hbm, down_hbm, pair_w, down_w, sems)
 
     @pl.when(i == 0)
     def _():
@@ -162,79 +164,62 @@
     def _():
         put_in_order(own_ref, other_ref, mine, i, held, rows_ref)
 
-    for f in range(ff_steps):
-        @pl.when(i == steps + f)
-        def _():
-            if f == 0:
-                for copy in ins:
-                    copy.wait()
-            wide = gate_ref.shape[1]
-            at = slice(f * wide, (f + 1) * wide)
-            gate = sum(dot(held[q], gate_w[q * quarter : (q + 1) * quarter, at]) for q in range(4))
-            up = sum(dot(held[q], up_w[q * quarter : (q + 1) * quarter, at]) for q in range(4))
-            gate_ref[...] = gate
-            up_ref[...] = up
-            hidden = (gate * jax.nn.sigmoid(gate) * up).astype(BF16)
-            hidden_ref[...] = hidden
-            hidden_all[:, at] = hidden
-
-    for h, far_ref in enumerate((far0, far1)):
-        @pl.when(i == steps + ff_steps + h)
-        def _():
-            if h == 0:
-                for copy in downs:
-                    copy.wait()
-            far_ref[...] = dot(hidden_all[...], down_w[2 * (1 - mine) + h]).astype(BF16)
-
-    for h in range(2):
-        @pl.when(i == steps + ff_steps + 2 + h)
-        def _():
-            near_ref[...] = dot(hidden_all[...], down_w[2 * mine + h]).astype(BF16)
-
-
-def expert_specs(raw, quarter, ff, model):
-    steps, ff_steps, rows = raw // TILE, 2, raw // 2
-    wide = ff // ff_steps
-    last = steps + ff_steps
-    source = pl.BlockSpec((TILE, quarter), lambda i, m: (jnp.minimum(i, steps - 1), 0))
-    ffs = pl.BlockSpec((rows, wide), lambda i, m: (0, jnp.clip(i - steps, 0, ff_steps - 1)))
-    ordered = pl.BlockSpec(
-        (4, GROUP * SLOTS, quarter), lambda i, m: (0, jnp.minimum(i, steps - 1), 0)
-    )
-    far = pl.BlockSpec((rows, quarter), lambda i, m: (0, 0))
-    near = pl.BlockSpec((rows, quarter), lambda i, m: (0, jnp.clip(i - last - 2, 0, 1)))
-    held = [
-        pltpu.VMEM((model, ff), BF16),
-        pltpu.VMEM((model, ff), BF16),
-        pltpu.VMEM((4, ff, quarter), BF16),
-        pltpu.SemaphoreType.DMA((6,)),
-    ]
-    return steps, ff_steps, rows, source, ffs, ordered, far, near, held
+    @pl.when(i == steps)
+    def _():
+        for copy in ins:
+            copy.wait()
+        both = dot(held[...], pair_w[...])
+        gate, up = both[:, :ff], both[:, ff:]
+        gate_ref[...] = gate
+        up_ref[...] = up
+        hidden_ref[...] = (gate * jax.nn.sigmoid(gate) * up).astype(BF16)
+
+    @pl.when(i == steps + 1)
+    def _():
+        for copy in downs:
+            copy.wait()
+        part = dot(hidden_ref[...], down_w[:, features(1 - mine, 2 * quarter)]).astype(BF16)
+        far0[...] = part[:, :quarter]
+        far1[...] = part[:, quarter:]
+
+    @pl.when(i == steps + 2)
+    def _():
+        near_ref[...] = dot(hidden_ref[...], down_w[:, features(mine, 2 * quarter)]).astype(BF16)
+
+
+A_TILE = 2 * TILE
 
 
 def forward(mine, own, other, gate_w, up_w, down_w):
     raw, quarter = own.shape
     model, ff = gate_w.shape
-    steps, ff_steps, rows, source, ffs, ordered, far, near, held = expert_specs(
-        raw, quarter, ff, model
-    )
+    rows, steps = raw // 2, raw // A_TILE
+    source = pl.BlockSpec((A_TILE, quarter), lambda i, m: (jnp.minimum(i, steps - 1), 0))
+    ordered = pl.BlockSpec((A_TILE // 2, model), lambda i, m: (jnp.minimum(i, steps - 1), 0))
+    whole = lambda width: pl.BlockSpec((rows, width), lambda i, m: (0, 0))
     hbm = pl.BlockSpec(memory_space=pl.ANY)
     return pl.pallas_call(
-        functools.partial(forward_kernel, steps, ff_steps),
+        functools.partial(forward_kernel, steps),
         grid_spec=pltpu.PrefetchScalarGridSpec(
             num_scalar_prefetch=1,
-            grid=(steps + ff_steps + 4,),
+            grid=(steps + 3,),
             in_specs=[source, source, hbm, hbm, hbm],
-            out_specs=[ffs, ffs, ffs, ordered, far, far, near],
+            out_specs=[
+                whole(ff), whole(ff), whole(ff), ordered, whole(quarter), whole(quarter),
+                whole(2 * quarter),
+            ],
             scratch_shapes=[
-                pltpu.VMEM((4, rows, quarter), BF16), pltpu.VMEM((rows, ff), BF16), *held
+                pltpu.VMEM((rows, model), BF16),
+                pltpu.VMEM((model, 2 * ff), BF16),
+                pltpu.VMEM((ff, model), BF16),
+                pltpu.SemaphoreType.DMA((3,)),
             ],
         ),
         out_shape=[
             jax.ShapeDtypeStruct((rows, ff), F32),
             jax.ShapeDtypeStruct((rows, ff), F32),
             jax.ShapeDtypeStruct((rows, ff), BF16),
-            jax.ShapeDtypeStruct((4, rows, quarter), BF16),
+            jax.ShapeDtypeStruct((rows, model), BF16),
             jax.ShapeDtypeStruct((rows, quarter), BF16),
             jax.ShapeDtypeStruct((rows, quarter), BF16),
             jax.ShapeDtypeStruct((rows, 2 * quarter), BF16),
@@ -246,14 +231,14 @@
 
 
 def backward_kernel(
-    steps, ff_steps, mine_ref, own_ref, other_ref, gate_hbm, up_hbm, down_hbm, gate_ref, up_ref,
-    gate_grad_ref, up_grad_ref, rows_ref, far0, far1, near_ref,
-    held, gate_grads, up_grads, gate_w, up_w, down_w, sems,
+    steps, mine_ref, own_ref, other_ref, gate_hbm, up_hbm, down_hbm, gate_ref, up_ref,
+    grads_ref, rows_ref, far0, far1, near_ref, held, pair_w, down_w, sems,
 ):
     i = pl.program_id(0)
     mine = mine_ref[0]
     quarter = own_ref.shape[1]
-    ins, downs = weight_copies(gate_hbm, up_hbm, down_hbm, gate_w, up_w, down_w, sems)
+    ff = down_w.shape[0]
+    ins, downs = weight_copies(gate_hbm, up_hbm, down_hbm, pair_w, down_w, sems)
 
     @pl.when(i == 0)
     def _():
@@ -264,69 +249,60 @@
     def _():
         put_in_order(own_ref, other_ref, mine, i, held, rows_ref)
 
-    for f in range(ff_steps):
-        @pl.when(i == steps + f)
-        def _():
-            if f == 0:
-                for copy in downs:
-                    copy.wait()
-            wide = gate_ref.shape[1]
-            at = slice(f * wide, (f + 1) * wide)
-            hidden_grad = sum(dot(held[q], down_w[q, at, :], NT) for q in range(4))
-            gate, up = gate_ref[...], up_ref[...]
-            logistic = jax.nn.sigmoid(gate)
-            gate_grad = (hidden_grad * up * logistic * (1.0 + gate * (1.0 - logistic))).astype(BF16)
-            up_grad = (hidden_grad * (gate * logistic)).astype(BF16)
-            gate_grad_ref[...] = gate_grad
-            up_grad_ref[...] = up_grad
-            gate_grads[:, at] = gate_grad
-            up_grads[:, at] = up_grad
-
-    def input_grads(q):
-        at = pl.ds(pl.multiple_of(q * quarter, quarter), quarter)
-        return (
-            dot(gate_grads[...], gate_w[at, :], NT) + dot(up_grads[...], up_w[at, :], NT)
+    @pl.when(i == steps)
+    def _():
+        for copy in downs:
+            copy.wait()
+        hidden_grad = dot(held[...], down_w[...], NT)
+        gate, up = gate_ref[...], up_ref[...]
+        logistic = jax.nn.sigmoid(gate)
+        grads_ref[:, :ff] = (
+            hidden_grad * up * logistic * (1.0 + gate * (1.0 - logistic))
         ).astype(BF16)
-
-    for h, far_ref in enumerate((far0, far1)):
-        @pl.when(i == steps + ff_steps + h)
-        def _():
-            if h == 0:
-                for copy in ins:
-                    copy.wait()
-            far_ref[...] = input_grads(2 * (1 - mine) + h)
-
-    for h in range(2):
-        @pl.when(i == steps + ff_steps + 2 + h)
-        def _():
-            near_ref[...] = input_grads(2 * mine + h)
+        grads_ref[:, ff:] = (hidden_grad * (gate * logistic)).astype(BF16)
+
+    @pl.when(i == steps + 1)
+    def _():
+        for copy in ins:
+            copy.wait()
+        part = dot(grads_ref[...], pair_w[features(1 - mine, 2 * quarter), :], NT).astype(BF16)
+        far0[...] = part[:, :quarter]
+        far1[...] = part[:, quarter:]
+
+    @pl.when(i == steps + 2)
+    def _():
+        near_ref[...] = dot(
+            grads_ref[...], pair_w[features(mine, 2 * quarter), :], NT
+        ).astype(BF16)
 
 
 def backward(mine, own, other, gate_w, up_w, down_w, gate_pre, up_pre):
     raw, quarter = own.shape
     model, ff = gate_w.shape
-    steps, ff_steps, rows, source, ffs, ordered, far, near, held = expert_specs(
-        raw, quarter, ff, model
-    )
+    rows, steps = raw // 2, raw // A_TILE
+    source = pl.BlockSpec((A_TILE, quarter), lambda i, m: (jnp.minimum(i, steps - 1), 0))
+    ordered = pl.BlockSpec((A_TILE // 2, model), lambda i, m: (jnp.minimum(i, steps - 1), 0))
+    whole = lambda width: pl.BlockSpec((rows, width), lambda i, m: (0, 0))
     hbm = pl.BlockSpec(memory_space=pl.ANY)
     return pl.pallas_call(
-        functools.partial(backward_kernel, steps, ff_steps),
+        functools.partial(backward_kernel, steps),
         grid_spec=pltpu.PrefetchScalarGridSpec(
             num_scalar_prefetch=1,
-            grid=(steps + ff_steps + 4,),
-            in_specs=[source, source, hbm, hbm, hbm, ffs, ffs],
-            out_specs=[ffs, ffs, ordered, far, far, near],
+            grid=(steps + 3,),
+            in_specs=[source, source, hbm, hbm, hbm, whole(ff), whole(ff)],
+            out_specs=[
+                whole(2 * ff), ordered, whole(quarter), whole(quarter), whole(2 * quarter)
+            ],
             scratch_shapes=[
-                pltpu.VMEM((4, rows, quarter), BF16),
-                pltpu.VMEM((rows, ff), BF16),
-                pltpu.VMEM((rows, ff), BF16),
-                *held,
+                pltpu.VMEM((rows, model), BF16),
+                pltpu.VMEM((model, 2 * ff), BF16),
+                pltpu.VMEM((ff, model), BF16),
+                pltpu.SemaphoreType.DMA((3,)),
             ],
         ),
         out_shape=[
-            jax.ShapeDtypeStruct((rows, ff), BF16),
-            jax.ShapeDtypeStruct((rows, ff), BF16),
-            jax.ShapeDtypeStruct((4, rows, quarter), BF16),
+            jax.ShapeDtypeStruct((rows, 2 * ff), BF16),
+            jax.ShapeDtypeStruct((rows, model), BF16),
             jax.ShapeDtypeStruct((rows, quarter), BF16),
             jax.ShapeDtypeStruct((rows, quarter), BF16),
             jax.ShapeDtypeStruct((rows, 2 * quarter), BF16),
@@ -375,36 +351,38 @@
     )(near, *fars)
 
 
-def weights_kernel(rows_ref, scaled_ref, hidden_ref, gate_grad_ref, up_grad_ref, gate_w, up_w, down_w):
-    rows = rows_ref[0]
-    gate_w[...] = dot(rows, gate_grad_ref[...], TN).astype(BF16)
-    up_w[...] = dot(rows, up_grad_ref[...], TN).astype(BF16)
-    down_w[...] = dot(hidden_ref[...], scaled_ref[0], TN).astype(BF16)
-
-
-def weight_grads(token_rows, scaled_rows, hidden, gate_grad, up_grad):
-    quarters, rows, quarter = token_rows.shape
+def weights_kernel(rows_ref, scaled_ref, hidden_ref, grads_ref, gate_w, up_w, down_w):
+    ff = hidden_ref.shape[1]
+    both = dot(rows_ref[...], grads_ref[...], TN)
+    gate_w[...] = both[:, :ff].astype(BF16)
+    up_w[...] = both[:, ff:].astype(BF16)
+    down_w[...] = dot(hidden_ref[...], scaled_ref[...], TN).astype(BF16)
+
+
+def weight_grads(token_rows, scaled_rows, hidden, grads):
+    rows, model = token_rows.shape
     ff = hidden.shape[1]
-    whole = pl.BlockSpec((rows, ff), lambda i: (0, 0))
-    part = pl.BlockSpec((1, rows, quarter), lambda i: (i, 0, 0))
+    step = 512
+    whole = lambda width: pl.BlockSpec((rows, width), lambda i: (0, 0))
+    part = pl.BlockSpec((rows, step), lambda i: (0, i))
     return pl.pallas_call(
         weights_kernel,
-        grid=(quarters,),
-        in_specs=[part, part, whole, whole, whole],
+        grid=(model // step,),
+        in_specs=[part, part, whole(ff), whole(2 * ff)],
         out_specs=[
-            pl.BlockSpec((quarter, ff), lambda i: (i, 0)),
-            pl.BlockSpec((quarter, ff), lambda i: (i, 0)),
-            pl.BlockSpec((ff, quarter), lambda i: (0, i)),
+            pl.BlockSpec((step, ff), lambda i: (i, 0)),
+            pl.BlockSpec((step, ff), lambda i: (i, 0)),
+            pl.BlockSpec((ff, step), lambda i: (0, i)),
         ],
         out_shape=[
-            jax.ShapeDtypeStruct((quarters * quarter, ff), BF16),
-            jax.ShapeDtypeStruct((quarters * quarter, ff), BF16),
-            jax.ShapeDtypeStruct((ff, quarters * quarter), BF16),
+            jax.ShapeDtypeStruct((model, ff), BF16),
+            jax.ShapeDtypeStruct((model, ff), BF16),
+            jax.ShapeDtypeStruct((ff, model), BF16),
         ],
         compiler_params=params(60),
         cost_estimate=cost(),
         name="weight_grads",
-    )(token_rows, scaled_rows, hidden, gate_grad, up_grad)
+    )(token_rows, scaled_rows, hidden, grads)
 
 
 def outputs_kernel(route_ref, probs_ref, cot_ref, back_ref, out_ref, grad_ref, sel_ref, total):
@@ -536,7 +514,7 @@
     got_scaled, send_out = lax.optimization_barrier((got_scaled, send_out))
     back_out = exchange(send_out)
 
-    gate_grad, up_grad, scaled_rows, far0, far1, in_near = backward(
+    grads, scaled_rows, far0, far1, in_near = backward(
         mine, got_scaled, swap(got_scaled), gate_w, up_w, down_w, gate_pre, up_pre
     )
     send_in = pack(in_near, [swap(far0), swap(far1)])
@@ -544,7 +522,7 @@
     back_in = exchange(send_in)
 
     grad_w_gate, grad_w_up, grad_w_down = weight_grads(
-        token_rows, scaled_rows, hidden, gate_grad, up_grad
+        token_rows, scaled_rows, hidden, grads
     )
     layer_out, grad_part, select = token_outputs(route_t, probs_t, cotangent, back_out)
     grad_probs = lax.psum(grad_part, "mp").T

time: 192 us -> 190 us (0.990)
  Pallas kernels: 87.2 us -> 79.5 us
  waiting for transfers between devices: 59.4 us -> 65.1 us
  starting transfers between devices: 38.1 us -> 35.7 us
    pallas_call x3, Pallas kernels: 60 us -> 52.3 us  [the longest x1 19.8 us: forward(): pl.pallas_call(functools.partial(forward_kernel, steps), grid_spec=pltpu....]
    all_to_all x4, waiting for transfers between devices: 49.7 us -> 55.4 us  [exchange(): lax.all_to_all(x.reshape(experts, ROWS, -1), 'expert', split_axis=0, conc...]
    all_to_all x4, starting transfers between devices: 32.2 us -> 29.9 us  [exchange(): lax.all_to_all(x.reshape(experts, ROWS, -1), 'expert', split_axis=0, conc...]
  transfers between devices with their start and end apart: 10 -> 10, of which waited for: 8 -> 8; matrix products, arithmetic and copies ran while one was open for 0% -> 0% of each run, Pallas kernels for 42% -> 39%
where the time goes in v5:
time: 190 us; the launch traced here: 187 us
  Pallas kernels  79.5 us (42%)
  waiting for transfers between devices  65.1 us (34%)
  starting transfers between devices  35.7 us (19%)
  blocking collectives  4.26 us (2%)
  local copies, waits for them, and re-layouts  1.92 us (1%)
    all_to_all x4, waiting for transfers between devices, exchange(): lax.all_to_all(x.reshape(experts, ROWS, -1), 'expert', split_axis=0, conc...  55.4 us
    all_to_all x4, starting transfers between devices, exchange(): lax.all_to_all(x.reshape(experts, ROWS, -1), 'expert', split_axis=0, conc...  29.9 us
    pallas_call x1, Pallas kernels, forward(): pl.pallas_call(functools.partial(forward_kernel, steps), grid_spec=pltpu....  19.8 us
    pallas_call x1, Pallas kernels, backward(): pl.pallas_call(functools.partial(backward_kernel, steps), grid_spec=pltpu...  18.8 us
    pallas_call x1, Pallas kernels, weight_grads(): pl.pallas_call(weights_kernel, grid=(model // step,), in_specs=[part, par...  13.7 us
    ppermute x6, waiting for transfers between devices, swap(): return lax.ppermute(x, 'mp', [(0, 1), (1, 0)])  9.69 us
    pallas_call x2, Pallas kernels, pack(): pl.pallas_call(pack_kernel, grid=(rows // step_rows,), in_specs=[pl.Block...  9.52 us
    pallas_call x2, Pallas kernels, send_rows(): pl.pallas_call(functools.partial(send_kernel, scaled), grid=(experts // G...  8.52 us
  transfers between devices with their start and end apart: 10, of which 8 were waited for; matrix products, arithmetic and copies ran while one was open for 0% of the time, Pallas kernels for 39%

profile of v5, /device:TPU:7, one launch (start us, length us, event | category | flops | bytes accessed | tf_op | source)
XLA Modules:
  0.0 187.2 jit_solution(11534503562587885606)
XLA Ops:
  0.6 4.3 %send_tokens.1 = bf16[1536,896]{1,0:T(8,128)(2,1)} custom-call(s32[8,64]{1,0:T(8,128)} %bitcast.29, f32[8,64]{1,0:T(8,128)} %bitcast.32, bf16[64,1792]{1,0:T(8,128)(2,1)} %rows_ref.2), custom_call_target="tpu_custom_call" | custom-call | flops 1 | bytes 1 | tf_op jit(solution)/shard_map/send_tokens/pallas_call | solution.py:91
  4.9 10.9 %all-to-all-start = ((bf16[64,24,896]{2,1,0:T(8,128)(2,1)}), bf16[64,24,896]{2,1,0:T(8,128)(2,1)S(1)}, u32[]{:S(2)}, u32[]{:S(2)}) async-start(bf16[64,24,896]{2,1,0:T(8,128)(2,1)} %bitcast.28), calls=%async_computation | async-start | bytes 5505024 | tf_op jit(solution)/shard_map/all_to_all | solution.py:489
  15.8 4.3 %send_scaled.1 = bf16[1536,896]{1,0:T(8,128)(2,1)} custom-call(s32[8,64]{1,0:T(8,128)} %bitcast.30, f32[8,64]{1,0:T(8,128)} %bitcast.33, bf16[64,1792]{1,0:T(8,128)(2,1)} %cot_ref.1), custom_call_target="tpu_custom_call" | custom-call | flops 1 | bytes 1 | tf_op jit(solution)/shard_map/send_scaled/pallas_call | solution.py:91
  20.0 31.8 %all-to-all-done = bf16[64,24,896]{2,1,0:T(8,128)(2,1)S(1)} async-done(((bf16[64,24,896]{2,1,0:T(8,128)(2,1)}), bf16[64,24,896]{2,1,0:T(8,128)(2,1)S(1)}, u32[]{:S(2)}, u32[]{:S(2)}) %all-to-all-start) | async-done | bytes 2752544 | tf_op jit(solution)/shard_map/all_to_all | solution.py:489
  51.9 1.2 collective-permute-start
  53.0 0.4 copy-done
  53.4 6.8 %all-to-all-start.1 = ((bf16[64,24,896]{2,1,0:T(8,128)(2,1)}), bf16[64,24,896]{2,1,0:T(8,128)(2,1)}, u32[]{:S(2)}, u32[]{:S(2)}) async-start(bf16[64,24,896]{2,1,0:T(8,128)(2,1)} %bitcast.27), calls=%async_computation.1 | async-start | bytes 5505024 | tf_op jit(solution)/shard_map/all_to_all | solution.py:489
  60.2 0.0 collective-permute-done.other_ref
  60.2 19.8 %expert_forward.1 = (f32[768,512]{1,0:T(8,128)}, f32[768,512]{1,0:T(8,128)}, bf16[768,512]{1,0:T(8,128)(2,1)}, bf16[768,3584]{1,0:T(8,128)(2,1)}, bf16[768,896]{...) custom-call(s32[1]{0:T(128)} %bitcast.6.mine_ref, bf16[1536,896]{1,0:T(8,128)(2,1)} %bitcast.25, ...), custom_call_target="tpu_custom_call" | custom-call | flops 1 | bytes 1 | tf_op jit(solution)/shard_map/expert_forward/pallas_call | solution.py:201
  80.0 2.2 %collective-permute-start.1 = (bf16[768,896]{1,0:T(8,128)(2,1)}, bf16[768,896]{1,0:T(8,128)(2,1)S(1)}, u32[]{:S(2)}, u32[]{:S(2)}) collective-permute-start(bf16[768,896]{1,0:T(8,128)(2,1)} %get-tuple-element.33), channel_id=1, source_target_pairs={{0,1},{1,0},{2,3},{3,2},{4,5},{5,4},{6,7},{7,6},{8,9},{9,8},{10,11... | collective-permute-start | bytes 4128776 | tf_op jit(solution)/shard_map/ppermute | solution.py:496
  82.1 0.1 collective-permute-start.2
  82.2 2.9 %collective-permute-done.1.far0 = bf16[768,896]{1,0:T(8,128)(2,1)S(1)} collective-permute-done((bf16[768,896]{1,0:T(8,128)(2,1)}, bf16[768,896]{1,0:T(8,128)(2,1)S(1)}, u32[]{:S(2)}, u32[]{:S(2)}) %collective-permute-start.1) | collective-permute-done | bytes 1376288 | tf_op jit(solution)/shard_map/ppermute | solution.py:496
  85.1 2.0 %collective-permute-done.2.far1 = bf16[768,896]{1,0:T(8,128)(2,1)S(1)} collective-permute-done((bf16[768,896]{1,0:T(8,128)(2,1)}, bf16[768,896]{1,0:T(8,128)(2,1)S(1)}, u32[]{:S(2)}, u32[]{:S(2)}) %collective-permute-start.2) | collective-permute-done | bytes 1376288 | tf_op jit(solution)/shard_map/ppermute | solution.py:496
  87.1 4.8 %pack.2 = bf16[1536,896]{1,0:T(8,128)(2,1)} custom-call(bf16[768,1792]{1,0:T(8,128)(2,1)} %get-tuple-element.32.near_ref, bf16[768,896]{1,0:T(8,128)(2,1)S(1)} %collective-permute-done.1.far0, bf16[768,896]{1,0:T(8,128)(2,1)S(1)} %collective-permute-done.2.far1), custom_call_target="tpu_custom_call" | custom-call | flops 1 | bytes 1 | tf_op jit(solution)/shard_map/pack/pallas_call | solution.py:338
  91.8 3.9 %all-to-all-done.1 = bf16[64,24,896]{2,1,0:T(8,128)(2,1)} async-done(((bf16[64,24,896]{2,1,0:T(8,128)(2,1)}), bf16[64,24,896]{2,1,0:T(8,128)(2,1)}, u32[]{:S(2)}, u32[]{:S(2)}) %all-to-all-start.1) | async-done | bytes 2752544 | tf_op jit(solution)/shard_map/all_to_all | solution.py:489
  95.7 1.6 collective-permute-start.3
  97.3 6.7 %all-to-all-start.2 = ((bf16[64,24,896]{2,1,0:T(8,128)(2,1)}), bf16[64,24,896]{2,1,0:T(8,128)(2,1)S(1)}, u32[]{:S(2)}, u32[]{:S(2)}) async-start(bf16[64,24,896]{2,1,0:T(8,128)(2,1)} %bitcast.10), calls=%async_computation.2 | async-start | bytes 5505024 | tf_op jit(solution)/shard_map/all_to_all | solution.py:489
  104.0 0.0 collective-permute-done.3.other_ref
  104.0 18.8 %expert_backward.1 = (bf16[768,1024]{1,0:T(8,128)(2,1)}, bf16[768,3584]{1,0:T(8,128)(2,1)}, bf16[768,896]{1,0:T(8,128)(2,1)}, bf16[768,896]{1,0:T(8,128)(2,1)}, bf16[768,1792]{1,0:T(8,128)(2,1)}) custom-call(s32[1]{0:T(128)} %bitcast.6.mine_ref, bf16[1536,896]{1,0:T(8,128)(2,1)} %bitcast.5.own_ref, bf16[1536,896]{1,0:T(8,128)(2,1)} %collective-permute-done.3.other_ref, ...), custom_call_target="tpu_custom_call" | custom-call | flops 1 | bytes 1 | tf_op jit(solution)/shard_map/expert_backward/pallas_call | solution.py:287
  122.8 0.6 collective-permute-start.4
  123.5 0.1 collective-permute-start.5
  123.6 2.9 %collective-permute-done.4.far0 = bf16[768,896]{1,0:T(8,128)(2,1)S(1)} collective-permute-done((bf16[768,896]{1,0:T(8,128)(2,1)}, bf16[768,896]{1,0:T(8,128)(2,1)S(1)}, u32[]{:S(2)}, u32[]{:S(2)}) %collective-permute-start.4) | collective-permute-done | bytes 1376288 | tf_op jit(solution)/shard_map/ppermute | solution.py:496
  126.4 2.0 %collective-permute-done.5.far1 = bf16[768,896]{1,0:T(8,128)(2,1)S(1)} collective-permute-done((bf16[768,896]{1,0:T(8,128)(2,1)}, bf16[768,896]{1,0:T(8,128)(2,1)S(1)}, u32[]{:S(2)}, u32[]{:S(2)}) %collective-permute-start.5) | collective-permute-done | bytes 1376288 | tf_op jit(solution)/shard_map/ppermute | solution.py:496
  128.4 4.8 %pack.3 = bf16[1536,896]{1,0:T(8,128)(2,1)} custom-call(bf16[768,1792]{1,0:T(8,128)(2,1)} %get-tuple-element.39.near_ref, bf16[768,896]{1,0:T(8,128)(2,1)S(1)} %collective-permute-done.4.far0, bf16[768,896]{1,0:T(8,128)(2,1)S(1)} %collective-permute-done.5.far1), custom_call_target="tpu_custom_call" | custom-call | flops 1 | bytes 1 | tf_op jit(solution)/shard_map/pack/pallas_call | solution.py:338
  133.2 8.3 %all-to-all-done.2 = bf16[64,24,896]{2,1,0:T(8,128)(2,1)S(1)} async-done(((bf16[64,24,896]{2,1,0:T(8,128)(2,1)}), bf16[64,24,896]{2,1,0:T(8,128)(2,1)S(1)}, u32[]{:S(2)}, u32[]{:S(2)}) %all-to-all-start.2) | async-done | bytes 2752544 | tf_op jit(solution)/shard_map/all_to_all | solution.py:489
  141.4 1.5 copy-done.1
  143.0 5.5 %all-to-all-start.3 = ((bf16[64,24,896]{2,1,0:T(8,128)(2,1)}), bf16[64,24,896]{2,1,0:T(8,128)(2,1)}, u32[]{:S(2)}, u32[]{:S(2)}) async-start(bf16[64,24,896]{2,1,0:T(8,128)(2,1)} %bitcast.12), calls=%async_computation.3 | async-start | bytes 5505024 | tf_op jit(solution)/shard_map/all_to_all | solution.py:489
  148.5 13.7 %weight_grads.1 = (bf16[3584,512]{1,0:T(8,128)(2,1)}, bf16[3584,512]{1,0:T(8,128)(2,1)}, bf16[512,3584]{1,0:T(8,128)(2,1)}) custom-call(bf16[768,3584]{1,0:T(8,128)(2,1)} %get-tuple-element.47.rows_ref, bf16[768,3584]{1,0:T(8,128)(2,1)} %get-tuple-element.48.scaled_ref, bf16[768,512]{1,0:T(8,128)(2,1)} %get-tuple-element.49.hidden_ref, ...), custom_call_target="tpu_custom_call" | custom-call | flops 1 | bytes 1 | tf_op jit(solution)/shard_map/weight_grads/pallas_call | solution.py:368
  162.2 6.2 %token_outputs.1 = (bf16[64,1792]{1,0:T(8,128)(2,1)}, f32[8,64]{1,0:T(8,128)}, bf16[128,1536]{1,0:T(8,128)(2,1)}) custom-call(s32[8,64]{1,0:T(8,128)} %bitcast.31, f32[8,64]{1,0:T(8,128)} %bitcast.34, bf16[64,1792]{1,0:T(8,128)(2,1)} %cot_ref.1, bf16[1536,896]{1,0:T(8,128)(2,1)} %bitcast.26), custom_call_target="tpu_custom_call" | custom-call | flops 1 | bytes 1 | tf_op jit(solution)/shard_map/token_outputs/pallas_call | solution.py:431
  168.4 4.3 %psum.7 = f32[64,8]{0,1:T(8,128)} all-reduce(f32[64,8]{0,1:T(8,128)} %bitcast.35), channel_id=1, replica_groups=mesh['expert'=64,'mp'=2] {'mp'}, use_global_device_ids=true, to_apply=%region_0.0 | all-reduce | flops 512 | bytes 4096 | tf_op jit(solution)/shard_map/psum | solution.py:528
  172.6 11.5 %all-to-all-done.3 = bf16[64,24,896]{2,1,0:T(8,128)(2,1)} async-done(((bf16[64,24,896]{2,1,0:T(8,128)(2,1)}), bf16[64,24,896]{2,1,0:T(8,128)(2,1)}, u32[]{:S(2)}, u32[]{:S(2)}) %all-to-all-start.3) | async-done | bytes 2752544 | tf_op jit(solution)/shard_map/all_to_all | solution.py:489
  184.1 3.1 %token_grads.1 = bf16[64,1792]{1,0:T(8,128)(2,1)} custom-call(bf16[128,1536]{1,0:T(8,128)(2,1)} %get-tuple-element.44.sel_ref, bf16[1536,896]{1,0:T(8,128)(2,1)} %bitcast.13.back_ref), custom_call_target="tpu_custom_call" | custom-call | flops 1 | bytes 1 | tf_op jit(solution)/shard_map/token_grads/pallas_call | solution.py:471
  (2 shorter events, 0.0 us)
Async XLA Ops:
  4.9 47.0 %all-to-all-start = ((bf16[64,24,896]{2,1,0:T(8,128)(2,1)}), bf16[64,24,896]{2,1,0:T(8,128)(2,1)S(1)}, u32[]{:S(2)}, u32[]{:S(2)}) async-start(bf16[64,24,896]{2,1,0:T(8,128)(2,1)} %bitcast.28), calls=%async_computation | async-start | bytes 5505024 | tf_op jit(solution)/shard_map/all_to_all | solution.py:489
  51.9 1.5 copy-start
  51.9 8.3 %collective-permute-start = (bf16[1536,896]{1,0:T(8,128)(2,1)S(1)}, bf16[1536,896]{1,0:T(8,128)(2,1)}, u32[]{:S(2)}, u32[]{:S(2)}) collective-permute-start(bf16[1536,896]{1,0:T(8,128)(2,1)S(1)} %bitcast.24), channel_id=1, source_target_pairs={{0,1},{1,0},{2,3},{3,2},{4,5},{5,4},{6,7},{7,6},{8,9},{9,8},{10,11... | collective-permute-start | bytes 8257544 | tf_op jit(solution)/shard_map/ppermute | solution.py:496
  53.4 42.3 %all-to-all-start.1 = ((bf16[64,24,896]{2,1,0:T(8,128)(2,1)}), bf16[64,24,896]{2,1,0:T(8,128)(2,1)}, u32[]{:S(2)}, u32[]{:S(2)}) async-start(bf16[64,24,896]{2,1,0:T(8,128)(2,1)} %bitcast.27), calls=%async_computation.1 | async-start | bytes 5505024 | tf_op jit(solution)/shard_map/all_to_all | solution.py:489
  80.0 5.1 %collective-permute-start.1 = (bf16[768,896]{1,0:T(8,128)(2,1)}, bf16[768,896]{1,0:T(8,128)(2,1)S(1)}, u32[]{:S(2)}, u32[]{:S(2)}) collective-permute-start(bf16[768,896]{1,0:T(8,128)(2,1)} %get-tuple-element.33), channel_id=1, source_target_pairs={{0,1},{1,0},{2,3},{3,2},{4,5},{5,4},{6,7},{7,6},{8,9},{9,8},{10,11... | collective-permute-start | bytes 4128776 | tf_op jit(solution)/shard_map/ppermute | solution.py:496
  82.1 4.9 %collective-permute-start.2 = (bf16[768,896]{1,0:T(8,128)(2,1)}, bf16[768,896]{1,0:T(8,128)(2,1)S(1)}, u32[]{:S(2)}, u32[]{:S(2)}) collective-permute-start(bf16[768,896]{1,0:T(8,128)(2,1)} %get-tuple-element.34), channel_id=1, source_target_pairs={{0,1},{1,0},{2,3},{3,2},{4,5},{5,4},{6,7},{7,6},{8,9},{9,8},{10,11... | collective-permute-start | bytes 4128776 | tf_op jit(solution)/shard_map/ppermute | solution.py:496
  95.7 8.4 %collective-permute-start.3 = (bf16[1536,896]{1,0:T(8,128)(2,1)}, bf16[1536,896]{1,0:T(8,128)(2,1)}, u32[]{:S(2)}, u32[]{:S(2)}) collective-permute-start(bf16[1536,896]{1,0:T(8,128)(2,1)} %bitcast.5.own_ref), channel_id=1, source_target_pairs={{0,1},{1,0},{2,3},{3,2},{4,5},{5,4},{6,7},{7,6},{8,9},{9,8},{10,11... | collective-permute-start | bytes 8257544 | tf_op jit(solution)/shard_map/ppermute | solution.py:496
  97.3 44.2 %all-to-all-start.2 = ((bf16[64,24,896]{2,1,0:T(8,128)(2,1)}), bf16[64,24,896]{2,1,0:T(8,128)(2,1)S(1)}, u32[]{:S(2)}, u32[]{:S(2)}) async-start(bf16[64,24,896]{2,1,0:T(8,128)(2,1)} %bitcast.10), calls=%async_computation.2 | async-start | bytes 5505024 | tf_op jit(solution)/shard_map/all_to_all | solution.py:489
  122.8 3.6 %collective-permute-start.4 = (bf16[768,896]{1,0:T(8,128)(2,1)}, bf16[768,896]{1,0:T(8,128)(2,1)S(1)}, u32[]{:S(2)}, u32[]{:S(2)}) collective-permute-start(bf16[768,896]{1,0:T(8,128)(2,1)} %get-tuple-element.40), channel_id=1, source_target_pairs={{0,1},{1,0},{2,3},{3,2},{4,5},{5,4},{6,7},{7,6},{8,9},{9,8},{10,11... | collective-permute-start | bytes 4128776 | tf_op jit(solution)/shard_map/ppermute | solution.py:496
  123.5 4.9 %collective-permute-start.5 = (bf16[768,896]{1,0:T(8,128)(2,1)}, bf16[768,896]{1,0:T(8,128)(2,1)S(1)}, u32[]{:S(2)}, u32[]{:S(2)}) collective-permute-start(bf16[768,896]{1,0:T(8,128)(2,1)} %get-tuple-element.41), channel_id=1, source_target_pairs={{0,1},{1,0},{2,3},{3,2},{4,5},{5,4},{6,7},{7,6},{8,9},{9,8},{10,11... | collective-permute-start | bytes 4128776 | tf_op jit(solution)/shard_map/ppermute | solution.py:496
  141.4 1.5 copy-start.1
  143.0 41.2 %all-to-all-start.3 = ((bf16[64,24,896]{2,1,0:T(8,128)(2,1)}), bf16[64,24,896]{2,1,0:T(8,128)(2,1)}, u32[]{:S(2)}, u32[]{:S(2)}) async-start(bf16[64,24,896]{2,1,0:T(8,128)(2,1)} %bitcast.12), calls=%async_computation.3 | async-start | bytes 5505024 | tf_op jit(solution)/shard_map/all_to_all | solution.py:489

commit v6 on v5

--- a/solution.py
+++ b/solution.py
@@ -33,22 +33,23 @@
 
 
 def spread(rows_of):
+    count, width = rows_of.shape
     return jnp.concatenate(
-        [jnp.broadcast_to(rows_of[i : i + 1], (ROWS, rows_of.shape[1])) for i in range(GROUP)], axis=0
-    )
-
-
-def routing(route_ref, first):
+        [jnp.broadcast_to(rows_of[i : i + 1], (ROWS, width)) for i in range(count)], axis=0
+    )
+
+
+def routing(route_ref, first, count):
     top, toks = route_ref.shape
     route = route_ref[...]
-    ids = lax.broadcasted_iota(jnp.int32, (GROUP, toks), 0) + first
-    hits = [jnp.broadcast_to(route[k : k + 1], (GROUP, toks)) == ids for k in range(top)]
+    ids = lax.broadcasted_iota(jnp.int32, (count, toks), 0) + first
+    hits = [jnp.broadcast_to(route[k : k + 1], (count, toks)) == ids for k in range(top)]
     named = sum(h.astype(F32) for h in hits)
     return named, hits
 
 
 def selection(named):
-    toks = named.shape[1]
+    count, toks = named.shape
     before = (
         lax.broadcasted_iota(jnp.int32, (toks, toks), 0)
         < lax.broadcasted_iota(jnp.int32, (toks, toks), 1)
@@ -57,7 +58,7 @@
     code = jnp.where(named > 0, slot, -100.0)
     code = jnp.concatenate([code, code + float(SLOTS)], axis=1)
     place = lax.broadcasted_iota(jnp.int32, (ROWS, 2 * toks), 0).astype(F32)
-    place = jnp.concatenate([place] * GROUP, axis=0)
+    place = jnp.concatenate([place] * count, axis=0)
     return spread(code) == place
 
 
@@ -75,7 +76,8 @@
 
 
 def send_kernel(scaled, route_ref, probs_ref, rows_ref, out_ref):
-    named, hits = routing(route_ref, pl.program_id(0) * GROUP)
+    count = out_ref.shape[0] // ROWS
+    named, hits = routing(route_ref, pl.program_id(0) * count, count)
     sel = selection(named)
     picked = dot(sel.astype(F32).astype(BF16), stacked(rows_ref[...]))
     if scaled:
@@ -84,21 +86,24 @@
     out_ref[...] = picked.astype(BF16)
 
 
+SEND_STEP = 32
+
+
 def send_rows(scaled, route_t, probs_t, rows, experts):
     toks, width = rows.shape
     top = route_t.shape[0]
     half = width // 2
     return pl.pallas_call(
         functools.partial(send_kernel, scaled),
-        grid=(experts // GROUP,),
+        grid=(experts // SEND_STEP,),
         in_specs=[
             pl.BlockSpec((top, toks), lambda i: (0, 0)),
             pl.BlockSpec((top, toks), lambda i: (0, 0)),
             pl.BlockSpec((toks, width), lambda i: (0, 0)),
         ],
-        out_specs=pl.BlockSpec((TILE, half), lambda i: (i, 0)),
+        out_specs=pl.BlockSpec((SEND_STEP * ROWS, half), lambda i: (i, 0)),
         out_shape=jax.ShapeDtypeStruct((experts * ROWS, half), BF16),
-        compiler_params=params(60),
+        compiler_params=params(52 if scaled else 60),
         cost_estimate=cost(),
         name="send_scaled" if scaled else "send_tokens",
     )(route_t, probs_t, rows)
@@ -345,7 +350,7 @@
         ],
         out_specs=pl.BlockSpec((TILE, width // 2), lambda i: (i, 0)),
         out_shape=jax.ShapeDtypeStruct((2 * rows, width // 2), BF16),
-        compiler_params=params(48),
+        compiler_params=params(50),
         cost_estimate=cost(),
         name="pack",
     )(near, *fars)
@@ -395,7 +400,7 @@
 
     toks = cot_ref.shape[0]
     half = back_ref.shape[1]
-    named, hits = routing(route_ref, i * GROUP)
+    named, hits = routing(route_ref, i * GROUP, GROUP)
     sel = selection(named)
     sel_ref[...] = sel.astype(F32).T.astype(BF16)
     weight = jnp.where(sel, probs_of(hits, probs_ref), 0.0)
@@ -439,7 +444,7 @@
             jax.ShapeDtypeStruct((2 * toks, back.shape[0]), BF16),
         ],
         scratch_shapes=[pltpu.VMEM((2 * toks, width // 2), F32)],
-        compiler_params=params(60),
+        compiler_params=params(32),
         cost_estimate=cost(),
         name="token_outputs",
     )(route_t, probs_t, cot, back)
@@ -465,15 +470,18 @@
         out_ref[:, half:] = total[toks:].astype(BF16)
 
 
+GRAD_STEPS = 2
+
+
 def token_grads(select, back):
     raw, half = back.shape
     toks = select.shape[0] // 2
     return pl.pallas_call(
         inputs_kernel,
-        grid=(2,),
+        grid=(GRAD_STEPS,),
         in_specs=[
-            pl.BlockSpec((2 * toks, raw // 2), lambda i: (0, i)),
-            pl.BlockSpec((raw // 2, half), lambda i: (i, 0)),
+            pl.BlockSpec((2 * toks, raw // GRAD_STEPS), lambda i: (0, i)),
+            pl.BlockSpec((raw // GRAD_STEPS, half), lambda i: (i, 0)),
         ],
         out_specs=pl.BlockSpec((toks, 2 * half), lambda i: (0, 0)),
         out_shape=jax.ShapeDtypeStruct((toks, 2 * half), BF16),
@@ -521,10 +529,11 @@
     back_out, send_in = lax.optimization_barrier((back_out, send_in))
     back_in = exchange(send_in)
 
+    layer_out, grad_part, select = token_outputs(route_t, probs_t, cotangent, back_out)
+    grad_part, grads = lax.optimization_barrier((grad_part, grads))
     grad_w_gate, grad_w_up, grad_w_down = weight_grads(
         token_rows, scaled_rows, hidden, grads
     )
-    layer_out, grad_part, select = token_outputs(route_t, probs_t, cotangent, back_out)
     grad_probs = lax.psum(grad_part, "mp").T
     grad_tokens = token_grads(select, back_in)
     return (

time: 190 us -> 187 us (0.984)
  Pallas kernels: 79.5 us -> 75.7 us
  waiting for transfers between devices: 65.1 us -> 67.5 us
    pallas_call x3, Pallas kernels: 11.6 us -> 9.11 us  [the longest x2 6.04 us: send_rows(): pl.pallas_call(functools.partial(send_kernel, scaled), grid=(experts // S...]
    all_to_all x4, waiting for transfers between devices: 55.4 us -> 57.8 us  [exchange(): lax.all_to_all(x.reshape(experts, ROWS, -1), 'expert', split_axis=0, conc...]
  transfers between devices with their start and end apart: 10 -> 10, of which waited for: 8 -> 8; matrix products, arithmetic and copies ran while one was open for 0% -> 0% of each run, Pallas kernels for 39% -> 37%
where the time goes in v6:
time: 187 us; the launch traced here: 185 us
  Pallas kernels  75.7 us (40%)
  waiting for transfers between devices  67.5 us (36%)
  starting transfers between devices  35.8 us (19%)
  blocking collectives  4.12 us (2%)
    all_to_all x4, waiting for transfers between devices, exchange(): lax.all_to_all(x.reshape(experts, ROWS, -1), 'expert', split_axis=0, conc...  57.8 us
    all_to_all x4, starting transfers between devices, exchange(): lax.all_to_all(x.reshape(experts, ROWS, -1), 'expert', split_axis=0, conc...  30.1 us
    pallas_call x1, Pallas kernels, forward(): pl.pallas_call(functools.partial(forward_kernel, steps), grid_spec=pltpu....  19.8 us
    pallas_call x1, Pallas kernels, backward(): pl.pallas_call(functools.partial(backward_kernel, steps), grid_spec=pltpu...  18.8 us
    pallas_call x1, Pallas kernels, weight_grads(): pl.pallas_call(weights_kernel, grid=(model // step,), in_specs=[part, par...  13.7 us
    ppermute x6, waiting for transfers between devices, swap(): return lax.ppermute(x, 'mp', [(0, 1), (1, 0)])  9.69 us
    pallas_call x2, Pallas kernels, pack(): pl.pallas_call(pack_kernel, grid=(rows // step_rows,), in_specs=[pl.Block...  9.53 us
    pallas_call x2, Pallas kernels, send_rows(): pl.pallas_call(functools.partial(send_kernel, scaled), grid=(experts // S...  6.04 us
  transfers between devices with their start and end apart: 10, of which 8 were waited for; matrix products, arithmetic and copies ran while one was open for 0% of the time, Pallas kernels for 37%

profile of v6, /device:TPU:7, one launch (start us, length us, event | category | flops | bytes accessed | tf_op | source)
XLA Modules:
  0.0 185.0 jit_solution(6661114180037585459)
XLA Ops:
  0.6 3.5 %send_tokens.1 = bf16[1536,896]{1,0:T(8,128)(2,1)} custom-call(s32[8,64]{1,0:T(8,128)} %bitcast.19, f32[8,64]{1,0:T(8,128)} %bitcast.22, bf16[64,1792]{1,0:T(8,128)(2,1)} %rows_ref.2), custom_call_target="tpu_custom_call" | custom-call | flops 1 | bytes 1 | tf_op jit(solution)/shard_map/send_tokens/pallas_call | solution.py:96
  4.1 11.0 %all-to-all-start = ((bf16[64,24,896]{2,1,0:T(8,128)(2,1)}), bf16[64,24,896]{2,1,0:T(8,128)(2,1)S(1)}, u32[]{:S(2)}, u32[]{:S(2)}) async-start(bf16[64,24,896]{2,1,0:T(8,128)(2,1)} %bitcast.37), calls=%async_computation | async-start | bytes 5505024 | tf_op jit(solution)/shard_map/all_to_all | solution.py:497
  15.2 2.6 %send_scaled.1 = bf16[1536,896]{1,0:T(8,128)(2,1)} custom-call(s32[8,64]{1,0:T(8,128)S(1)} %bitcast.20, f32[8,64]{1,0:T(8,128)S(1)} %bitcast.23, bf16[64,1792]{1,0:T(8,128)(2,1)S(1)} %copy-done), custom_call_target="tpu_custom_call" | custom-call | flops 1 | bytes 1 | tf_op jit(solution)/shard_map/send_scaled/pallas_call | solution.py:96
  17.7 33.5 %all-to-all-done = bf16[64,24,896]{2,1,0:T(8,128)(2,1)S(1)} async-done(((bf16[64,24,896]{2,1,0:T(8,128)(2,1)}), bf16[64,24,896]{2,1,0:T(8,128)(2,1)S(1)}, u32[]{:S(2)}, u32[]{:S(2)}) %all-to-all-start) | async-done | bytes 2752544 | tf_op jit(solution)/shard_map/all_to_all | solution.py:497
  51.2 1.2 collective-permute-start
  52.4 0.4 copy-done.4
  52.8 6.8 %all-to-all-start.1 = ((bf16[64,24,896]{2,1,0:T(8,128)(2,1)}), bf16[64,24,896]{2,1,0:T(8,128)(2,1)}, u32[]{:S(2)}, u32[]{:S(2)}) async-start(bf16[64,24,896]{2,1,0:T(8,128)(2,1)} %bitcast.34), calls=%async_computation.1 | async-start | bytes 5505024 | tf_op jit(solution)/shard_map/all_to_all | solution.py:497
  59.5 0.0 collective-permute-done.other_ref
  59.5 19.8 %expert_forward.1 = (f32[768,512]{1,0:T(8,128)}, f32[768,512]{1,0:T(8,128)}, bf16[768,512]{1,0:T(8,128)(2,1)}, bf16[768,3584]{1,0:T(8,128)(2,1)}, bf16[768,896]{...) custom-call(s32[1]{0:T(128)} %bitcast.6.mine_ref, bf16[1536,896]{1,0:T(8,128)(2,1)} %bitcast.33, ...), custom_call_target="tpu_custom_call" | custom-call | flops 1 | bytes 1 | tf_op jit(solution)/shard_map/expert_forward/pallas_call | solution.py:206
  79.3 2.2 %collective-permute-start.1 = (bf16[768,896]{1,0:T(8,128)(2,1)}, bf16[768,896]{1,0:T(8,128)(2,1)S(1)}, u32[]{:S(2)}, u32[]{:S(2)}) collective-permute-start(bf16[768,896]{1,0:T(8,128)(2,1)} %get-tuple-element.35), channel_id=1, source_target_pairs={{0,1},{1,0},{2,3},{3,2},{4,5},{5,4},{6,7},{7,6},{8,9},{9,8},{10,11... | collective-permute-start | bytes 4128776 | tf_op jit(solution)/shard_map/ppermute | solution.py:504
  81.5 0.1 collective-permute-start.2
  81.6 2.9 %collective-permute-done.1.far0 = bf16[768,896]{1,0:T(8,128)(2,1)S(1)} collective-permute-done((bf16[768,896]{1,0:T(8,128)(2,1)}, bf16[768,896]{1,0:T(8,128)(2,1)S(1)}, u32[]{:S(2)}, u32[]{:S(2)}) %collective-permute-start.1) | collective-permute-done | bytes 1376288 | tf_op jit(solution)/shard_map/ppermute | solution.py:504
  84.5 2.0 %collective-permute-done.2.far1 = bf16[768,896]{1,0:T(8,128)(2,1)S(1)} collective-permute-done((bf16[768,896]{1,0:T(8,128)(2,1)}, bf16[768,896]{1,0:T(8,128)(2,1)S(1)}, u32[]{:S(2)}, u32[]{:S(2)}) %collective-permute-start.2) | collective-permute-done | bytes 1376288 | tf_op jit(solution)/shard_map/ppermute | solution.py:504
  86.4 4.8 %pack.2 = bf16[1536,896]{1,0:T(8,128)(2,1)} custom-call(bf16[768,1792]{1,0:T(8,128)(2,1)} %get-tuple-element.34.near_ref, bf16[768,896]{1,0:T(8,128)(2,1)S(1)} %collective-permute-done.1.far0, bf16[768,896]{1,0:T(8,128)(2,1)S(1)} %collective-permute-done.2.far1), custom_call_target="tpu_custom_call" | custom-call | flops 1 | bytes 1 | tf_op jit(solution)/shard_map/pack/pallas_call | solution.py:343
  91.2 3.8 %all-to-all-done.1 = bf16[64,24,896]{2,1,0:T(8,128)(2,1)} async-done(((bf16[64,24,896]{2,1,0:T(8,128)(2,1)}), bf16[64,24,896]{2,1,0:T(8,128)(2,1)}, u32[]{:S(2)}, u32[]{:S(2)}) %all-to-all-start.1) | async-done | bytes 2752544 | tf_op jit(solution)/shard_map/all_to_all | solution.py:497
  95.0 1.6 collective-permute-start.3
  96.7 6.7 %all-to-all-start.2 = ((bf16[64,24,896]{2,1,0:T(8,128)(2,1)}), bf16[64,24,896]{2,1,0:T(8,128)(2,1)S(1)}, u32[]{:S(2)}, u32[]{:S(2)}) async-start(bf16[64,24,896]{2,1,0:T(8,128)(2,1)} %bitcast.35), calls=%async_computation.2 | async-start | bytes 5505024 | tf_op jit(solution)/shard_map/all_to_all | solution.py:497
  103.4 0.0 collective-permute-done.3.other_ref
  103.4 18.8 %expert_backward.1 = (bf16[768,1024]{1,0:T(8,128)(2,1)}, bf16[768,3584]{1,0:T(8,128)(2,1)}, bf16[768,896]{1,0:T(8,128)(2,1)}, bf16[768,896]{1,0:T(8,128)(2,1)}, bf16[768,1792]{1,0:T(8,128)(2,1)}) custom-call(s32[1]{0:T(128)} %bitcast.6.mine_ref, bf16[1536,896]{1,0:T(8,128)(2,1)} %bitcast.5.own_ref, bf16[1536,896]{1,0:T(8,128)(2,1)} %collective-permute-done.3.other_ref, ...), custom_call_target="tpu_custom_call" | custom-call | flops 1 | bytes 1 | tf_op jit(solution)/shard_map/expert_backward/pallas_call | solution.py:292
  122.2 0.6 collective-permute-start.4
  122.8 0.1 collective-permute-start.5
  122.9 2.9 %collective-permute-done.4.far0 = bf16[768,896]{1,0:T(8,128)(2,1)S(1)} collective-permute-done((bf16[768,896]{1,0:T(8,128)(2,1)}, bf16[768,896]{1,0:T(8,128)(2,1)S(1)}, u32[]{:S(2)}, u32[]{:S(2)}) %collective-permute-start.4) | collective-permute-done | bytes 1376288 | tf_op jit(solution)/shard_map/ppermute | solution.py:504
  125.8 2.0 %collective-permute-done.5.far1 = bf16[768,896]{1,0:T(8,128)(2,1)S(1)} collective-permute-done((bf16[768,896]{1,0:T(8,128)(2,1)}, bf16[768,896]{1,0:T(8,128)(2,1)S(1)}, u32[]{:S(2)}, u32[]{:S(2)}) %collective-permute-start.5) | collective-permute-done | bytes 1376288 | tf_op jit(solution)/shard_map/ppermute | solution.py:504
  127.8 4.8 %pack.3 = bf16[1536,896]{1,0:T(8,128)(2,1)} custom-call(bf16[768,1792]{1,0:T(8,128)(2,1)} %get-tuple-element.41.near_ref, bf16[768,896]{1,0:T(8,128)(2,1)S(1)} %collective-permute-done.4.far0, bf16[768,896]{1,0:T(8,128)(2,1)S(1)} %collective-permute-done.5.far1), custom_call_target="tpu_custom_call" | custom-call | flops 1 | bytes 1 | tf_op jit(solution)/shard_map/pack/pallas_call | solution.py:343
  132.5 8.3 %all-to-all-done.2 = bf16[64,24,896]{2,1,0:T(8,128)(2,1)S(1)} async-done(((bf16[64,24,896]{2,1,0:T(8,128)(2,1)}), bf16[64,24,896]{2,1,0:T(8,128)(2,1)S(1)}, u32[]{:S(2)}, u32[]{:S(2)}) %all-to-all-start.2) | async-done | bytes 2752544 | tf_op jit(solution)/shard_map/all_to_all | solution.py:497
  140.8 5.5 %all-to-all-start.3 = ((bf16[64,24,896]{2,1,0:T(8,128)(2,1)}), bf16[64,24,896]{2,1,0:T(8,128)(2,1)}, u32[]{:S(2)}, u32[]{:S(2)}) async-start(bf16[64,24,896]{2,1,0:T(8,128)(2,1)} %bitcast.36), calls=%async_computation.3 | async-start | bytes 5505024 | tf_op jit(solution)/shard_map/all_to_all | solution.py:497
  146.4 4.9 %token_outputs.1 = (bf16[64,1792]{1,0:T(8,128)(2,1)}, f32[8,64]{1,0:T(8,128)S(1)}, bf16[128,1536]{1,0:T(8,128)(2,1)S(1)}) custom-call(s32[8,64]{1,0:T(8,128)S(1)} %bitcast.21, f32[8,64]{1,0:T(8,128)S(1)} %bitcast.24, bf16[64,1792]{1,0:T(8,128)(2,1)S(1)} %copy-done, bf16[1536,896]{1,0:T(8,128)(2,1)S(1)} %bitcast.18), custom_call_target="tpu_custom_call" | custom-call | flops 1 | bytes 1 | tf_op jit(solution)/shard_map/token_outputs/pallas_call | solution.py:436
  151.2 0.8 copy-done.1
  152.0 13.7 %weight_grads.1 = (bf16[3584,512]{1,0:T(8,128)(2,1)}, bf16[3584,512]{1,0:T(8,128)(2,1)}, bf16[512,3584]{1,0:T(8,128)(2,1)}) custom-call(bf16[768,3584]{1,0:T(8,128)(2,1)} %get-tuple-element.51.rows_ref, bf16[768,3584]{1,0:T(8,128)(2,1)} %get-tuple-element.52.scaled_ref, bf16[768,512]{1,0:T(8,128)(2,1)} %get-tuple-element.53.hidden_ref, ...), custom_call_target="tpu_custom_call" | custom-call | flops 1 | bytes 1 | tf_op jit(solution)/shard_map/weight_grads/pallas_call | solution.py:373
  165.7 4.1 %psum.7 = f32[64,8]{0,1:T(8,128)} all-reduce(f32[64,8]{0,1:T(8,128)S(1)} %bitcast.25), channel_id=1, replica_groups=mesh['expert'=64,'mp'=2] {'mp'}, use_global_device_ids=true, to_apply=%region_0.0 | all-reduce | flops 512 | bytes 4096 | tf_op jit(solution)/shard_map/psum | solution.py:537
  169.8 12.2 %all-to-all-done.3 = bf16[64,24,896]{2,1,0:T(8,128)(2,1)} async-done(((bf16[64,24,896]{2,1,0:T(8,128)(2,1)}), bf16[64,24,896]{2,1,0:T(8,128)(2,1)}, u32[]{:S(2)}, u32[]{:S(2)}) %all-to-all-start.3) | async-done | bytes 2752544 | tf_op jit(solution)/shard_map/all_to_all | solution.py:497
  182.0 3.1 %token_grads.1 = bf16[64,1792]{1,0:T(8,128)(2,1)} custom-call(bf16[128,1536]{1,0:T(8,128)(2,1)} %copy-done.1, bf16[1536,896]{1,0:T(8,128)(2,1)} %bitcast.13.back_ref), custom_call_target="tpu_custom_call" | custom-call | flops 1 | bytes 1 | tf_op jit(solution)/shard_map/token_grads/pallas_call | solution.py:479
  (8 shorter events, 0.0 us)
Async XLA Ops:
  4.1 11.0 %copy-start = (bf16[64,1792]{1,0:T(8,128)(2,1)S(1)}, bf16[64,1792]{1,0:T(8,128)(2,1)}, u32[]{:S(2)}) copy-start(bf16[64,1792]{1,0:T(8,128)(2,1)} %cot_ref.1) | copy-start | bytes 688132
  4.1 11.0 %copy-start.2 = (s32[64,8]{0,1:T(8,128)S(1)}, s32[64,8]{0,1:T(8,128)}, u32[]{:S(2)}) copy-start(s32[64,8]{0,1:T(8,128)} %param.9) | copy-start | bytes 6148
  4.1 11.1 %copy-start.3 = (f32[64,8]{0,1:T(8,128)S(1)}, f32[64,8]{0,1:T(8,128)}, u32[]{:S(2)}) copy-start(f32[64,8]{0,1:T(8,128)} %param.10) | copy-start | bytes 6148
  4.1 47.1 %all-to-all-start = ((bf16[64,24,896]{2,1,0:T(8,128)(2,1)}), bf16[64,24,896]{2,1,0:T(8,128)(2,1)S(1)}, u32[]{:S(2)}, u32[]{:S(2)}) async-start(bf16[64,24,896]{2,1,0:T(8,128)(2,1)} %bitcast.37), calls=%async_computation | async-start | bytes 5505024 | tf_op jit(solution)/shard_map/all_to_all | solution.py:497
  51.2 1.5 copy-start.4
  51.2 8.3 %collective-permute-start = (bf16[1536,896]{1,0:T(8,128)(2,1)S(1)}, bf16[1536,896]{1,0:T(8,128)(2,1)}, u32[]{:S(2)}, u32[]{:S(2)}) collective-permute-start(bf16[1536,896]{1,0:T(8,128)(2,1)S(1)} %bitcast.32), channel_id=1, source_target_pairs={{0,1},{1,0},{2,3},{3,2},{4,5},{5,4},{6,7},{7,6},{8,9},{9,8},{10,11... | collective-permute-start | bytes 8257544 | tf_op jit(solution)/shard_map/ppermute | solution.py:504
  52.8 42.3 %all-to-all-start.1 = ((bf16[64,24,896]{2,1,0:T(8,128)(2,1)}), bf16[64,24,896]{2,1,0:T(8,128)(2,1)}, u32[]{:S(2)}, u32[]{:S(2)}) async-start(bf16[64,24,896]{2,1,0:T(8,128)(2,1)} %bitcast.34), calls=%async_computation.1 | async-start | bytes 5505024 | tf_op jit(solution)/shard_map/all_to_all | solution.py:497
  79.3 5.1 %collective-permute-start.1 = (bf16[768,896]{1,0:T(8,128)(2,1)}, bf16[768,896]{1,0:T(8,128)(2,1)S(1)}, u32[]{:S(2)}, u32[]{:S(2)}) collective-permute-start(bf16[768,896]{1,0:T(8,128)(2,1)} %get-tuple-element.35), channel_id=1, source_target_pairs={{0,1},{1,0},{2,3},{3,2},{4,5},{5,4},{6,7},{7,6},{8,9},{9,8},{10,11... | collective-permute-start | bytes 4128776 | tf_op jit(solution)/shard_map/ppermute | solution.py:504
  81.5 4.9 %collective-permute-start.2 = (bf16[768,896]{1,0:T(8,128)(2,1)}, bf16[768,896]{1,0:T(8,128)(2,1)S(1)}, u32[]{:S(2)}, u32[]{:S(2)}) collective-permute-start(bf16[768,896]{1,0:T(8,128)(2,1)} %get-tuple-element.36), channel_id=1, source_target_pairs={{0,1},{1,0},{2,3},{3,2},{4,5},{5,4},{6,7},{7,6},{8,9},{9,8},{10,11... | collective-permute-start | bytes 4128776 | tf_op jit(solution)/shard_map/ppermute | solution.py:504
  95.0 8.4 %collective-permute-start.3 = (bf16[1536,896]{1,0:T(8,128)(2,1)}, bf16[1536,896]{1,0:T(8,128)(2,1)}, u32[]{:S(2)}, u32[]{:S(2)}) collective-permute-start(bf16[1536,896]{1,0:T(8,128)(2,1)} %bitcast.5.own_ref), channel_id=1, source_target_pairs={{0,1},{1,0},{2,3},{3,2},{4,5},{5,4},{6,7},{7,6},{8,9},{9,8},{10,11... | collective-permute-start | bytes 8257544 | tf_op jit(solution)/shard_map/ppermute | solution.py:504
  96.7 44.1 %all-to-all-start.2 = ((bf16[64,24,896]{2,1,0:T(8,128)(2,1)}), bf16[64,24,896]{2,1,0:T(8,128)(2,1)S(1)}, u32[]{:S(2)}, u32[]{:S(2)}) async-start(bf16[64,24,896]{2,1,0:T(8,128)(2,1)} %bitcast.35), calls=%async_computation.2 | async-start | bytes 5505024 | tf_op jit(solution)/shard_map/all_to_all | solution.py:497
  122.2 3.6 %collective-permute-start.4 = (bf16[768,896]{1,0:T(8,128)(2,1)}, bf16[768,896]{1,0:T(8,128)(2,1)S(1)}, u32[]{:S(2)}, u32[]{:S(2)}) collective-permute-start(bf16[768,896]{1,0:T(8,128)(2,1)} %get-tuple-element.42), channel_id=1, source_target_pairs={{0,1},{1,0},{2,3},{3,2},{4,5},{5,4},{6,7},{7,6},{8,9},{9,8},{10,11... | collective-permute-start | bytes 4128776 | tf_op jit(solution)/shard_map/ppermute | solution.py:504
  122.8 4.9 %collective-permute-start.5 = (bf16[768,896]{1,0:T(8,128)(2,1)}, bf16[768,896]{1,0:T(8,128)(2,1)S(1)}, u32[]{:S(2)}, u32[]{:S(2)}) collective-permute-start(bf16[768,896]{1,0:T(8,128)(2,1)} %get-tuple-element.43), channel_id=1, source_target_pairs={{0,1},{1,0},{2,3},{3,2},{4,5},{5,4},{6,7},{7,6},{8,9},{9,8},{10,11... | collective-permute-start | bytes 4128776 | tf_op jit(solution)/shard_map/ppermute | solution.py:504
  140.8 41.2 %all-to-all-start.3 = ((bf16[64,24,896]{2,1,0:T(8,128)(2,1)}), bf16[64,24,896]{2,1,0:T(8,128)(2,1)}, u32[]{:S(2)}, u32[]{:S(2)}) async-start(bf16[64,24,896]{2,1,0:T(8,128)(2,1)} %bitcast.36), calls=%async_computation.3 | async-start | bytes 5505024 | tf_op jit(solution)/shard_map/all_to_all | solution.py:497
  151.2 0.8 copy-start.1

commit v7 on v6

--- a/solution.py
+++ b/solution.py
@@ -384,7 +384,7 @@
             jax.ShapeDtypeStruct((model, ff), BF16),
             jax.ShapeDtypeStruct((ff, model), BF16),
         ],
-        compiler_params=params(60),
+        compiler_params=params(54),
         cost_estimate=cost(),
         name="weight_grads",
     )(token_rows, scaled_rows, hidden, grads)
@@ -486,7 +486,7 @@
         out_specs=pl.BlockSpec((toks, 2 * half), lambda i: (0, 0)),
         out_shape=jax.ShapeDtypeStruct((toks, 2 * half), BF16),
         scratch_shapes=[pltpu.VMEM((2 * toks, half), F32)],
-        compiler_params=params(60),
+        compiler_params=params(16),
         cost_estimate=cost(),
         name="token_grads",
     )(select, back)

time: 187 us -> 187 us (level)
  no operation moved by 1% of the time
where the time goes in v7:
time: 187 us; the launch traced here: 185 us
  Pallas kernels  75.6 us (40%)
  waiting for transfers between devices  68.2 us (36%)
  starting transfers between devices  35.8 us (19%)
  blocking collectives  4.12 us (2%)
    all_to_all x4, waiting for transfers between devices, exchange(): lax.all_to_all(x.reshape(experts, ROWS, -1), 'expert', split_axis=0, conc...  58.5 us
    all_to_all x4, starting transfers between devices, exchange(): lax.all_to_all(x.reshape(experts, ROWS, -1), 'expert', split_axis=0, conc...  30.1 us
    pallas_call x1, Pallas kernels, forward(): pl.pallas_call(functools.partial(forward_kernel, steps), grid_spec=pltpu....  19.8 us
    pallas_call x1, Pallas kernels, backward(): pl.pallas_call(functools.partial(backward_kernel, steps), grid_spec=pltpu...  18.8 us
    pallas_call x1, Pallas kernels, weight_grads(): pl.pallas_call(weights_kernel, grid=(model // step,), in_specs=[part, par...  13.7 us
    ppermute x6, waiting for transfers between devices, swap(): return lax.ppermute(x, 'mp', [(0, 1), (1, 0)])  9.69 us
    pallas_call x2, Pallas kernels, pack(): pl.pallas_call(pack_kernel, grid=(rows // step_rows,), in_specs=[pl.Block...  9.56 us
    pallas_call x2, Pallas kernels, send_rows(): pl.pallas_call(functools.partial(send_kernel, scaled), grid=(experts // S...  6.04 us
  transfers between devices with their start and end apart: 10, of which 8 were waited for; matrix products, arithmetic and copies ran while one was open for 0% of the time, Pallas kernels for 37%

profile of v7, /device:TPU:7, one launch (start us, length us, event | category | flops | bytes accessed | tf_op | source)
XLA Modules:
  0.0 184.9 jit_solution(6422596450208180282)
XLA Ops:
  0.6 3.5 %send_tokens.1 = bf16[1536,896]{1,0:T(8,128)(2,1)} custom-call(s32[8,64]{1,0:T(8,128)} %bitcast.19, f32[8,64]{1,0:T(8,128)} %bitcast.22, bf16[64,1792]{1,0:T(8,128)(2,1)} %rows_ref.2), custom_call_target="tpu_custom_call" | custom-call | flops 1 | bytes 1 | tf_op jit(solution)/shard_map/send_tokens/pallas_call | solution.py:96
  4.1 11.0 %all-to-all-start = ((bf16[64,24,896]{2,1,0:T(8,128)(2,1)}), bf16[64,24,896]{2,1,0:T(8,128)(2,1)S(1)}, u32[]{:S(2)}, u32[]{:S(2)}) async-start(bf16[64,24,896]{2,1,0:T(8,128)(2,1)} %bitcast.37), calls=%async_computation | async-start | bytes 5505024 | tf_op jit(solution)/shard_map/all_to_all | solution.py:497
  15.2 0.0 copy-done
  15.2 2.6 %send_scaled.1 = bf16[1536,896]{1,0:T(8,128)(2,1)} custom-call(s32[8,64]{1,0:T(8,128)S(1)} %bitcast.20, f32[8,64]{1,0:T(8,128)S(1)} %bitcast.23, bf16[64,1792]{1,0:T(8,128)(2,1)S(1)} %copy-done), custom_call_target="tpu_custom_call" | custom-call | flops 1 | bytes 1 | tf_op jit(solution)/shard_map/send_scaled/pallas_call | solution.py:96
  17.7 33.5 %all-to-all-done = bf16[64,24,896]{2,1,0:T(8,128)(2,1)S(1)} async-done(((bf16[64,24,896]{2,1,0:T(8,128)(2,1)}), bf16[64,24,896]{2,1,0:T(8,128)(2,1)S(1)}, u32[]{:S(2)}, u32[]{:S(2)}) %all-to-all-start) | async-done | bytes 2752544 | tf_op jit(solution)/shard_map/all_to_all | solution.py:497
  51.2 1.2 collective-permute-start
  52.4 0.4 copy-done.3
  52.8 6.8 %all-to-all-start.1 = ((bf16[64,24,896]{2,1,0:T(8,128)(2,1)}), bf16[64,24,896]{2,1,0:T(8,128)(2,1)}, u32[]{:S(2)}, u32[]{:S(2)}) async-start(bf16[64,24,896]{2,1,0:T(8,128)(2,1)} %bitcast.34), calls=%async_computation.1 | async-start | bytes 5505024 | tf_op jit(solution)/shard_map/all_to_all | solution.py:497
  59.5 0.0 collective-permute-done.other_ref
  59.5 19.8 %expert_forward.1 = (f32[768,512]{1,0:T(8,128)}, f32[768,512]{1,0:T(8,128)}, bf16[768,512]{1,0:T(8,128)(2,1)}, bf16[768,3584]{1,0:T(8,128)(2,1)}, bf16[768,896]{...) custom-call(s32[1]{0:T(128)} %bitcast.6.mine_ref, bf16[1536,896]{1,0:T(8,128)(2,1)} %bitcast.33, ...), custom_call_target="tpu_custom_call" | custom-call | flops 1 | bytes 1 | tf_op jit(solution)/shard_map/expert_forward/pallas_call | solution.py:206
  79.3 2.2 %collective-permute-start.1 = (bf16[768,896]{1,0:T(8,128)(2,1)}, bf16[768,896]{1,0:T(8,128)(2,1)S(1)}, u32[]{:S(2)}, u32[]{:S(2)}) collective-permute-start(bf16[768,896]{1,0:T(8,128)(2,1)} %get-tuple-element.35), channel_id=1, source_target_pairs={{0,1},{1,0},{2,3},{3,2},{4,5},{5,4},{6,7},{7,6},{8,9},{9,8},{10,11... | collective-permute-start | bytes 4128776 | tf_op jit(solution)/shard_map/ppermute | solution.py:504
  81.5 0.1 collective-permute-start.2
  81.6 2.9 %collective-permute-done.1.far0 = bf16[768,896]{1,0:T(8,128)(2,1)S(1)} collective-permute-done((bf16[768,896]{1,0:T(8,128)(2,1)}, bf16[768,896]{1,0:T(8,128)(2,1)S(1)}, u32[]{:S(2)}, u32[]{:S(2)}) %collective-permute-start.1) | collective-permute-done | bytes 1376288 | tf_op jit(solution)/shard_map/ppermute | solution.py:504
  84.5 2.0 %collective-permute-done.2.far1 = bf16[768,896]{1,0:T(8,128)(2,1)S(1)} collective-permute-done((bf16[768,896]{1,0:T(8,128)(2,1)}, bf16[768,896]{1,0:T(8,128)(2,1)S(1)}, u32[]{:S(2)}, u32[]{:S(2)}) %collective-permute-start.2) | collective-permute-done | bytes 1376288 | tf_op jit(solution)/shard_map/ppermute | solution.py:504
  86.4 4.8 %pack.2 = bf16[1536,896]{1,0:T(8,128)(2,1)} custom-call(bf16[768,1792]{1,0:T(8,128)(2,1)} %get-tuple-element.34.near_ref, bf16[768,896]{1,0:T(8,128)(2,1)S(1)} %collective-permute-done.1.far0, bf16[768,896]{1,0:T(8,128)(2,1)S(1)} %collective-permute-done.2.far1), custom_call_target="tpu_custom_call" | custom-call | flops 1 | bytes 1 | tf_op jit(solution)/shard_map/pack/pallas_call | solution.py:343
  91.2 3.8 %all-to-all-done.1 = bf16[64,24,896]{2,1,0:T(8,128)(2,1)} async-done(((bf16[64,24,896]{2,1,0:T(8,128)(2,1)}), bf16[64,24,896]{2,1,0:T(8,128)(2,1)}, u32[]{:S(2)}, u32[]{:S(2)}) %all-to-all-start.1) | async-done | bytes 2752544 | tf_op jit(solution)/shard_map/all_to_all | solution.py:497
  95.0 1.6 collective-permute-start.3
  96.7 6.7 %all-to-all-start.2 = ((bf16[64,24,896]{2,1,0:T(8,128)(2,1)}), bf16[64,24,896]{2,1,0:T(8,128)(2,1)S(1)}, u32[]{:S(2)}, u32[]{:S(2)}) async-start(bf16[64,24,896]{2,1,0:T(8,128)(2,1)} %bitcast.35), calls=%async_computation.2 | async-start | bytes 5505024 | tf_op jit(solution)/shard_map/all_to_all | solution.py:497
  103.4 0.0 collective-permute-done.3.other_ref
  103.4 18.8 %expert_backward.1 = (bf16[768,1024]{1,0:T(8,128)(2,1)}, bf16[768,3584]{1,0:T(8,128)(2,1)}, bf16[768,896]{1,0:T(8,128)(2,1)}, bf16[768,896]{1,0:T(8,128)(2,1)}, bf16[768,1792]{1,0:T(8,128)(2,1)}) custom-call(s32[1]{0:T(128)} %bitcast.6.mine_ref, bf16[1536,896]{1,0:T(8,128)(2,1)} %bitcast.5.own_ref, bf16[1536,896]{1,0:T(8,128)(2,1)} %collective-permute-done.3.other_ref, ...), custom_call_target="tpu_custom_call" | custom-call | flops 1 | bytes 1 | tf_op jit(solution)/shard_map/expert_backward/pallas_call | solution.py:292
  122.2 0.6 collective-permute-start.4
  122.8 0.1 collective-permute-start.5
  122.9 2.9 %collective-permute-done.4.far0 = bf16[768,896]{1,0:T(8,128)(2,1)S(1)} collective-permute-done((bf16[768,896]{1,0:T(8,128)(2,1)}, bf16[768,896]{1,0:T(8,128)(2,1)S(1)}, u32[]{:S(2)}, u32[]{:S(2)}) %collective-permute-start.4) | collective-permute-done | bytes 1376288 | tf_op jit(solution)/shard_map/ppermute | solution.py:504
  125.8 2.0 %collective-permute-done.5.far1 = bf16[768,896]{1,0:T(8,128)(2,1)S(1)} collective-permute-done((bf16[768,896]{1,0:T(8,128)(2,1)}, bf16[768,896]{1,0:T(8,128)(2,1)S(1)}, u32[]{:S(2)}, u32[]{:S(2)}) %collective-permute-start.5) | collective-permute-done | bytes 1376288 | tf_op jit(solution)/shard_map/ppermute | solution.py:504
  127.8 4.8 %pack.3 = bf16[1536,896]{1,0:T(8,128)(2,1)} custom-call(bf16[768,1792]{1,0:T(8,128)(2,1)} %get-tuple-element.41.near_ref, bf16[768,896]{1,0:T(8,128)(2,1)S(1)} %collective-permute-done.4.far0, bf16[768,896]{1,0:T(8,128)(2,1)S(1)} %collective-permute-done.5.far1), custom_call_target="tpu_custom_call" | custom-call | flops 1 | bytes 1 | tf_op jit(solution)/shard_map/pack/pallas_call | solution.py:343
  132.6 8.3 %all-to-all-done.2 = bf16[64,24,896]{2,1,0:T(8,128)(2,1)S(1)} async-done(((bf16[64,24,896]{2,1,0:T(8,128)(2,1)}), bf16[64,24,896]{2,1,0:T(8,128)(2,1)S(1)}, u32[]{:S(2)}, u32[]{:S(2)}) %all-to-all-start.2) | async-done | bytes 2752544 | tf_op jit(solution)/shard_map/all_to_all | solution.py:497
  140.8 5.5 %all-to-all-start.3 = ((bf16[64,24,896]{2,1,0:T(8,128)(2,1)}), bf16[64,24,896]{2,1,0:T(8,128)(2,1)}, u32[]{:S(2)}, u32[]{:S(2)}) async-start(bf16[64,24,896]{2,1,0:T(8,128)(2,1)} %bitcast.36), calls=%async_computation.3 | async-start | bytes 5505024 | tf_op jit(solution)/shard_map/all_to_all | solution.py:497
  146.4 4.9 %token_outputs.1 = (bf16[64,1792]{1,0:T(8,128)(2,1)}, f32[8,64]{1,0:T(8,128)S(1)}, bf16[128,1536]{1,0:T(8,128)(2,1)S(1)}) custom-call(s32[8,64]{1,0:T(8,128)S(1)} %bitcast.21, f32[8,64]{1,0:T(8,128)S(1)} %bitcast.24, bf16[64,1792]{1,0:T(8,128)(2,1)S(1)} %copy-done, bf16[1536,896]{1,0:T(8,128)(2,1)S(1)} %bitcast.18), custom_call_target="tpu_custom_call" | custom-call | flops 1 | bytes 1 | tf_op jit(solution)/shard_map/token_outputs/pallas_call | solution.py:436
  151.2 13.7 %weight_grads.1 = (bf16[3584,512]{1,0:T(8,128)(2,1)}, bf16[3584,512]{1,0:T(8,128)(2,1)}, bf16[512,3584]{1,0:T(8,128)(2,1)}) custom-call(bf16[768,3584]{1,0:T(8,128)(2,1)} %get-tuple-element.51.rows_ref, bf16[768,3584]{1,0:T(8,128)(2,1)} %get-tuple-element.52.scaled_ref, bf16[768,512]{1,0:T(8,128)(2,1)} %get-tuple-element.53.hidden_ref, ...), custom_call_target="tpu_custom_call" | custom-call | flops 1 | bytes 1 | tf_op jit(solution)/shard_map/weight_grads/pallas_call | solution.py:373
  164.9 4.1 %psum.7 = f32[64,8]{0,1:T(8,128)} all-reduce(f32[64,8]{0,1:T(8,128)S(1)} %bitcast.25), channel_id=1, replica_groups=mesh['expert'=64,'mp'=2] {'mp'}, use_global_device_ids=true, to_apply=%region_0.0 | all-reduce | flops 512 | bytes 4096 | tf_op jit(solution)/shard_map/psum | solution.py:537
  169.0 13.0 %all-to-all-done.3 = bf16[64,24,896]{2,1,0:T(8,128)(2,1)} async-done(((bf16[64,24,896]{2,1,0:T(8,128)(2,1)}), bf16[64,24,896]{2,1,0:T(8,128)(2,1)}, u32[]{:S(2)}, u32[]{:S(2)}) %all-to-all-start.3) | async-done | bytes 2752544 | tf_op jit(solution)/shard_map/all_to_all | solution.py:497
  182.0 2.9 %token_grads.1 = bf16[64,1792]{1,0:T(8,128)(2,1)} custom-call(bf16[128,1536]{1,0:T(8,128)(2,1)S(1)} %get-tuple-element.46.sel_ref, bf16[1536,896]{1,0:T(8,128)(2,1)} %bitcast.13.back_ref), custom_call_target="tpu_custom_call" | custom-call | flops 1 | bytes 1 | tf_op jit(solution)/shard_map/token_grads/pallas_call | solution.py:479
  (6 shorter events, 0.0 us)
Async XLA Ops:
  4.1 11.0 %copy-start = (bf16[64,1792]{1,0:T(8,128)(2,1)S(1)}, bf16[64,1792]{1,0:T(8,128)(2,1)}, u32[]{:S(2)}) copy-start(bf16[64,1792]{1,0:T(8,128)(2,1)} %cot_ref.1) | copy-start | bytes 688132
  4.1 11.0 %copy-start.1 = (s32[64,8]{0,1:T(8,128)S(1)}, s32[64,8]{0,1:T(8,128)}, u32[]{:S(2)}) copy-start(s32[64,8]{0,1:T(8,128)} %param.9) | copy-start | bytes 6148
  4.1 11.1 %copy-start.2 = (f32[64,8]{0,1:T(8,128)S(1)}, f32[64,8]{0,1:T(8,128)}, u32[]{:S(2)}) copy-start(f32[64,8]{0,1:T(8,128)} %param.10) | copy-start | bytes 6148
  4.1 47.1 %all-to-all-start = ((bf16[64,24,896]{2,1,0:T(8,128)(2,1)}), bf16[64,24,896]{2,1,0:T(8,128)(2,1)S(1)}, u32[]{:S(2)}, u32[]{:S(2)}) async-start(bf16[64,24,896]{2,1,0:T(8,128)(2,1)} %bitcast.37), calls=%async_computation | async-start | bytes 5505024 | tf_op jit(solution)/shard_map/all_to_all | solution.py:497
  51.2 1.5 copy-start.3
  51.2 8.3 %collective-permute-start = (bf16[1536,896]{1,0:T(8,128)(2,1)S(1)}, bf16[1536,896]{1,0:T(8,128)(2,1)}, u32[]{:S(2)}, u32[]{:S(2)}) collective-permute-start(bf16[1536,896]{1,0:T(8,128)(2,1)S(1)} %bitcast.32), channel_id=1, source_target_pairs={{0,1},{1,0},{2,3},{3,2},{4,5},{5,4},{6,7},{7,6},{8,9},{9,8},{10,11... | collective-permute-start | bytes 8257544 | tf_op jit(solution)/shard_map/ppermute | solution.py:504
  52.8 42.3 %all-to-all-start.1 = ((bf16[64,24,896]{2,1,0:T(8,128)(2,1)}), bf16[64,24,896]{2,1,0:T(8,128)(2,1)}, u32[]{:S(2)}, u32[]{:S(2)}) async-start(bf16[64,24,896]{2,1,0:T(8,128)(2,1)} %bitcast.34), calls=%async_computation.1 | async-start | bytes 5505024 | tf_op jit(solution)/shard_map/all_to_all | solution.py:497
  79.3 5.1 %collective-permute-start.1 = (bf16[768,896]{1,0:T(8,128)(2,1)}, bf16[768,896]{1,0:T(8,128)(2,1)S(1)}, u32[]{:S(2)}, u32[]{:S(2)}) collective-permute-start(bf16[768,896]{1,0:T(8,128)(2,1)} %get-tuple-element.35), channel_id=1, source_target_pairs={{0,1},{1,0},{2,3},{3,2},{4,5},{5,4},{6,7},{7,6},{8,9},{9,8},{10,11... | collective-permute-start | bytes 4128776 | tf_op jit(solution)/shard_map/ppermute | solution.py:504
  81.5 4.9 %collective-permute-start.2 = (bf16[768,896]{1,0:T(8,128)(2,1)}, bf16[768,896]{1,0:T(8,128)(2,1)S(1)}, u32[]{:S(2)}, u32[]{:S(2)}) collective-permute-start(bf16[768,896]{1,0:T(8,128)(2,1)} %get-tuple-element.36), channel_id=1, source_target_pairs={{0,1},{1,0},{2,3},{3,2},{4,5},{5,4},{6,7},{7,6},{8,9},{9,8},{10,11... | collective-permute-start | bytes 4128776 | tf_op jit(solution)/shard_map/ppermute | solution.py:504
  95.0 8.4 %collective-permute-start.3 = (bf16[1536,896]{1,0:T(8,128)(2,1)}, bf16[1536,896]{1,0:T(8,128)(2,1)}, u32[]{:S(2)}, u32[]{:S(2)}) collective-permute-start(bf16[1536,896]{1,0:T(8,128)(2,1)} %bitcast.5.own_ref), channel_id=1, source_target_pairs={{0,1},{1,0},{2,3},{3,2},{4,5},{5,4},{6,7},{7,6},{8,9},{9,8},{10,11... | collective-permute-start | bytes 8257544 | tf_op jit(solution)/shard_map/ppermute | solution.py:504
  96.7 44.1 %all-to-all-start.2 = ((bf16[64,24,896]{2,1,0:T(8,128)(2,1)}), bf16[64,24,896]{2,1,0:T(8,128)(2,1)S(1)}, u32[]{:S(2)}, u32[]{:S(2)}) async-start(bf16[64,24,896]{2,1,0:T(8,128)(2,1)} %bitcast.35), calls=%async_computation.2 | async-start | bytes 5505024 | tf_op jit(solution)/shard_map/all_to_all | solution.py:497
  122.2 3.6 %collective-permute-start.4 = (bf16[768,896]{1,0:T(8,128)(2,1)}, bf16[768,896]{1,0:T(8,128)(2,1)S(1)}, u32[]{:S(2)}, u32[]{:S(2)}) collective-permute-start(bf16[768,896]{1,0:T(8,128)(2,1)} %get-tuple-element.42), channel_id=1, source_target_pairs={{0,1},{1,0},{2,3},{3,2},{4,5},{5,4},{6,7},{7,6},{8,9},{9,8},{10,11... | collective-permute-start | bytes 4128776 | tf_op jit(solution)/shard_map/ppermute | solution.py:504
  122.8 4.9 %collective-permute-start.5 = (bf16[768,896]{1,0:T(8,128)(2,1)}, bf16[768,896]{1,0:T(8,128)(2,1)S(1)}, u32[]{:S(2)}, u32[]{:S(2)}) collective-permute-start(bf16[768,896]{1,0:T(8,128)(2,1)} %get-tuple-element.43), channel_id=1, source_target_pairs={{0,1},{1,0},{2,3},{3,2},{4,5},{5,4},{6,7},{7,6},{8,9},{9,8},{10,11... | collective-permute-start | bytes 4128776 | tf_op jit(solution)/shard_map/ppermute | solution.py:504
  140.8 41.2 %all-to-all-start.3 = ((bf16[64,24,896]{2,1,0:T(8,128)(2,1)}), bf16[64,24,896]{2,1,0:T(8,128)(2,1)}, u32[]{:S(2)}, u32[]{:S(2)}) async-start(bf16[64,24,896]{2,1,0:T(8,128)(2,1)} %bitcast.36), calls=%async_computation.3 | async-start | bytes 5505024 | tf_op jit(solution)/shard_map/all_to_all | solution.py:497
